TPU v7x, 128 devices: a whole 4x4x4 slice. The times are simulated.
128 devices in a mesh: gx: 8 (over y, core), gy: 16 (over z, x).
Axes of the slice: x: 4, y: 4, z: 4, core: 2. Of those that a mesh axis runs over, the one named last changes fastest.
Arguments:
- hidden: bfloat16 [1024, 16384], P('gx', 'gy'), as said below
- gain: bfloat16 [16384], P('gy'), may hold values from 0.099609375 to 1.8984375
- w_query: bfloat16 [16384, 16384], P('gy', 'gx'), may hold values from -0.046875 to 0.046875
- w_key: bfloat16 [16384, 1024], P('gy', 'gx'), may hold values from -0.125 to 0.125
- w_value: bfloat16 [16384, 1024], P('gy', 'gx'), may hold values from -0.046875 to 0.046875
- w_out: bfloat16 [16384, 16384], P('gx', 'gy'), may hold values from -0.046875 to 0.046875
- key_cache: bfloat16 [512, 1024, 1024], P('gy', None, 'gx'), as said below
- value_cache: bfloat16 [512, 1024, 1024], P('gy', None, 'gx'), may hold values from -6 to 6
- lengths: int32 [512], P('gy'), may hold values from 4 to 1024, as said below
Outputs:
- layer_out: bfloat16 [1024, 16384], P('gx', 'gy')
- new_keys: bfloat16 [1024, 1024], P('gy', 'gx')
- new_values: bfloat16 [1024, 1024], P('gy', 'gx')
Inputs may be any that keep to these rules, and one draw needn't show every extreme that they name: `lengths`: each sequence's live cache slots; some sequence has all 1024 in every draw. `hidden`: residual stream entries. `key_cache`: cached keys.
All inputs are finite; a program needn't handle non-finite values.
Results may differ from a plain program's by a relative error of at most 0.0058.
Values may be sent and summed in bfloat16 or wider, within the bound.
No kernel may reach another device: no remote copies, remote signals or barrier semaphores. Data moves between devices by JAX's collectives and lax.ppermute only.
A program may use at most 128 MiB of HBM per device.

v0:
```python
import jax
import jax.numpy as jnp
from jax import lax
from jax.sharding import PartitionSpec as P

D = 16384
HD = 128
NEW = 2


EPSILON = 1e-05
ROPE_BASE = 500000.0


def rotate(values, positions):
    half_dim = values.shape[-1] // 2
    indices = jnp.arange(half_dim, dtype=jnp.float32)
    inverse = jnp.power(jnp.float32(ROPE_BASE), -2.0 * indices / values.shape[-1])
    angles = positions.astype(jnp.float32)[:, None] * inverse[None, :]
    cosine = jnp.cos(angles)[:, None, :]
    sine = jnp.sin(angles)[:, None, :]
    first_half = values[..., :half_dim]
    second_half = values[..., half_dim:]
    return jnp.concatenate(
        [first_half * cosine - second_half * sine, second_half * cosine + first_half * sine], -1
    )


def attend(queries, keys_new, values_new, cache_keys, cache_values, lengths):
    scale = HD ** (-0.5)
    cache_scores = (
        jnp.einsum("stkgd,spkd->stkgp", queries, cache_keys, preferred_element_type=jnp.float32)
        * scale
    )
    fresh_scores = (
        jnp.einsum("stkgd,sukd->stkgu", queries, keys_new, preferred_element_type=jnp.float32)
        * scale
    )
    live = jnp.arange(cache_keys.shape[1], dtype=jnp.int32)[None, :] < lengths[:, None]
    cache_scores = jnp.where(live[:, None, None, None, :], cache_scores, -jnp.inf)
    causal = jnp.arange(NEW, dtype=jnp.int32)[None, :] <= jnp.arange(NEW, dtype=jnp.int32)[:, None]
    fresh_scores = jnp.where(causal[None, :, None, None, :], fresh_scores, -jnp.inf)
    highest = jnp.maximum(jnp.max(cache_scores, -1), jnp.max(fresh_scores, -1))[..., None]
    cache_exp = jnp.exp(cache_scores - highest)
    fresh_exp = jnp.exp(fresh_scores - highest)
    total = jnp.sum(cache_exp, -1, keepdims=True) + jnp.sum(fresh_exp, -1, keepdims=True)
    cache_probs = (cache_exp / total).astype(jnp.bfloat16)
    fresh_probs = (fresh_exp / total).astype(jnp.bfloat16)
    context = jnp.einsum(
        "stkgp,spkd->stkgd", cache_probs, cache_values, preferred_element_type=jnp.float32
    )
    context = context + jnp.einsum(
        "stkgu,sukd->stkgd", fresh_probs, values_new, preferred_element_type=jnp.float32
    )
    return context.astype(jnp.bfloat16)


def local(hidden, gain, w_query, w_key, w_value, w_out, key_cache, value_cache, lengths):
    seq_count = key_cache.shape[0]
    slot_count = key_cache.shape[1]
    kv_local = key_cache.shape[2] // HD
    heads_local = w_query.shape[1] // HD
    group = heads_local // kv_local
    own_rows = seq_count * NEW
    gathered_raw = lax.all_gather(hidden, "gx", axis=0, tiled=True)
    gathered_f = gathered_raw.astype(jnp.float32)
    scaled_in = (gathered_f * gain.astype(jnp.float32)[None, :]).astype(jnp.bfloat16)
    squares = jnp.sum(gathered_f * gathered_f, axis=1)
    first_row = lax.axis_index("gy") * own_rows
    totals = lax.psum(squares, "gy")
    own_totals = lax.dynamic_slice_in_dim(totals, first_row, own_rows, 0)
    positions = (lengths[:, None] + jnp.arange(NEW, dtype=jnp.int32)[None, :]).reshape(-1)
    cache_k = key_cache.reshape(seq_count, slot_count, kv_local, HD)
    cache_v = value_cache.reshape(seq_count, slot_count, kv_local, HD)
    matrices = [w_query, w_key, w_value]
    pieces = [jnp.dot(scaled_in, matrix, preferred_element_type=jnp.float32) for matrix in matrices]
    summed = lax.psum_scatter(jnp.concatenate(pieces, 1), "gy", scatter_dimension=0, tiled=True)
    scales = lax.rsqrt(own_totals / D + EPSILON)[:, None]
    query_cols = heads_local * HD
    kv_cols = kv_local * HD
    key_raw = summed[:, query_cols : query_cols + kv_cols] * scales
    fresh_values = (summed[:, query_cols + kv_cols : query_cols + 2 * kv_cols] * scales).astype(
        jnp.bfloat16
    )
    fresh_keys = rotate(key_raw.reshape(own_rows, kv_local, HD), positions).astype(jnp.bfloat16)
    fresh_keys, fresh_values = (fresh_keys, fresh_values)
    rotated = rotate(
        (summed[:, :query_cols] * scales).reshape(own_rows, kv_local * group, HD), positions
    ).astype(jnp.bfloat16)
    queries = rotated.reshape(seq_count, NEW, kv_local, group, HD)
    context = attend(
        queries,
        fresh_keys.reshape(seq_count, NEW, kv_local, HD),
        fresh_values.reshape(seq_count, NEW, kv_local, HD),
        cache_k,
        cache_v,
        lengths,
    )
    context = context.reshape(own_rows, heads_local * HD)
    terms = jnp.dot(
        lax.all_gather(context, "gy", axis=0, tiled=True), w_out, preferred_element_type=jnp.float32
    )
    mixed = lax.psum_scatter(terms, "gx", scatter_dimension=0, tiled=True)
    layer_out = (hidden.astype(jnp.float32) + mixed).astype(jnp.bfloat16)
    return (layer_out, fresh_keys.reshape(own_rows, kv_local * HD), fresh_values)


def solution(mesh):
    return jax.shard_map(
        local,
        mesh=mesh,
        in_specs=(
            P("gx", "gy"),
            P("gy"),
            P("gy", "gx"),
            P("gy", "gx"),
            P("gy", "gx"),
            P("gx", "gy"),
            P("gy", None, "gx"),
            P("gy", None, "gx"),
            P("gy"),
        ),
        out_specs=(P("gx", "gy"), P("gy", "gx"), P("gy", "gx")),
        check_vma=False,
    )
```

profile of v0, /device:TPU:0, one launch (start us, length us, event | category | flops | bytes accessed | tf_op | source)
XLA Modules:
  0.0 260.5 jit_solution(6345378466875338306)
XLA Ops:
  7.2 0.7 all-gather.3.cloned.1.call-update
  8.0 0.7 convert_element_type.56
  8.6 28.8 %all-gather.3.cloned.1.call-done = bf16[1024,1024]{1,0:T(8,128)(2,1)} async-done(((bf16[128,1024]{1,0:T(8,128)(2,1)}), bf16[1024,1024]{1,0:T(8,128)(2,1)}) %all-gather.3.cloned.1.call-update) | async-done | bytes 2097168 | tf_op jit(solution)/shard_map/all_gather | solution.py:65
  37.4 2.5 fusion.16
  39.9 2.3 fusion.14
  42.2 4.5 %fusion.18 = f32[1024,2048]{1,0:T(8,128)S(1)} fusion(bf16[1024,2048]{1,0:T(8,128)(2,1)S(1)} %copy-done.5, bf16[1024,1024]{1,0:T(8,128)(2,1)S(1)} %copy-done.1, f32[1024]{0:T(1024)S(1)} %convert_element_type.56), kind=kOutput, calls=%fused_computation.22 | convolution fusion | flops 4298113024 | bytes 14684160 | tf_op jit(solution)/shard_map/dot_general | solution.py:76
  46.7 4.4 %pad_maximum_fusion = f32[1024,2304]{1,0:T(8,128)} fusion(f32[1024,128]{1,0:T(8,128)S(1)} %fusion.14, f32[1024,128]{1,0:T(8,128)S(1)} %fusion.16, f32[1024,2048]{1,0:T(8,128)S(1)} %fusion.18), kind=kLoop, calls=%fused_computation | loop fusion | flops 4718592 | bytes 18874368 | tf_op jit(solution)/shard_map/concatenate | solution.py:77
  51.2 0.6 copy-done.4
  52.3 0.5 fusion.5
  52.8 41.2 %psum.7 = f32[1024]{0:T(1024)S(1)} all-reduce(f32[1024]{0:T(1024)S(1)} %fusion.5), channel_id=1, replica_groups=mesh['gx'=8,'gy'=16] {'gy'}, use_global_device_ids=true, to_apply=%region_2.0 | all-reduce | flops 1024 | bytes 8192 | tf_op jit(solution)/shard_map/psum | solution.py:70
  94.1 45.0 %reduce-scatter.3.cloned.1.call-done = f32[64,2304]{1,0:T(8,128)} async-done(((f32[1024,2304]{1,0:T(8,128)}), f32[64,2304]{1,0:T(8,128)}) %reduce-scatter.3.cloned.1.call-update) | async-done | bytes 589840 | tf_op jit(solution)/shard_map/reduce_scatter | solution.py:77
  139.1 0.8 fusion.38
  140.2 1.1 fusion.28
  141.7 6.7 %fusion.8 = (f32[32,2,16]{2,1,0:T(2,128)S(1)}, f32[32,2,16,1024]{3,2,1,0:T(8,128)S(1)}) fusion(pred[32,1024]{1,0:T(8,128)(4,1)S(1)} %iota_compare_fusion, bf16[32,1024,128]{2,1,0:T(8,128)(2,1)} %param.15, bf16[32,2,16,64]{3,2,1,0:T(8,128)(2,1)S(1)} %bitcast.101, bf16[32,2,16,64]{3,2,1,0:T(8,128)(2,1)S(1)} %bitcast.99), kind=kOutput, calls=%fused_computation.14 | convolution fusion | flops 272104448 | bytes 12881920 | tf_op jit(solution)/shard_map/stkgd,spkd->stkgp/dot_general | solution.py:32
  148.4 0.8 fusion.48
  149.4 1.2 fusion.7
  150.7 2.0 fusion.20
  152.8 0.3 fusion.25
  153.1 0.8 copy.25
  153.9 50.9 %all-gather.5.cloned.1.call-done = bf16[1024,2048]{1,0:T(8,128)(2,1)} async-done(((bf16[64,2048]{1,0:T(8,128)(2,1)}), bf16[1024,2048]{1,0:T(8,128)(2,1)}) %all-gather.5.cloned.1.call-update) | async-done | bytes 4194320 | tf_op jit(solution)/shard_map/all_gather | solution.py:101
  204.8 9.9 %fusion.49 = f32[1024,1024]{1,0:T(8,128)} fusion(bf16[1024,2048]{1,0:T(8,128)(2,1)} %all-gather.5.cloned.1.call-done, bf16[2048,1024]{1,0:T(8,128)(2,1)} %param.14), kind=kOutput, calls=%fused_computation.71 | convolution fusion | flops 4294967296 | bytes 12582912 | tf_op jit(solution)/shard_map/dot_general | solution.py:100
  214.7 0.7 pad_maximum_fusion.4
  215.4 36.8 %reduce-scatter.5.cloned.1.call-done = f32[128,1024]{1,0:T(8,128)} async-done(((f32[1024,1024]{1,0:T(8,128)}), f32[128,1024]{1,0:T(8,128)}) %reduce-scatter.5.cloned.1.call-update) | async-done | bytes 524304 | tf_op jit(solution)/shard_map/reduce_scatter | solution.py:103
  252.2 1.8 add_convert_fusion
  (36 shorter events, 1.5 us)
Async XLA Ops:
  7.2 30.2 %copy-start = (bf16[1024,128]{1,0:T(8,128)(2,1)S(1)}, bf16[1024,128]{1,0:T(8,128)(2,1)}, u32[]{:S(2)}) copy-start(bf16[1024,128]{1,0:T(8,128)(2,1)} %param.12) | copy-start | bytes 786436
  7.2 30.2 %all-gather.3.cloned.1.call-start = ((), (), s32[]{:S(2)}) async-start(), calls=%async_computation.2 | async-start | bytes 2359296 | tf_op jit(solution)/shard_map/all_gather | solution.py:65
  7.9 131.2 %reduce-scatter.3.cloned.1.call-start = ((), (), s32[]{:S(2)}) async-start(), calls=%async_computation.3 | async-start | bytes 10027008 | tf_op jit(solution)/shard_map/reduce_scatter | solution.py:77
  37.4 4.8 %copy-start.1 = (bf16[1024,1024]{1,0:T(8,128)(2,1)S(1)}, bf16[1024,1024]{1,0:T(8,128)(2,1)}, u32[]{:S(2)}) copy-start(bf16[1024,1024]{1,0:T(8,128)(2,1)} %all-gather.3.cloned.1.call-done) | copy-start | bytes 6291460
  37.4 4.8 %copy-start.5 = (bf16[1024,2048]{1,0:T(8,128)(2,1)S(1)}, bf16[1024,2048]{1,0:T(8,128)(2,1)}, u32[]{:S(2)}) copy-start(bf16[1024,2048]{1,0:T(8,128)(2,1)} %param.11) | copy-start | bytes 12582916
  51.1 0.7 copy-start.4
  51.2 153.6 %all-gather.5.cloned.1.call-start = ((), (), s32[]{:S(2)}) async-start(), calls=%async_computation.4 | async-start | bytes 4456448 | tf_op jit(solution)/shard_map/all_gather | solution.py:101
  140.0 12.8 %copy-start.3 = (bf16[64,128]{1,0:T(8,128)(2,1)}, bf16[64,128]{1,0:T(8,128)(2,1)S(1)}, u32[]{:S(2)}) copy-start(bf16[64,128]{1,0:T(8,128)(2,1)S(1)} %get-tuple-element.3) | copy-start | bytes 49156
  141.7 9.0 %slice-start = ((s8[8388608]{0:T(1024)(128)(4,1)}), s8[4194304]{0:T(1024)(128)(4,1)S(1)}, s32[]{:S(2)}) async-start(s8[8388608]{0:T(1024)(128)(4,1)} %bitcast.110), calls=%async_computation.6 | async-start | bytes 8388608
  141.7 9.0 %slice-start.1 = ((s8[8388608]{0:T(1024)(128)(4,1)}), s8[4194304]{0:T(1024)(128)(4,1)S(1)}, s32[]{:S(2)}) async-start(s8[8388608]{0:T(1024)(128)(4,1)} %bitcast.110), calls=%async_computation.7 | async-start | bytes 8388608
  153.8 98.4 %reduce-scatter.5.cloned.1.call-start = ((), (), s32[]{:S(2)}) async-start(), calls=%async_computation.5 | async-start | bytes 4718592 | tf_op jit(solution)/shard_map/reduce_scatter | solution.py:103
  214.7 37.6 %copy-start.2 = (bf16[128,1024]{1,0:T(8,128)(2,1)S(1)}, bf16[128,1024]{1,0:T(8,128)(2,1)}, u32[]{:S(2)}) copy-start(bf16[128,1024]{1,0:T(8,128)(2,1)} %param.9) | copy-start | bytes 786436
Sparse Core Ops, SparseCore 0:
  9.7 27.6 all-gather.2
  51.3 87.8 reduce-scatter.2
  154.0 50.7 all-gather.4
  214.8 37.3 reduce-scatter.4
where the time goes:
time: 261 us
  waiting for transfers between devices  162 us (62%)
  blocking collectives  41.2 us (16%)
  matrix products  29 us (11%)
  between operations  14 us (5%)
  other arithmetic  12.3 us (5%)
    all_gather x1, waiting for transfers between devices, local(): lax.all_gather(context, 'gy', axis=0, tiled=True)  50.9 us
    reduce_scatter x1, waiting for transfers between devices, local(): lax.psum_scatter(jnp.concatenate(pieces, 1), 'gy', scatter_dimension=0, t...  45 us
    psum x1, blocking collectives, local(): totals = lax.psum(squares, 'gy')  41.2 us
    reduce_scatter x1, waiting for transfers between devices, local(): mixed = lax.psum_scatter(terms, 'gx', scatter_dimension=0, tiled=True)  36.8 us
    all_gather x1, waiting for transfers between devices, local(): gathered_raw = lax.all_gather(hidden, 'gx', axis=0, tiled=True)  28.8 us
    dot_general x1, matrix products, local(): jnp.dot(lax.all_gather(context, 'gy', axis=0, tiled=True), w_out, preferr...  9.89 us
    dot_general x3, matrix products, local(): jnp.dot(scaled_in, matrix, preferred_element_type=jnp.float32)  9.29 us
    dot_general x1, matrix products, attend(): jnp.einsum('stkgd,spkd->stkgp', queries, cache_keys, preferred_element_ty...  6.7 us
  transfers between devices with their start and end apart: 4, of which 4 were waited for; matrix products, arithmetic and copies ran while one was open for 1% of the time, Pallas kernels for 0%

commit v1 on v0

v1 whole, which is shorter than its diff:
```python
import functools

import jax
import jax.numpy as jnp
from jax import lax
from jax.experimental import pallas as pl
from jax.experimental.pallas import tpu as pltpu
from jax.sharding import PartitionSpec as P

D = 16384
HD = 128
NEW = 2
EPSILON = 1e-05
ROPE_BASE = 500000.0

NY = NZ = NX = 4
NC = 2
AXES = ("gx", "gy")
BF16 = jnp.bfloat16
F32 = jnp.float32
VMEM_LIMIT = 60 * 1024 * 1024


def pairs(move):
    out = []
    for y in range(NY):
        for c in range(NC):
            for z in range(NZ):
                for x in range(NX):
                    y2, c2, z2, x2 = move(y, c, z, x)
                    source = ((y * NC + c) * NZ + z) * NX + x
                    target = (((y2 % NY) * NC + c2 % NC) * NZ + z2 % NZ) * NX + x2 % NX
                    out.append((source, target))
    return out


def swap_core(value):
    return lax.ppermute(value, AXES, pairs(lambda y, c, z, x: (y, c + 1, z, x)))


def shift_y(value, step):
    return lax.ppermute(value, AXES, pairs(lambda y, c, z, x: (y + step, c, z, x)))


def shift_first(value, step):
    def move(y, c, z, x):
        return (y, c, z, x + step) if c == 0 else (y, c, z + step, x)

    return lax.ppermute(value, AXES, pairs(move))


def shift_second(value, step):
    def move(y, c, z, x):
        return (y, c, z + step, x) if c == 0 else (y, c, z, x + step)

    return lax.ppermute(value, AXES, pairs(move))


VSPEC = pl.BlockSpec(memory_space=pltpu.VMEM)
SSPEC = pl.BlockSpec(memory_space=pltpu.SMEM)
ANYSPEC = pl.BlockSpec(memory_space=pl.ANY)


def call(body, outs, in_specs, name, scratch=(), flops=0, moved=0):
    return pl.pallas_call(
        body,
        out_shape=outs,
        in_specs=in_specs,
        out_specs=[VSPEC] * len(outs),
        scratch_shapes=list(scratch),
        compiler_params=pltpu.CompilerParams(vmem_limit_bytes=VMEM_LIMIT),
        cost_estimate=pl.CostEstimate(flops=flops, bytes_accessed=moved, transcendentals=0),
        name=name,
    )


def shape(dims, dtype=BF16):
    return jax.ShapeDtypeStruct(dims, dtype)


def split_high_low(total):
    high = total.astype(BF16).astype(F32)
    return jnp.concatenate([high, total - high], axis=0).astype(BF16)


def scale_body(rows, pos_ref, gain_ref, *refs):
    blocks, (hs_ref, sq_ref) = refs[:8], refs[8:]
    gain = gain_ref[...].astype(F32)
    ones = jnp.ones((8, gain.shape[1]), BF16)
    pad = jnp.zeros((HD - rows, gain.shape[1]), BF16)
    for i, block in enumerate(blocks):
        for j in range(2):
            value = block[j * rows : (j + 1) * rows, :].astype(F32)
            slot = pos_ref[2 * i + j]
            hs_ref[slot] = (value * gain).astype(BF16)
            square = value * value
            high = square.astype(BF16)
            low = (square - high.astype(F32)).astype(BF16)
            total = jnp.zeros((8, HD), F32)
            for part in (high, low):
                total += lax.dot_general(
                    ones,
                    jnp.concatenate([part, pad], axis=0),
                    (((1,), (1,)), ((), ())),
                    preferred_element_type=F32,
                )
            sq_ref[slot] = split_high_low(total)


def project_body(rows, heads, group, hs_ref, sq_ref, wq_ref, wkv_ref, out_ref):
    depth = hs_ref.shape[2]
    lhs = hs_ref[4 * group : 4 * group + 4].reshape(4 * rows, depth)
    for n in range(heads // 2 + 1):
        rhs = wkv_ref[...] if n == heads // 2 else wq_ref[:, n * 256 : (n + 1) * 256]
        acc = jnp.dot(lhs, rhs, preferred_element_type=F32).astype(BF16)
        for f in range(4):
            for hh in range(2):
                head = 2 * n + hh
                out_ref[f, head * rows : (head + 1) * rows, :] = acc[
                    f * rows : (f + 1) * rows, hh * HD : (hh + 1) * HD
                ]
    for f in range(4):
        out_ref[f, (heads + 2) * rows :, :] = sq_ref[4 * group + f]


def first_sum_body(main, own_ref, r1_ref, r2_ref, r3_ref, *outs):
    for f in range(4):
        total = (
            own_ref[f].astype(F32)
            + r1_ref[f].astype(F32)
            + r2_ref[f].astype(F32)
            + r3_ref[f].astype(F32)
        )
        if f == 0:
            outs[0][...] = total
        else:
            outs[f][0:main, :] = total[:main].astype(BF16)
            outs[f][main:, :] = split_high_low(total[main : main + 8] + total[main + 8 :])


def attend_body(
    rows, heads, len_ref, p0_ref, r1_ref, r2_ref, r3_ref, cos_ref, sin_ref, kc_ref, vc_ref,
    ctx_ref, nk_ref, nv_ref, kbuf, vbuf, qs, os, kf, vf, sems,
):
    seqs = rows // NEW
    slots = kbuf.shape[1]
    main = (heads + 2) * rows

    def copies(s):
        return (
            pltpu.make_async_copy(kc_ref.at[s], kbuf.at[s], sems.at[s, 0]),
            pltpu.make_async_copy(vc_ref.at[s], vbuf.at[s], sems.at[s, 1]),
        )

    def start(s, carry):
        for copy in copies(s):
            copy.start()
        return carry

    lax.fori_loop(0, seqs, start, 0)

    def total(lo, hi):
        return (
            p0_ref[lo:hi, :]
            + r1_ref[lo:hi, :].astype(F32)
            + r2_ref[lo:hi, :].astype(F32)
            + r3_ref[lo:hi, :].astype(F32)
        )

    square = total(main, main + 16)
    column = jnp.transpose(square[:8] + square[8:])[:rows, 0:1]
    scales = lax.rsqrt(column / D + EPSILON)
    cosine, sine = cos_ref[...], sin_ref[...]

    def rope(value):
        return value * cosine + pltpu.roll(value, HD // 2, 1) * sine

    for head in range(heads):
        value = total(head * rows, (head + 1) * rows) * scales
        qs[pl.ds(head, rows, stride=heads), :] = rope(value).astype(BF16).astype(F32)
    key = rope(total(heads * rows, (heads + 1) * rows) * scales).astype(BF16)
    nk_ref[...] = key
    kf[...] = key.astype(F32)
    fresh = (total((heads + 1) * rows, (heads + 2) * rows) * scales).astype(BF16)
    nv_ref[...] = fresh
    vf[...] = fresh.astype(F32)

    per = NEW * heads
    scale = HD ** (-0.5)
    slot_of = lax.broadcasted_iota(jnp.int32, (per, slots), 1)
    second = lax.broadcasted_iota(jnp.int32, (per, 1), 0) >= heads

    def one(s):
        for copy in copies(s):
            copy.wait()
        query = qs[pl.ds(pl.multiple_of(s * per, per), per), :]
        k0, k1 = kf[pl.ds(2 * s, 1), :], kf[pl.ds(2 * s + 1, 1), :]
        v0, v1 = vf[pl.ds(2 * s, 1), :], vf[pl.ds(2 * s + 1, 1), :]
        s0 = jnp.sum(query * k0, axis=1, keepdims=True) * scale
        s1 = jnp.sum(query * k1, axis=1, keepdims=True) * scale
        s1 = jnp.where(second, s1, -jnp.inf)
        scores = (
            lax.dot_general(
                query.astype(BF16), kbuf[s], (((1,), (1,)), ((), ())), preferred_element_type=F32
            )
            * scale
        )
        scores = jnp.where(slot_of < len_ref[s], scores, -jnp.inf)
        highest = jnp.maximum(jnp.max(scores, axis=1, keepdims=True), jnp.maximum(s0, s1))
        probs = jnp.exp(scores - highest)
        p0, p1 = jnp.exp(s0 - highest), jnp.exp(s1 - highest)
        norm = 1.0 / (jnp.sum(probs, axis=1, keepdims=True) + p0 + p1)
        out = jnp.dot((probs * norm).astype(BF16), vbuf[s], preferred_element_type=F32)
        out += (p0 * norm).astype(BF16).astype(F32) * v0 + (p1 * norm).astype(BF16).astype(F32) * v1
        os[pl.ds(pl.multiple_of(s * per, per), per), :] = out

    def step(i, carry):
        for u in range(2):
            one(2 * i + u)
        return carry

    lax.fori_loop(0, seqs // 2, step, 0)
    for head in range(heads):
        ctx_ref[:, head * HD : (head + 1) * HD] = os[pl.ds(head, rows, stride=heads), :].astype(BF16)


def output_body(rows, pos_ref, *refs):
    a_refs, b_refs, (w_ref, mine_ref, theirs_ref) = refs[:4], refs[4:7], refs[7:]
    width = w_ref.shape[1]
    for f in range(4):
        if f == 0:
            lhs = jnp.concatenate([a[...] for a in a_refs], axis=0)
        else:
            lhs = b_refs[f - 1][...]
        for n in range(width // 256):
            cols = slice(n * 256, (n + 1) * 256)
            acc = jnp.dot(lhs, w_ref[:, cols], preferred_element_type=F32).astype(BF16)
            for e in range(4):
                slot = pos_ref[4 * f + e]
                part = acc[e * rows : (e + 1) * rows]

                @pl.when(slot < 8)
                def _(slot=slot, part=part, cols=cols):
                    mine_ref[slot, :, cols] = part

                @pl.when(slot >= 8)
                def _(slot=slot, part=part, cols=cols):
                    theirs_ref[slot - 8, :, cols] = part


def local(hidden, gain, w_query, w_key, w_value, w_out, key_cache, value_cache, lengths):
    seqs = key_cache.shape[0]
    slots = key_cache.shape[1]
    heads = w_query.shape[1] // HD
    rows = seqs * NEW
    depth = hidden.shape[1]
    width = w_out.shape[1]
    gx, gy = lax.axis_index("gx"), lax.axis_index("gy")
    y, c, z, x = gx // NC, gx % NC, gy // NX, gy % NX
    first_axis_x = c == 0

    positions = (lengths[:, None] + jnp.arange(NEW, dtype=jnp.int32)[None, :]).reshape(-1)
    indices = jnp.arange(HD // 2, dtype=F32)
    inverse = jnp.power(F32(ROPE_BASE), -2.0 * indices / HD)
    angles = positions.astype(F32)[:, None] * inverse[None, :]
    cosine, sine = jnp.cos(angles), jnp.sin(angles)
    cosine = jnp.concatenate([cosine, cosine], 1)
    sine = jnp.concatenate([-sine, sine], 1)
    w_kv = jnp.concatenate([w_key, w_value], 1)

    own = hidden
    received = [own] + [shift_y(own, d) for d in (1, 2, 3)]
    blocks = []
    for value in received:
        blocks += [value, swap_core(value)]

    places = []
    for d in range(4):
        for k in range(2):
            for j in range(2):
                zz, xx = (y - d) % 4, 2 * (c ^ k) + j
                dz, dx = (zz - z) % 4, (xx - x) % 4
                e, f = jnp.where(first_axis_x, dx, dz), jnp.where(first_axis_x, dz, dx)
                places.append(4 * e + f)
    places = jnp.stack(places).astype(jnp.int32)
    scaled, squares = call(
        functools.partial(scale_body, rows),
        [shape((16, rows, depth)), shape((16, 16, HD))],
        [SSPEC] + [VSPEC] * 9,
        "scale_rows",
        flops=4 * 16 * rows * depth,
        moved=8 * 16 * rows * depth,
    )(places, gain.reshape(1, -1), *blocks)

    main = (heads + 2) * rows
    length = main + 16

    def project(e):
        return call(
            functools.partial(project_body, rows, heads, e),
            [shape((4, length, HD))],
            [VSPEC] * 4,
            "project_%d" % e,
            flops=2 * 4 * rows * depth * (heads + 2) * HD,
            moved=2 * depth * (heads + 2) * HD,
        )(scaled, squares, w_query, w_kv)[0]

    sent = {e: shift_first(project(e), e) for e in (2, 1, 3)}
    kept = project(0)
    sums = call(
        functools.partial(first_sum_body, main),
        [shape((length, HD), F32)] + [shape((length, HD))] * 3,
        [VSPEC] * 4,
        "first_sum",
        flops=16 * length * HD,
        moved=10 * length * HD,
    )(kept, sent[1], sent[2], sent[3])
    arrived = [shift_second(sums[f], f) for f in (1, 2, 3)]

    context, fresh_keys, fresh_values = call(
        functools.partial(attend_body, rows, heads),
        [shape((rows, heads * HD)), shape((rows, HD)), shape((rows, HD))],
        [SSPEC] + [VSPEC] * 6 + [ANYSPEC] * 2,
        "attend",
        scratch=[
            pltpu.VMEM((seqs, slots, HD), BF16),
            pltpu.VMEM((seqs, slots, HD), BF16),
            pltpu.VMEM((rows * heads, HD), F32),
            pltpu.VMEM((rows * heads, HD), F32),
            pltpu.VMEM((rows, HD), F32),
            pltpu.VMEM((rows, HD), F32),
            pltpu.SemaphoreType.DMA((seqs, 2)),
        ],
        flops=4 * rows * heads * slots * HD,
        moved=4 * seqs * slots * HD,
    )(lengths, sums[0], *arrived, cosine, sine, key_cache, value_cache)

    near = [context] + [shift_first(context, e) for e in (1, 2, 3)]
    stacked = jnp.concatenate(near, axis=0)
    far = [shift_second(stacked, f) for f in (1, 2, 3)]
    places = []
    for f in range(4):
        for e in range(4):
            zz = jnp.where(first_axis_x, z - f, z - e) % 4
            xx = jnp.where(first_axis_x, x - e, x - f) % 4
            places.append(8 * ((xx // 2) ^ c) + 2 * ((zz - y) % 4) + xx % 2)
    places = jnp.stack(places).astype(jnp.int32)
    mine, theirs = call(
        functools.partial(output_body, rows),
        [shape((8, rows, width)), shape((8, rows, width))],
        [SSPEC] + [VSPEC] * 8,
        "project_out",
        flops=2 * 16 * rows * heads * HD * width,
        moved=2 * heads * HD * width,
    )(places, *near, *far, w_out)

    both = mine.astype(F32) + swap_core(theirs).astype(F32)
    both = both.reshape(4, 2 * rows, width)
    result = hidden.astype(F32) + both[0]
    for value in [shift_y(both[g].astype(BF16), g) for g in (1, 2, 3)]:
        result = result + value.astype(F32)
    return result.astype(BF16), fresh_keys, fresh_values


def solution(mesh):
    return jax.shard_map(
        local,
        mesh=mesh,
        in_specs=(
            P("gx", "gy"),
            P("gy"),
            P("gy", "gx"),
            P("gy", "gx"),
            P("gy", "gx"),
            P("gx", "gy"),
            P("gy", None, "gx"),
            P("gy", None, "gx"),
            P("gy"),
        ),
        out_specs=(P("gx", "gy"), P("gy", "gx"), P("gy", "gx")),
        check_vma=False,
    )
```

time: 261 us -> 195 us (0.75)
  waiting for transfers between devices: 162 us -> 81.7 us
  Pallas kernels: 0 us -> 66.4 us
  blocking collectives: 41.2 us -> 0 us
  starting transfers between devices: 0.16 us -> 32 us
  matrix products: 29 us -> 0 us
  between operations: 14 us -> 0.87 us
  other arithmetic: 12.3 us -> 3.57 us
  local copies, waits for them, and re-layouts: 1.59 us -> 9.27 us
    reduce_scatter x2 -> x0, waiting for transfers between devices: 81.9 us -> none  [the longest x1 45 us: local(): lax.psum_scatter(jnp.concatenate(pieces, 1), 'gy', scatter_dimension=0, t...]
    ppermute x0 -> x23, waiting for transfers between devices: none -> 81.7 us  [the longest x6 28.8 us: shift_second(): return lax.ppermute(value, AXES, pairs(move))]
    all_gather x2 -> x0, waiting for transfers between devices: 79.6 us -> none  [the longest x1 50.9 us: local(): lax.all_gather(context, 'gy', axis=0, tiled=True)]
    pallas_call x0 -> x8, Pallas kernels: none -> 66.4 us  [the longest x4 21.5 us: project(): call(functools.partial(project_body, rows, heads, e), [shape((4, length,...]
    psum x1 -> x0, blocking collectives: 41.2 us -> none  [local(): totals = lax.psum(squares, 'gy')]
    ppermute x0 -> x23, starting transfers between devices: none -> 32 us  [the longest x6 11.6 us: shift_second(): return lax.ppermute(value, AXES, pairs(move))]
    dot_general x8 -> x0, matrix products: 29 us -> none  [the longest x1 9.89 us: local(): jnp.dot(lax.all_gather(context, 'gy', axis=0, tiled=True), w_out, preferr...]
    concatenate x2 -> x1, other arithmetic: 5.09 us -> 0.72 us  [local(): cosine = jnp.concatenate([cosine, cosine], 1)]
  transfers between devices with their start and end apart: 4 -> 23, of which waited for: 4 -> 15; matrix products, arithmetic and copies ran while one was open for 1% -> 3% of each run, Pallas kernels for 0% -> 3%
where the time goes in v1:
time: 195 us; the launch traced here: 194 us
  waiting for transfers between devices  81.7 us (42%)
  Pallas kernels  66.4 us (34%)
  starting transfers between devices  32 us (16%)
  local copies, waits for them, and re-layouts  9.27 us (5%)
  other arithmetic  3.57 us (2%)
    ppermute x6, waiting for transfers between devices, shift_second(): return lax.ppermute(value, AXES, pairs(move))  28.8 us
    ppermute x6, waiting for transfers between devices, shift_first(): return lax.ppermute(value, AXES, pairs(move))  26.2 us
    ppermute x6, waiting for transfers between devices, shift_y(): lax.ppermute(value, AXES, pairs(lambda y, c, z, x: (y + step, c, z, x)))  23.8 us
    pallas_call x4, Pallas kernels, project(): call(functools.partial(project_body, rows, heads, e), [shape((4, length,...  21.5 us
    pallas_call x1, Pallas kernels, local(): call(functools.partial(attend_body, rows, heads), [shape((rows, heads * H...  20.7 us
    pallas_call x1, Pallas kernels, local(): call(functools.partial(output_body, rows), [shape((8, rows, width)), shap...  16.5 us
    ppermute x6, starting transfers between devices, shift_second(): return lax.ppermute(value, AXES, pairs(move))  11.6 us
    ppermute x6, starting transfers between devices, shift_first(): return lax.ppermute(value, AXES, pairs(move))  10.4 us
  transfers between devices with their start and end apart: 23, of which 15 were waited for; matrix products, arithmetic and copies ran while one was open for 3% of the time, Pallas kernels for 3%

profile of v1, /device:TPU:0, one launch (start us, length us, event | category | flops | bytes accessed | tf_op | source)
XLA Modules:
  0.0 193.9 jit_solution(501454487070609741)
XLA Ops:
  2.4 2.9 %collective-permute-start.3 = (bf16[128,1024]{1,0:T(8,128)(2,1)}, bf16[128,1024]{1,0:T(8,128)(2,1)S(1)}, u32[]{:S(2)}, u32[]{:S(2)}) collective-permute-start(bf16[128,1024]{1,0:T(8,128)(2,1)} %refs_0_.1), channel_id=1, source_target_pairs={{0,64},{1,65},{2,66},{3,67},{4,68},{5,69},{6,70},{7,71},{8,72},{9,... | collective-permute-start | bytes 786440 | tf_op jit(solution)/shard_map/ppermute | solution.py:42
  6.6 3.7 %collective-permute-done.1.refs_2_ = bf16[128,1024]{1,0:T(8,128)(2,1)S(1)} collective-permute-done((bf16[128,1024]{1,0:T(8,128)(2,1)}, bf16[128,1024]{1,0:T(8,128)(2,1)S(1)}, u32[]{:S(2)}, u32[]{:S(2)}) %collective-permute-start.1) | collective-permute-done | bytes 262176 | tf_op jit(solution)/shard_map/ppermute | solution.py:42
  10.3 6.8 %collective-permute-done.3.refs_4_ = bf16[128,1024]{1,0:T(8,128)(2,1)S(1)} collective-permute-done((bf16[128,1024]{1,0:T(8,128)(2,1)}, bf16[128,1024]{1,0:T(8,128)(2,1)S(1)}, u32[]{:S(2)}, u32[]{:S(2)}) %collective-permute-start.3) | collective-permute-done | bytes 262176 | tf_op jit(solution)/shard_map/ppermute | solution.py:42
  23.2 4.1 %scale_rows.1 = (bf16[16,64,1024]{2,1,0:T(8,128)(2,1)}, bf16[16,16,128]{2,1,0:T(8,128)(2,1)}) custom-call(s32[16]{0:T(128)} %stack.135.pos_ref, bf16[1,1024]{1,0:T(2,128)(2,1)} %reshape.42.gain_ref, bf16[128,1024]{1,0:T(8,128)(2,1)} %refs_0_.1, bf16[128,1024]{1,0:T(8,128)(2,1)} %copy-done.10, bf16[128,1024]{1,0:T(8,128)(2,1)} %copy-done.7, ...), custom_call_target="tpu_custom_call" | custom-call | flops 4194304 | bytes 8388608 | tf_op jit(solution)/shard_map/scale_rows/pallas_call | solution.py:286
  27.3 5.4 %project_1.1 = bf16[4,1168,128]{2,1,0:T(8,128)(2,1)} custom-call(bf16[16,64,1024]{2,1,0:T(8,128)(2,1)} %get-tuple-element.14.hs_ref, bf16[16,16,128]{2,1,0:T(8,128)(2,1)} %get-tuple-element.15.sq_ref, bf16[1024,2048]{1,0:T(8,128)(2,1)} %wq_ref.7, bf16[1024,256]{1,0:T(8,128)(2,1)} %copy-done), custom_call_target="tpu_custom_call" | custom-call | flops 1207959552 | bytes 4718592 | tf_op jit(solution)/shard_map/project_1/pallas_call | solution.py:299
  32.7 5.3 %project_2.1 = bf16[4,1168,128]{2,1,0:T(8,128)(2,1)} custom-call(bf16[16,64,1024]{2,1,0:T(8,128)(2,1)} %get-tuple-element.14.hs_ref, bf16[16,16,128]{2,1,0:T(8,128)(2,1)} %get-tuple-element.15.sq_ref, bf16[1024,2048]{1,0:T(8,128)(2,1)} %wq_ref.7, bf16[1024,256]{1,0:T(8,128)(2,1)} %copy-done), custom_call_target="tpu_custom_call" | custom-call | flops 1207959552 | bytes 4718592 | tf_op jit(solution)/shard_map/project_2/pallas_call | solution.py:299
  38.1 5.4 %project_3.1 = bf16[4,1168,128]{2,1,0:T(8,128)(2,1)} custom-call(bf16[16,64,1024]{2,1,0:T(8,128)(2,1)} %get-tuple-element.14.hs_ref, bf16[16,16,128]{2,1,0:T(8,128)(2,1)} %get-tuple-element.15.sq_ref, bf16[1024,2048]{1,0:T(8,128)(2,1)} %wq_ref.7, bf16[1024,256]{1,0:T(8,128)(2,1)} %copy-done), custom_call_target="tpu_custom_call" | custom-call | flops 1207959552 | bytes 4718592 | tf_op jit(solution)/shard_map/project_3/pallas_call | solution.py:299
  44.9 2.7 %collective-permute-start.8 = (bf16[4,1168,128]{2,1,0:T(8,128)(2,1)}, bf16[4,1168,128]{2,1,0:T(8,128)(2,1)S(1)}, u32[]{:S(2)}, u32[]{:S(2)}) collective-permute-start(bf16[4,1168,128]{2,1,0:T(8,128)(2,1)} %project_2.1), channel_id=1, source_target_pairs={{0,2},{1,3},{2,0},{3,1},{4,6},{5,7},{6,4},{7,5},{8,10},{9,11},{10,... | collective-permute-start | bytes 3588104 | tf_op jit(solution)/shard_map/ppermute | solution.py:49
  49.3 5.3 %project_0.1.own_ref = bf16[4,1168,128]{2,1,0:T(8,128)(2,1)} custom-call(bf16[16,64,1024]{2,1,0:T(8,128)(2,1)} %get-tuple-element.14.hs_ref, bf16[16,16,128]{2,1,0:T(8,128)(2,1)} %get-tuple-element.15.sq_ref, bf16[1024,2048]{1,0:T(8,128)(2,1)} %wq_ref.7, bf16[1024,256]{1,0:T(8,128)(2,1)} %copy-done), custom_call_target="tpu_custom_call" | custom-call | flops 1207959552 | bytes 4718592 | tf_op jit(solution)/shard_map/project_0/pallas_call | solution.py:299
  54.6 6.6 %collective-permute-done.7.r1_ref = bf16[4,1168,128]{2,1,0:T(8,128)(2,1)S(1)} collective-permute-done((bf16[4,1168,128]{2,1,0:T(8,128)(2,1)}, bf16[4,1168,128]{2,1,0:T(8,128)(2,1)S(1)}, u32[]{:S(2)}, u32[]{:S(2)}) %collective-permute-start.7) | collective-permute-done | bytes 1196064 | tf_op jit(solution)/shard_map/ppermute | solution.py:49
  61.2 13.8 %collective-permute-done.8.r2_ref = bf16[4,1168,128]{2,1,0:T(8,128)(2,1)S(1)} collective-permute-done((bf16[4,1168,128]{2,1,0:T(8,128)(2,1)}, bf16[4,1168,128]{2,1,0:T(8,128)(2,1)S(1)}, u32[]{:S(2)}, u32[]{:S(2)}) %collective-permute-start.8) | collective-permute-done | bytes 1196064 | tf_op jit(solution)/shard_map/ppermute | solution.py:49
  76.1 3.7 %first_sum.1 = (f32[1168,128]{1,0:T(8,128)}, bf16[1168,128]{1,0:T(8,128)(2,1)}, bf16[1168,128]{1,0:T(8,128)(2,1)}, bf16[1168,128]{1,0:T(8,128)(2,1)}) custom-call(bf16[4,1168,128]{2,1,0:T(8,128)(2,1)} %project_0.1.own_ref, bf16[4,1168,128]{2,1,0:T(8,128)(2,1)} %copy-done.1, bf16[4,1168,128]{2,1,0:T(8,128)(2,1)} %copy-done.2, ...), custom_call_target="tpu_custom_call" | custom-call | flops 2392064 | bytes 1495040 | tf_op jit(solution)/shard_map/first_sum/pallas_call | solution.py:310
  81.7 3.6 %collective-permute-start.11 = (bf16[1168,128]{1,0:T(8,128)(2,1)}, bf16[1168,128]{1,0:T(8,128)(2,1)S(1)}, u32[]{:S(2)}, u32[]{:S(2)}) collective-permute-start(bf16[1168,128]{1,0:T(8,128)(2,1)} %get-tuple-element.18), channel_id=1, source_target_pairs={{0,8},{1,9},{2,10},{3,11},{4,12},{5,13},{6,14},{7,15},{8,0},{9,1},... | collective-permute-start | bytes 897032 | tf_op jit(solution)/shard_map/ppermute | solution.py:56
  88.7 4.7 %collective-permute-done.11.r2_ref = bf16[1168,128]{1,0:T(8,128)(2,1)S(1)} collective-permute-done((bf16[1168,128]{1,0:T(8,128)(2,1)}, bf16[1168,128]{1,0:T(8,128)(2,1)S(1)}, u32[]{:S(2)}, u32[]{:S(2)}) %collective-permute-start.11) | collective-permute-done | bytes 299040 | tf_op jit(solution)/shard_map/ppermute | solution.py:56
  94.3 20.7 %attend.1 = (bf16[64,2048]{1,0:T(8,128)(2,1)}, bf16[64,128]{1,0:T(8,128)(2,1)}, bf16[64,128]{1,0:T(8,128)(2,1)}) custom-call(s32[32]{0:T(128)} %len_ref.1, f32[1168,128]{1,0:T(8,128)} %get-tuple-element.16.p0_ref, bf16[1168,128]{1,0:T(8,128)(2,1)} %copy-done.4, bf16[1168,128]{1,0:T(8,128)(2,1)} %copy-done.5, bf16[1168,128]{1,0:T(8,128)(2,1)} %copy-done.6, ...), custom_call_target="tpu_custom_call" | custom-call | flops 536870912 | bytes 16777216 | tf_op jit(solution)/shard_map/attend/pallas_call | solution.py:320
  116.0 2.1 %collective-permute-start.14 = (bf16[64,2048]{1,0:T(8,128)(2,1)}, bf16[64,2048]{1,0:T(8,128)(2,1)S(1)}, u32[]{:S(2)}, u32[]{:S(2)}) collective-permute-start(bf16[64,2048]{1,0:T(8,128)(2,1)} %get-tuple-element.20.refs_0_), channel_id=1, source_target_pairs={{0,2},{1,3},{2,0},{3,1},{4,6},{5,7},{6,4},{7,5},{8,10},{9,11},{10,... | collective-permute-start | bytes 786440 | tf_op jit(solution)/shard_map/ppermute | solution.py:49
  120.7 4.9 %collective-permute-done.13.refs_1_ = bf16[64,2048]{1,0:T(8,128)(2,1)S(1)} collective-permute-done((bf16[64,2048]{1,0:T(8,128)(2,1)}, bf16[64,2048]{1,0:T(8,128)(2,1)S(1)}, u32[]{:S(2)}, u32[]{:S(2)}) %collective-permute-start.13) | collective-permute-done | bytes 262176 | tf_op jit(solution)/shard_map/ppermute | solution.py:49
  132.3 10.3 %collective-permute-done.16.refs_4_ = bf16[256,2048]{1,0:T(8,128)(2,1)S(1)} collective-permute-done((bf16[256,2048]{1,0:T(8,128)(2,1)S(1)}, bf16[256,2048]{1,0:T(8,128)(2,1)S(1)}, u32[]{:S(2)}, u32[]{:S(2)}) %collective-permute-start.16) | collective-permute-done | bytes 1048608 | tf_op jit(solution)/shard_map/ppermute | solution.py:56
  142.6 11.5 %collective-permute-done.17.refs_5_ = bf16[256,2048]{1,0:T(8,128)(2,1)} collective-permute-done((bf16[256,2048]{1,0:T(8,128)(2,1)S(1)}, bf16[256,2048]{1,0:T(8,128)(2,1)}, u32[]{:S(2)}, u32[]{:S(2)}) %collective-permute-start.17) | collective-permute-done | bytes 1048608 | tf_op jit(solution)/shard_map/ppermute | solution.py:56
  154.8 16.5 %project_out.1 = (bf16[8,64,1024]{2,1,0:T(8,128)(2,1)}, bf16[8,64,1024]{2,1,0:T(8,128)(2,1)}) custom-call(s32[16]{0:T(128)} %stack.118.pos_ref, bf16[64,2048]{1,0:T(8,128)(2,1)} %get-tuple-element.20.refs_0_, bf16[64,2048]{1,0:T(8,128)(2,1)} %copy-done.14, bf16[64,2048]{1,0:T(8,128)(2,1)} %copy-done.15, bf16[64,2048]{1,0:T(8,128)(2,1)} %copy-done.16, ...), custom_call_target="tpu_custom_call" | custom-call | flops 4294967296 | bytes 4194304 | tf_op jit(solution)/shard_map/project_out/pallas_call | solution.py:348
  171.4 2.9 %collective-permute-done.19 = bf16[8,64,1024]{2,1,0:T(8,128)(2,1)S(1)} collective-permute-done((bf16[8,64,1024]{2,1,0:T(8,128)(2,1)}, bf16[8,64,1024]{2,1,0:T(8,128)(2,1)S(1)}, u32[]{:S(2)}, u32[]{:S(2)}) %collective-permute-start.19) | collective-permute-done | bytes 1048608 | tf_op jit(solution)/shard_map/ppermute | solution.py:38
  179.6 5.6 %collective-permute-done.22 = bf16[128,1024]{1,0:T(8,128)(2,1)S(1)} collective-permute-done((bf16[128,1024]{1,0:T(8,128)(2,1)S(1)}, bf16[128,1024]{1,0:T(8,128)(2,1)S(1)}, u32[]{:S(2)}, u32[]{:S(2)}) %collective-permute-start.22) | collective-permute-done | bytes 262176 | tf_op jit(solution)/shard_map/ppermute | solution.py:42
  185.2 3.3 %collective-permute-done.21 = bf16[128,1024]{1,0:T(8,128)(2,1)S(1)} collective-permute-done((bf16[128,1024]{1,0:T(8,128)(2,1)S(1)}, bf16[128,1024]{1,0:T(8,128)(2,1)S(1)}, u32[]{:S(2)}, u32[]{:S(2)}) %collective-permute-start.21) | collective-permute-done | bytes 262176 | tf_op jit(solution)/shard_map/ppermute | solution.py:42
  188.5 4.4 %collective-permute-done.20 = bf16[128,1024]{1,0:T(8,128)(2,1)S(1)} collective-permute-done((bf16[128,1024]{1,0:T(8,128)(2,1)S(1)}, bf16[128,1024]{1,0:T(8,128)(2,1)S(1)}, u32[]{:S(2)}, u32[]{:S(2)}) %collective-permute-start.20) | collective-permute-done | bytes 262176 | tf_op jit(solution)/shard_map/ppermute | solution.py:42
  (86 shorter events, 36.7 us)
Async XLA Ops:
  0.6 9.7 %collective-permute-start.1 = (bf16[128,1024]{1,0:T(8,128)(2,1)}, bf16[128,1024]{1,0:T(8,128)(2,1)S(1)}, u32[]{:S(2)}, u32[]{:S(2)}) collective-permute-start(bf16[128,1024]{1,0:T(8,128)(2,1)} %refs_0_.1), channel_id=1, source_target_pairs={{0,32},{1,33},{2,34},{3,35},{4,36},{5,37},{6,38},{7,39},{8,40},{9,... | collective-permute-start | bytes 786440 | tf_op jit(solution)/shard_map/ppermute | solution.py:42
  2.4 14.7 %collective-permute-start.3 = (bf16[128,1024]{1,0:T(8,128)(2,1)}, bf16[128,1024]{1,0:T(8,128)(2,1)S(1)}, u32[]{:S(2)}, u32[]{:S(2)}) collective-permute-start(bf16[128,1024]{1,0:T(8,128)(2,1)} %refs_0_.1), channel_id=1, source_target_pairs={{0,64},{1,65},{2,66},{3,67},{4,68},{5,69},{6,70},{7,71},{8,72},{9,... | collective-permute-start | bytes 786440 | tf_op jit(solution)/shard_map/ppermute | solution.py:42
  5.3 11.9 %collective-permute-start.5 = (bf16[128,1024]{1,0:T(8,128)(2,1)}, bf16[128,1024]{1,0:T(8,128)(2,1)S(1)}, u32[]{:S(2)}, u32[]{:S(2)}) collective-permute-start(bf16[128,1024]{1,0:T(8,128)(2,1)} %refs_0_.1), channel_id=1, source_target_pairs={{0,96},{1,97},{2,98},{3,99},{4,100},{5,101},{6,102},{7,103},{8,104... | collective-permute-start | bytes 786440 | tf_op jit(solution)/shard_map/ppermute | solution.py:42
  6.6 15.0 %collective-permute-start = (bf16[128,1024]{1,0:T(8,128)(2,1)}, bf16[128,1024]{1,0:T(8,128)(2,1)S(1)}, u32[]{:S(2)}, u32[]{:S(2)}) collective-permute-start(bf16[128,1024]{1,0:T(8,128)(2,1)} %refs_0_.1), channel_id=1, source_target_pairs={{0,16},{1,17},{2,18},{3,19},{4,20},{5,21},{6,22},{7,23},{8,24},{9,... | collective-permute-start | bytes 786440 | tf_op jit(solution)/shard_map/ppermute | solution.py:38
  10.3 11.3 %collective-permute-start.2 = (bf16[128,1024]{1,0:T(8,128)(2,1)S(1)}, bf16[128,1024]{1,0:T(8,128)(2,1)S(1)}, u32[]{:S(2)}, u32[]{:S(2)}) collective-permute-start(bf16[128,1024]{1,0:T(8,128)(2,1)S(1)} %collective-permute-done.1.refs_2_), channel_id=1, source_target_pairs={{0,16},{1,17},{2,18},{3,19},{4,20},{5,21},{6,22},{7,23},{8,24},{9,... | collective-permute-start | bytes 786440 | tf_op jit(solution)/shard_map/ppermute | solution.py:38
  17.1 4.5 %collective-permute-start.4 = (bf16[128,1024]{1,0:T(8,128)(2,1)S(1)}, bf16[128,1024]{1,0:T(8,128)(2,1)S(1)}, u32[]{:S(2)}, u32[]{:S(2)}) collective-permute-start(bf16[128,1024]{1,0:T(8,128)(2,1)S(1)} %collective-permute-done.3.refs_4_), channel_id=1, source_target_pairs={{0,16},{1,17},{2,18},{3,19},{4,20},{5,21},{6,22},{7,23},{8,24},{9,... | collective-permute-start | bytes 786440 | tf_op jit(solution)/shard_map/ppermute | solution.py:38
  17.1 4.5 %collective-permute-start.6 = (bf16[128,1024]{1,0:T(8,128)(2,1)S(1)}, bf16[128,1024]{1,0:T(8,128)(2,1)S(1)}, u32[]{:S(2)}, u32[]{:S(2)}) collective-permute-start(bf16[128,1024]{1,0:T(8,128)(2,1)S(1)} %collective-permute-done.5.refs_6_), channel_id=1, source_target_pairs={{0,16},{1,17},{2,18},{3,19},{4,20},{5,21},{6,22},{7,23},{8,24},{9,... | collective-permute-start | bytes 786440 | tf_op jit(solution)/shard_map/ppermute | solution.py:38
  43.4 17.8 %collective-permute-start.7 = (bf16[4,1168,128]{2,1,0:T(8,128)(2,1)}, bf16[4,1168,128]{2,1,0:T(8,128)(2,1)S(1)}, u32[]{:S(2)}, u32[]{:S(2)}) collective-permute-start(bf16[4,1168,128]{2,1,0:T(8,128)(2,1)} %project_1.1), channel_id=1, source_target_pairs={{0,1},{1,2},{2,3},{3,0},{4,5},{5,6},{6,7},{7,4},{8,9},{9,10},{10,1... | collective-permute-start | bytes 3588104 | tf_op jit(solution)/shard_map/ppermute | solution.py:49
  44.9 30.1 %collective-permute-start.8 = (bf16[4,1168,128]{2,1,0:T(8,128)(2,1)}, bf16[4,1168,128]{2,1,0:T(8,128)(2,1)S(1)}, u32[]{:S(2)}, u32[]{:S(2)}) collective-permute-start(bf16[4,1168,128]{2,1,0:T(8,128)(2,1)} %project_2.1), channel_id=1, source_target_pairs={{0,2},{1,3},{2,0},{3,1},{4,6},{5,7},{6,4},{7,5},{8,10},{9,11},{10,... | collective-permute-start | bytes 3588104 | tf_op jit(solution)/shard_map/ppermute | solution.py:49
  47.7 27.4 %collective-permute-start.9 = (bf16[4,1168,128]{2,1,0:T(8,128)(2,1)}, bf16[4,1168,128]{2,1,0:T(8,128)(2,1)}, u32[]{:S(2)}, u32[]{:S(2)}) collective-permute-start(bf16[4,1168,128]{2,1,0:T(8,128)(2,1)} %project_3.1), channel_id=1, source_target_pairs={{0,3},{1,0},{2,1},{3,2},{4,7},{5,4},{6,5},{7,6},{8,11},{9,8},{10,9... | collective-permute-start | bytes 3588104 | tf_op jit(solution)/shard_map/ppermute | solution.py:49
  79.8 9.0 %collective-permute-start.10 = (bf16[1168,128]{1,0:T(8,128)(2,1)}, bf16[1168,128]{1,0:T(8,128)(2,1)S(1)}, u32[]{:S(2)}, u32[]{:S(2)}) collective-permute-start(bf16[1168,128]{1,0:T(8,128)(2,1)} %get-tuple-element.17), channel_id=1, source_target_pairs={{0,4},{1,5},{2,6},{3,7},{4,8},{5,9},{6,10},{7,11},{8,12},{9,13},{1... | collective-permute-start | bytes 897032 | tf_op jit(solution)/shard_map/ppermute | solution.py:56
  81.7 11.7 %collective-permute-start.11 = (bf16[1168,128]{1,0:T(8,128)(2,1)}, bf16[1168,128]{1,0:T(8,128)(2,1)S(1)}, u32[]{:S(2)}, u32[]{:S(2)}) collective-permute-start(bf16[1168,128]{1,0:T(8,128)(2,1)} %get-tuple-element.18), channel_id=1, source_target_pairs={{0,8},{1,9},{2,10},{3,11},{4,12},{5,13},{6,14},{7,15},{8,0},{9,1},... | collective-permute-start | bytes 897032 | tf_op jit(solution)/shard_map/ppermute | solution.py:56
  85.3 8.2 %collective-permute-start.12 = (bf16[1168,128]{1,0:T(8,128)(2,1)}, bf16[1168,128]{1,0:T(8,128)(2,1)S(1)}, u32[]{:S(2)}, u32[]{:S(2)}) collective-permute-start(bf16[1168,128]{1,0:T(8,128)(2,1)} %get-tuple-element.19), channel_id=1, source_target_pairs={{0,12},{1,13},{2,14},{3,15},{4,0},{5,1},{6,2},{7,3},{8,4},{9,5},{1... | collective-permute-start | bytes 897032 | tf_op jit(solution)/shard_map/ppermute | solution.py:56
  114.9 10.7 %collective-permute-start.13 = (bf16[64,2048]{1,0:T(8,128)(2,1)}, bf16[64,2048]{1,0:T(8,128)(2,1)S(1)}, u32[]{:S(2)}, u32[]{:S(2)}) collective-permute-start(bf16[64,2048]{1,0:T(8,128)(2,1)} %get-tuple-element.20.refs_0_), channel_id=1, source_target_pairs={{0,1},{1,2},{2,3},{3,0},{4,5},{5,6},{6,7},{7,4},{8,9},{9,10},{10,1... | collective-permute-start | bytes 786440 | tf_op jit(solution)/shard_map/ppermute | solution.py:49
  116.0 9.6 %collective-permute-start.14 = (bf16[64,2048]{1,0:T(8,128)(2,1)}, bf16[64,2048]{1,0:T(8,128)(2,1)S(1)}, u32[]{:S(2)}, u32[]{:S(2)}) collective-permute-start(bf16[64,2048]{1,0:T(8,128)(2,1)} %get-tuple-element.20.refs_0_), channel_id=1, source_target_pairs={{0,2},{1,3},{2,0},{3,1},{4,6},{5,7},{6,4},{7,5},{8,10},{9,11},{10,... | collective-permute-start | bytes 786440 | tf_op jit(solution)/shard_map/ppermute | solution.py:49
  118.1 8.4 %collective-permute-start.15 = (bf16[64,2048]{1,0:T(8,128)(2,1)}, bf16[64,2048]{1,0:T(8,128)(2,1)S(1)}, u32[]{:S(2)}, u32[]{:S(2)}) collective-permute-start(bf16[64,2048]{1,0:T(8,128)(2,1)} %get-tuple-element.20.refs_0_), channel_id=1, source_target_pairs={{0,3},{1,0},{2,1},{3,2},{4,7},{5,4},{6,5},{7,6},{8,11},{9,8},{10,9... | collective-permute-start | bytes 786440 | tf_op jit(solution)/shard_map/ppermute | solution.py:49
  125.6 29.2 %copy-start.14 = (bf16[64,2048]{1,0:T(8,128)(2,1)}, bf16[64,2048]{1,0:T(8,128)(2,1)S(1)}, u32[]{:S(2)}) copy-start(bf16[64,2048]{1,0:T(8,128)(2,1)S(1)} %collective-permute-done.13.refs_1_) | copy-start | bytes 786436
  126.5 16.1 %collective-permute-start.16 = (bf16[256,2048]{1,0:T(8,128)(2,1)S(1)}, bf16[256,2048]{1,0:T(8,128)(2,1)S(1)}, u32[]{:S(2)}, u32[]{:S(2)}) collective-permute-start(bf16[256,2048]{1,0:T(8,128)(2,1)S(1)} %constant_dynamic-update-slice_fusion.2), channel_id=1, source_target_pairs={{0,4},{1,5},{2,6},{3,7},{4,8},{5,9},{6,10},{7,11},{8,12},{9,13},{1... | collective-permute-start | bytes 3145736 | tf_op jit(solution)/shard_map/ppermute | solution.py:56
  127.9 26.2 %collective-permute-start.17 = (bf16[256,2048]{1,0:T(8,128)(2,1)S(1)}, bf16[256,2048]{1,0:T(8,128)(2,1)}, u32[]{:S(2)}, u32[]{:S(2)}) collective-permute-start(bf16[256,2048]{1,0:T(8,128)(2,1)S(1)} %constant_dynamic-update-slice_fusion.2), channel_id=1, source_target_pairs={{0,8},{1,9},{2,10},{3,11},{4,12},{5,13},{6,14},{7,15},{8,0},{9,1},... | collective-permute-start | bytes 3145736 | tf_op jit(solution)/shard_map/ppermute | solution.py:56
  130.0 24.9 %collective-permute-start.18 = (bf16[256,2048]{1,0:T(8,128)(2,1)S(1)}, bf16[256,2048]{1,0:T(8,128)(2,1)}, u32[]{:S(2)}, u32[]{:S(2)}) collective-permute-start(bf16[256,2048]{1,0:T(8,128)(2,1)S(1)} %constant_dynamic-update-slice_fusion.2), channel_id=1, source_target_pairs={{0,12},{1,13},{2,14},{3,15},{4,0},{5,1},{6,2},{7,3},{8,4},{9,5},{1... | collective-permute-start | bytes 3145736 | tf_op jit(solution)/shard_map/ppermute | solution.py:56
  171.4 2.9 %collective-permute-start.19 = (bf16[8,64,1024]{2,1,0:T(8,128)(2,1)}, bf16[8,64,1024]{2,1,0:T(8,128)(2,1)S(1)}, u32[]{:S(2)}, u32[]{:S(2)}) collective-permute-start(bf16[8,64,1024]{2,1,0:T(8,128)(2,1)} %get-tuple-element.22), channel_id=1, source_target_pairs={{0,16},{1,17},{2,18},{3,19},{4,20},{5,21},{6,22},{7,23},{8,24},{9,... | collective-permute-start | bytes 3145736 | tf_op jit(solution)/shard_map/ppermute | solution.py:38
  176.0 9.2 %collective-permute-start.22 = (bf16[128,1024]{1,0:T(8,128)(2,1)S(1)}, bf16[128,1024]{1,0:T(8,128)(2,1)S(1)}, u32[]{:S(2)}, u32[]{:S(2)}) collective-permute-start(bf16[128,1024]{1,0:T(8,128)(2,1)S(1)} %bitcast.47), channel_id=1, source_target_pairs={{0,96},{1,97},{2,98},{3,99},{4,100},{5,101},{6,102},{7,103},{8,104... | collective-permute-start | bytes 786440 | tf_op jit(solution)/shard_map/ppermute | solution.py:42
  177.8 10.7 %collective-permute-start.21 = (bf16[128,1024]{1,0:T(8,128)(2,1)S(1)}, bf16[128,1024]{1,0:T(8,128)(2,1)S(1)}, u32[]{:S(2)}, u32[]{:S(2)}) collective-permute-start(bf16[128,1024]{1,0:T(8,128)(2,1)S(1)} %bitcast.46), channel_id=1, source_target_pairs={{0,64},{1,65},{2,66},{3,67},{4,68},{5,69},{6,70},{7,71},{8,72},{9,... | collective-permute-start | bytes 786440 | tf_op jit(solution)/shard_map/ppermute | solution.py:42
  178.9 14.1 %collective-permute-start.20 = (bf16[128,1024]{1,0:T(8,128)(2,1)S(1)}, bf16[128,1024]{1,0:T(8,128)(2,1)S(1)}, u32[]{:S(2)}, u32[]{:S(2)}) collective-permute-start(bf16[128,1024]{1,0:T(8,128)(2,1)S(1)} %bitcast.45), channel_id=1, source_target_pairs={{0,32},{1,33},{2,34},{3,35},{4,36},{5,37},{6,38},{7,39},{8,40},{9,... | collective-permute-start | bytes 786440 | tf_op jit(solution)/shard_map/ppermute | solution.py:42
  (18 other events, 148.3 us)

commit v2 on v1

v2 whole, which is shorter than its diff:
```python
import functools

import jax
import jax.numpy as jnp
from jax import lax
from jax.experimental import pallas as pl
from jax.experimental.pallas import tpu as pltpu
from jax.sharding import PartitionSpec as P

D = 16384
HD = 128
NEW = 2
EPSILON = 1e-05
ROPE_BASE = 500000.0

NY = NZ = NX = 4
NC = 2
AXES = ("gx", "gy")
BF16 = jnp.bfloat16
F32 = jnp.float32
MIB = 1024 * 1024
TOGETHER = 4


def pairs(move):
    out = []
    for y in range(NY):
        for c in range(NC):
            for z in range(NZ):
                for x in range(NX):
                    y2, c2, z2, x2 = move(y, c, z, x)
                    source = ((y * NC + c) * NZ + z) * NX + x
                    target = (((y2 % NY) * NC + c2 % NC) * NZ + z2 % NZ) * NX + x2 % NX
                    out.append((source, target))
    return out


def swap_core(value):
    return lax.ppermute(value, AXES, pairs(lambda y, c, z, x: (y, c + 1, z, x)))


def shift_y(value, step):
    return lax.ppermute(value, AXES, pairs(lambda y, c, z, x: (y + step, c, z, x)))


def shift_first(value, step):
    def move(y, c, z, x):
        return (y, c, z, x + step) if c == 0 else (y, c, z + step, x)

    return lax.ppermute(value, AXES, pairs(move))


def shift_second(value, step):
    def move(y, c, z, x):
        return (y, c, z + step, x) if c == 0 else (y, c, z, x + step)

    return lax.ppermute(value, AXES, pairs(move))


VSPEC = pl.BlockSpec(memory_space=pltpu.VMEM)
SSPEC = pl.BlockSpec(memory_space=pltpu.SMEM)
HSPEC = pl.BlockSpec(memory_space=pltpu.HBM)


def call(body, outs, in_specs, name, vmem, scratch=(), flops=0, moved=0):
    return pl.pallas_call(
        body,
        out_shape=outs,
        in_specs=in_specs,
        out_specs=[VSPEC] * len(outs),
        scratch_shapes=list(scratch),
        compiler_params=pltpu.CompilerParams(vmem_limit_bytes=vmem * MIB),
        cost_estimate=pl.CostEstimate(flops=flops, bytes_accessed=moved, transcendentals=0),
        name=name,
    )


def shape(dims, dtype=BF16):
    return jax.ShapeDtypeStruct(dims, dtype)


def in_hbm(value):
    return pltpu.with_memory_space_constraint(value, pltpu.HBM)


def place():
    gx, gy = lax.axis_index("gx"), lax.axis_index("gy")
    return gx // NC, gx % NC, gy // NX, gy % NX


def split_high_low(total):
    high = total.astype(BF16).astype(F32)
    return jnp.concatenate([high, total - high], axis=0).astype(BF16)


def load_body(back_ref, hidden_hbm, gain_hbm, wq_hbm, wk_hbm, wv_hbm, *refs):
    outs, sems = refs[:-1], refs[-1]
    sources = (back_ref, hidden_hbm, gain_hbm, wq_hbm, wk_hbm, wv_hbm)
    copies = [
        pltpu.make_async_copy(source, out, sems.at[i])
        for i, (source, out) in enumerate(zip(sources, outs))
    ]
    for copy in copies:
        copy.start()
    for copy in copies:
        copy.wait()


def project_group(rows, heads, group, hs, sq, wq_ref, wk_ref, wv_ref, outs):
    first, count = group[0], len(group)
    depth = hs.shape[2]
    lhs = hs[4 * first : 4 * (first + count)].reshape(4 * count * rows, depth)
    for n in range(heads // 2 + 1):
        if n == heads // 2:
            rhs = jnp.concatenate([wk_ref[...], wv_ref[...]], axis=1)
        else:
            rhs = wq_ref[:, n * 256 : (n + 1) * 256]
        acc = jnp.dot(lhs, rhs, preferred_element_type=F32).astype(BF16)
        for i in range(count):
            for f in range(4):
                top = (4 * i + f) * rows
                for hh in range(2):
                    head = 2 * n + hh
                    outs[i][f, head * rows : (head + 1) * rows, :] = acc[
                        top : top + rows, hh * HD : (hh + 1) * HD
                    ]
    for i in range(count):
        for f in range(4):
            outs[i][f, (heads + 2) * rows :, :] = sq[4 * (first + i) + f]


ORDER = (2, 1, 3, 0)


def project_first_body(rows, heads, gain_ref, wq_ref, wk_ref, wv_ref, *refs):
    blocks, (out_ref, hs, sq) = refs[:8], refs[8:]
    y, c, z, x = place()
    gain = gain_ref[...].astype(F32).reshape(1, -1)
    depth = gain.shape[1]
    ones = jnp.ones((8, depth), BF16)
    pad = jnp.zeros((HD - rows, depth), BF16)
    for i, block in enumerate(blocks):
        for j in range(2):
            value = block[j * rows : (j + 1) * rows, :].astype(F32)
            dz = (y - i // 2 - z) % 4
            dx = (2 * (c ^ (i % 2)) + j - x) % 4
            e, f = jnp.where(c == 0, dx, dz), jnp.where(c == 0, dz, dx)
            at = jnp.where(e == 2, 0, jnp.where(e == 0, 3, (e + 1) // 2))
            slot = 4 * at + f
            hs[slot] = (value * gain).astype(BF16)
            square = value * value
            high = square.astype(BF16)
            low = (square - high.astype(F32)).astype(BF16)
            total = jnp.zeros((8, HD), F32)
            for part in (high, low):
                total += lax.dot_general(
                    ones,
                    jnp.concatenate([part, pad], axis=0),
                    (((1,), (1,)), ((), ())),
                    preferred_element_type=F32,
                )
            sq[slot] = split_high_low(total)
    project_group(rows, heads, (0,), hs, sq, wq_ref, wk_ref, wv_ref, [out_ref])


def project_middle_body(rows, heads, token_ref, hs, sq, wq_ref, wk_ref, wv_ref, *outs):
    project_group(rows, heads, (1, 2), hs, sq, wq_ref, wk_ref, wv_ref, outs)


def project_last_body(
    rows, heads, hs, sq, wq_ref, wk_ref, wv_ref, kc_hbm, vc_hbm, out_ref, kc_ref, vc_ref, sems
):
    copies = [
        pltpu.make_async_copy(kc_hbm, kc_ref, sems.at[0]),
        pltpu.make_async_copy(vc_hbm, vc_ref, sems.at[1]),
    ]
    for copy in copies:
        copy.start()
    project_group(rows, heads, (3,), hs, sq, wq_ref, wk_ref, wv_ref, [out_ref])
    for copy in copies:
        copy.wait()


def first_sum_body(main, own_ref, r1_ref, r2_ref, r3_ref, *outs):
    for f in range(4):
        total = (
            own_ref[f].astype(F32)
            + r1_ref[f].astype(F32)
            + r2_ref[f].astype(F32)
            + r3_ref[f].astype(F32)
        )
        if f == 0:
            outs[0][...] = total
        else:
            outs[f][0:main, :] = total[:main].astype(BF16)
            outs[f][main:, :] = split_high_low(total[main : main + 8] + total[main + 8 :])


def attend_body(
    rows, heads, len_ref, p0_ref, r1_ref, r2_ref, r3_ref, cos_ref, sin_ref, kbuf, vbuf,
    ctx_ref, nk_ref, nv_ref, qs, os, kf, vf,
):
    seqs = rows // NEW
    slots = kbuf.shape[1]
    main = (heads + 2) * rows

    def total(lo, hi):
        return (
            p0_ref[lo:hi, :]
            + r1_ref[lo:hi, :].astype(F32)
            + r2_ref[lo:hi, :].astype(F32)
            + r3_ref[lo:hi, :].astype(F32)
        )

    square = total(main, main + 16)
    column = jnp.transpose(square[:8] + square[8:])[:rows, 0:1]
    scales = lax.rsqrt(column / D + EPSILON)
    cosine, sine = cos_ref[...], sin_ref[...]

    def rope(value):
        return value * cosine + pltpu.roll(value, HD // 2, 1) * sine

    for head in range(heads):
        value = total(head * rows, (head + 1) * rows) * scales
        qs[pl.ds(head, rows, stride=heads), :] = rope(value).astype(BF16).astype(F32)
    key = rope(total(heads * rows, (heads + 1) * rows) * scales).astype(BF16)
    nk_ref[...] = key
    kf[...] = key.astype(F32)
    fresh = (total((heads + 1) * rows, (heads + 2) * rows) * scales).astype(BF16)
    nv_ref[...] = fresh
    vf[...] = fresh.astype(F32)

    per = NEW * heads
    scale = HD ** (-0.5)
    slot_of = lax.broadcasted_iota(jnp.int32, (per, slots), 1)
    second = lax.broadcasted_iota(jnp.int32, (per, 1), 0) >= heads

    def several(first, count):
        ids = [first + u for u in range(count)]
        query = [qs[pl.ds(pl.multiple_of(s * per, per), per), :] for s in ids]
        scores = [
            lax.dot_general(
                q.astype(BF16), kbuf[s], (((1,), (1,)), ((), ())), preferred_element_type=F32
            )
            for q, s in zip(query, ids)
        ]
        scores = [
            jnp.where(slot_of < len_ref[s], v * scale, -jnp.inf) for v, s in zip(scores, ids)
        ]
        s0 = [
            jnp.sum(q * kf[pl.ds(2 * s, 1), :], axis=1, keepdims=True) * scale
            for q, s in zip(query, ids)
        ]
        s1 = [
            jnp.sum(q * kf[pl.ds(2 * s + 1, 1), :], axis=1, keepdims=True) * scale
            for q, s in zip(query, ids)
        ]
        s1 = [jnp.where(second, v, -jnp.inf) for v in s1]
        highest = [
            jnp.maximum(jnp.max(v, axis=1, keepdims=True), jnp.maximum(a, b))
            for v, a, b in zip(scores, s0, s1)
        ]
        probs = [jnp.exp(v - m) for v, m in zip(scores, highest)]
        p0 = [jnp.exp(v - m) for v, m in zip(s0, highest)]
        p1 = [jnp.exp(v - m) for v, m in zip(s1, highest)]
        norm = [
            1.0 / (jnp.sum(v, axis=1, keepdims=True) + a + b) for v, a, b in zip(probs, p0, p1)
        ]
        out = [
            jnp.dot((v * n).astype(BF16), vbuf[s], preferred_element_type=F32)
            for v, n, s in zip(probs, norm, ids)
        ]
        for u, s in enumerate(ids):
            w0 = (p0[u] * norm[u]).astype(BF16).astype(F32)
            w1 = (p1[u] * norm[u]).astype(BF16).astype(F32)
            os[pl.ds(pl.multiple_of(s * per, per), per), :] = (
                out[u] + w0 * vf[pl.ds(2 * s, 1), :] + w1 * vf[pl.ds(2 * s + 1, 1), :]
            )

    def step(i, carry):
        several(TOGETHER * i, TOGETHER)
        return carry

    lax.fori_loop(0, seqs // TOGETHER, step, 0)
    for head in range(heads):
        ctx_ref[:, head * HD : (head + 1) * HD] = os[pl.ds(head, rows, stride=heads), :].astype(BF16)


def output_body(count, *refs):
    a_refs, (w_ref, out_ref) = refs[:count], refs[count:]
    lhs = jnp.concatenate([a[...] for a in a_refs], axis=0) if count > 1 else a_refs[0][...]
    for n in range(w_ref.shape[1] // 256):
        cols = slice(n * 256, (n + 1) * 256)
        out_ref[:, cols] = jnp.dot(lhs, w_ref[:, cols], preferred_element_type=F32).astype(BF16)


def arrange_body(rows, *refs):
    y_refs, (mine_ref, theirs_ref) = refs[:4], refs[4:]
    y, c, z, x = place()
    for f in range(4):
        for e in range(4):
            zz = jnp.where(c == 0, z - f, z - e) % 4
            xx = jnp.where(c == 0, x - e, x - f) % 4
            slot = 2 * ((zz - y) % 4) + xx % 2
            part = y_refs[f][e * rows : (e + 1) * rows, :]
            own = xx // 2 == c

            @pl.when(own)
            def _(slot=slot, part=part):
                mine_ref[slot] = part

            @pl.when(jnp.logical_not(own))
            def _(slot=slot, part=part):
                theirs_ref[slot] = part


def local(hidden, gain, w_query, w_key, w_value, w_out, key_cache, value_cache, lengths):
    heads = w_query.shape[1] // HD
    depth = hidden.shape[1]
    width = w_out.shape[1]
    rows = key_cache.shape[0] * NEW
    main = (heads + 2) * rows
    length = main + 16

    positions = (lengths[:, None] + jnp.arange(NEW, dtype=jnp.int32)[None, :]).reshape(-1)
    indices = jnp.arange(HD // 2, dtype=F32)
    inverse = jnp.power(F32(ROPE_BASE), -2.0 * indices / HD)
    angles = positions.astype(F32)[:, None] * inverse[None, :]
    cosine, sine = jnp.cos(angles), jnp.sin(angles)
    cosine = jnp.concatenate([cosine, cosine], 1)
    sine = jnp.concatenate([-sine, sine], 1)

    received = [shift_y(hidden, d) for d in (1, 2, 3)]
    sources = [hidden, gain, w_query, w_key, w_value]
    back, own, scale, *weights = call(
        load_body,
        [pltpu.VMEM(v.shape, v.dtype) for v in [received[0]] + sources],
        [VSPEC] + [HSPEC] * 5,
        "load",
        4,
        scratch=[pltpu.SemaphoreType.DMA((6,))],
    )(received[0], *[in_hbm(v) for v in sources])
    blocks = [own, swap_core(hidden)]
    for value in [back] + received[1:]:
        blocks += [value, swap_core(value)]

    group = shape((4, length, HD))
    sent = {}
    kept = {}
    kept[2], scaled, squares = call(
        functools.partial(project_first_body, rows, heads),
        [group, shape((16, rows, depth)), shape((16, 16, HD))],
        [VSPEC] * 12,
        "project_first",
        12,
    )(scale, *weights, *blocks)
    sent[2] = shift_first(kept[2], 2)
    token = swap_core(squares[0])
    kept[1], kept[3] = call(
        functools.partial(project_middle_body, rows, heads),
        [group, group],
        [VSPEC] * 6,
        "project_middle",
        12,
    )(token, scaled, squares, *weights)
    sent[1], sent[3] = shift_first(kept[1], 1), shift_first(kept[3], 3)
    kept[0], keys, values = call(
        functools.partial(project_last_body, rows, heads),
        [group] + [pltpu.VMEM(v.shape, v.dtype) for v in (key_cache, value_cache)],
        [VSPEC] * 5 + [HSPEC] * 2,
        "project_last",
        12,
        scratch=[pltpu.SemaphoreType.DMA((2,))],
    )(scaled, squares, *weights, in_hbm(key_cache), in_hbm(value_cache))
    sums = call(
        functools.partial(first_sum_body, main),
        [shape((length, HD), F32)] + [shape((length, HD))] * 3,
        [VSPEC] * 4,
        "first_sum",
        10,
    )(kept[0], sent[1], sent[2], sent[3])
    parts = [sums[0]] + [shift_second(sums[f], f) for f in (1, 2, 3)]

    context, fresh_keys, fresh_values = call(
        functools.partial(attend_body, rows, heads),
        [shape((rows, heads * HD)), shape((rows, HD)), shape((rows, HD))],
        [SSPEC] + [VSPEC] * 8,
        "attend",
        10,
        scratch=[
            pltpu.VMEM((rows * heads, HD), F32),
            pltpu.VMEM((rows * heads, HD), F32),
            pltpu.VMEM((rows, HD), F32),
            pltpu.VMEM((rows, HD), F32),
        ],
    )(lengths, *parts, cosine, sine, keys, values)

    near = [context] + [shift_first(context, e) for e in (1, 2, 3)]
    stacked = jnp.concatenate(near, axis=0)
    far = [shift_second(stacked, f) for f in (1, 2, 3)]
    partial = []
    for rows_in in [stacked] + far:
        partial += call(
            functools.partial(output_body, 1),
            [shape((4 * rows, width))],
            [VSPEC] * 2,
            "project_out",
            8,
        )(rows_in, w_out)
    mine, theirs = call(
        functools.partial(arrange_body, rows),
        [shape((8, rows, width)), shape((8, rows, width))],
        [VSPEC] * 4,
        "arrange",
        8,
    )(*partial)
    both = mine.astype(F32) + swap_core(theirs).astype(F32)
    both = both.reshape(4, 2 * rows, width)
    result = hidden.astype(F32) + both[0]
    for value in [shift_y(both[g].astype(BF16), g) for g in (1, 2, 3)]:
        result = result + value.astype(F32)
    return result.astype(BF16), fresh_keys, fresh_values


def solution(mesh):
    return jax.shard_map(
        local,
        mesh=mesh,
        in_specs=(
            P("gx", "gy"),
            P("gy"),
            P("gy", "gx"),
            P("gy", "gx"),
            P("gy", "gx"),
            P("gx", "gy"),
            P("gy", None, "gx"),
            P("gy", None, "gx"),
            P("gy"),
        ),
        out_specs=(P("gx", "gy"), P("gy", "gx"), P("gy", "gx")),
        check_vma=False,
    )
```

time: 195 us -> 141 us (0.72)
  Pallas kernels: 66.4 us -> 31.9 us
  waiting for transfers between devices: 81.7 us -> 67.7 us
  local copies, waits for them, and re-layouts: 9.27 us -> 2.47 us
  starting transfers between devices: 32 us -> 35.7 us
    pallas_call x6 -> x9, Pallas kernels: 42.1 us -> 21.5 us  [the longest x1 5.78 us: local(): call(functools.partial(project_last_body, rows, heads), [group] + [pltpu....]
    pallas_call x1, Pallas kernels: 20.7 us -> 7.84 us  [local(): call(functools.partial(attend_body, rows, heads), [shape((rows, heads * H...]
    ppermute x6, waiting for transfers between devices: 26.2 us -> 19.6 us  [shift_first(): return lax.ppermute(value, AXES, pairs(move))]
    ppermute x6, waiting for transfers between devices: 23.8 us -> 17.5 us  [shift_y(): lax.ppermute(value, AXES, pairs(lambda y, c, z, x: (y + step, c, z, x)))]
    unnamed x42 -> x13, local copies, waits for them, and re-layouts: 5.45 us -> 2.26 us
    ppermute x6, starting transfers between devices: 9.55 us -> 12.3 us  [shift_y(): lax.ppermute(value, AXES, pairs(lambda y, c, z, x: (y + step, c, z, x)))]
    ppermute x6, waiting for transfers between devices: 28.8 us -> 26.6 us  [shift_second(): return lax.ppermute(value, AXES, pairs(move))]
    ppermute x5 -> x6, waiting for transfers between devices: 2.88 us -> 4.04 us  [swap_core(): return lax.ppermute(value, AXES, pairs(lambda y, c, z, x: (y, c + 1, z, x)))]
  transfers between devices with their start and end apart: 23 -> 24, of which waited for: 15 -> 15; matrix products, arithmetic and copies ran while one was open for 3% -> 0% of each run, Pallas kernels for 3% -> 11%
where the time goes in v2:
time: 141 us; the launch traced here: 140 us
  waiting for transfers between devices  67.7 us (48%)
  starting transfers between devices  35.7 us (25%)
  Pallas kernels  31.9 us (23%)
  local copies, waits for them, and re-layouts  2.47 us (2%)
  other arithmetic  1.75 us (1%)
    ppermute x6, waiting for transfers between devices, shift_second(): return lax.ppermute(value, AXES, pairs(move))  26.6 us
    ppermute x6, waiting for transfers between devices, shift_first(): return lax.ppermute(value, AXES, pairs(move))  19.6 us
    ppermute x6, waiting for transfers between devices, shift_y(): lax.ppermute(value, AXES, pairs(lambda y, c, z, x: (y + step, c, z, x)))  17.5 us
    ppermute x6, starting transfers between devices, shift_y(): lax.ppermute(value, AXES, pairs(lambda y, c, z, x: (y + step, c, z, x)))  12.3 us
    ppermute x6, starting transfers between devices, shift_second(): return lax.ppermute(value, AXES, pairs(move))  11.8 us
    ppermute x6, starting transfers between devices, shift_first(): return lax.ppermute(value, AXES, pairs(move))  10.8 us
    pallas_call x1, Pallas kernels, local(): call(functools.partial(attend_body, rows, heads), [shape((rows, heads * H...  7.84 us
    pallas_call x1, Pallas kernels, local(): call(functools.partial(project_last_body, rows, heads), [group] + [pltpu....  5.78 us
  transfers between devices with their start and end apart: 24, of which 15 were waited for; matrix products, arithmetic and copies ran while one was open for 0% of the time, Pallas kernels for 11%

profile of v2, /device:TPU:0, one launch (start us, length us, event | category | flops | bytes accessed | tf_op | source)
XLA Modules:
  0.0 140.4 jit_solution(7029659366942356243)
XLA Ops:
  2.4 2.9 %collective-permute-start.3 = (bf16[128,1024]{1,0:T(8,128)(2,1)}, bf16[128,1024]{1,0:T(8,128)(2,1)S(1)}, u32[]{:S(2)}, u32[]{:S(2)}) collective-permute-start(bf16[128,1024]{1,0:T(8,128)(2,1)} %hidden_hbm.1), channel_id=1, source_target_pairs={{0,64},{1,65},{2,66},{3,67},{4,68},{5,69},{6,70},{7,71},{8,72},{9,... | collective-permute-start | bytes 786440 | tf_op jit(solution)/shard_map/ppermute | solution.py:43
  6.6 3.7 %collective-permute-done.back_ref = bf16[128,1024]{1,0:T(8,128)(2,1)S(1)} collective-permute-done((bf16[128,1024]{1,0:T(8,128)(2,1)}, bf16[128,1024]{1,0:T(8,128)(2,1)S(1)}, u32[]{:S(2)}, u32[]{:S(2)}) %collective-permute-start) | collective-permute-done | bytes 262176 | tf_op jit(solution)/shard_map/ppermute | solution.py:43
  10.3 2.5 %load.1 = (bf16[128,1024]{1,0:T(8,128)(2,1)S(1)}, bf16[128,1024]{1,0:T(8,128)(2,1)S(1)}, bf16[1024]{0:T(1024)(128)(2,1)S(1)}, bf16[1024,2048]{1,0:T(8,128)(2,1)S...) custom-call(bf16[128,1024]{1,0:T(8,128)(2,1)S(1)} %collective-permute-done.back_ref, ...), custom_call_target="tpu_custom_call" | custom-call | tf_op jit(solution)/shard_map/load/pallas_call | solution.py:335
  12.9 4.2 %collective-permute-done.3.refs_4_ = bf16[128,1024]{1,0:T(8,128)(2,1)S(1)} collective-permute-done((bf16[128,1024]{1,0:T(8,128)(2,1)}, bf16[128,1024]{1,0:T(8,128)(2,1)S(1)}, u32[]{:S(2)}, u32[]{:S(2)}) %collective-permute-start.3) | collective-permute-done | bytes 262176 | tf_op jit(solution)/shard_map/ppermute | solution.py:43
  19.0 3.7 %project_first.1 = (bf16[4,1168,128]{2,1,0:T(8,128)(2,1)}, bf16[16,64,1024]{2,1,0:T(8,128)(2,1)S(1)}, bf16[16,16,128]{2,1,0:T(8,128)(2,1)S(1)}) custom-call(bf16[1024]{0:T(1024)(128)(2,1)S(1)} %get-tuple-element.26.gain_ref, bf16[1024,2048]{1,0:T(8,128)(2,1)S(1)} %get-tuple-element.27.wq_ref, bf16[1024,128]{1,0:T(8,128)(2,1)S(1)} %get-tuple-element.28.wk_ref, ...), custom_call_target="tpu_custom_call" | custom-call | tf_op jit(solution)/shard_map/project_first/pallas_call | solution.py:350
  22.9 3.0 %collective-permute-start.9 = (bf16[4,1168,128]{2,1,0:T(8,128)(2,1)}, bf16[4,1168,128]{2,1,0:T(8,128)(2,1)}, u32[]{:S(2)}, u32[]{:S(2)}) collective-permute-start(bf16[4,1168,128]{2,1,0:T(8,128)(2,1)} %get-tuple-element.36), channel_id=1, source_target_pairs={{0,2},{1,3},{2,0},{3,1},{4,6},{5,7},{6,4},{7,5},{8,10},{9,11},{10,... | collective-permute-start | bytes 3588104 | tf_op jit(solution)/shard_map/ppermute | solution.py:50
  25.9 4.0 %project_middle.1 = (bf16[4,1168,128]{2,1,0:T(8,128)(2,1)}, bf16[4,1168,128]{2,1,0:T(8,128)(2,1)}) custom-call(bf16[16,128]{1,0:T(8,128)(2,1)S(1)} %collective-permute-done.7.token_ref, bf16[16,64,1024]{2,1,0:T(8,128)(2,1)S(1)} %get-tuple-element.32.hs, bf16[16,16,128]{2,1,0:T(8,128)(2,1)S(1)} %get-tuple-element.33.sq, ...), custom_call_target="tpu_custom_call" | custom-call | tf_op jit(solution)/shard_map/project_middle/pallas_call | solution.py:359
  32.1 2.2 %copy-done.2 = bf16[1024,2048]{1,0:T(8,128)(2,1)S(1)} copy-done((bf16[1024,2048]{1,0:T(8,128)(2,1)S(1)}, bf16[1024,2048]{1,0:T(8,128)(2,1)}, u32[]{:S(2)}) %copy-start.2) | copy-done | bytes 4194328
  34.3 5.8 %project_last.1 = (bf16[4,1168,128]{2,1,0:T(8,128)(2,1)S(1)}, bf16[32,1024,128]{2,1,0:T(8,128)(2,1)S(1)}, bf16[32,1024,128]{2,1,0:T(8,128)(2,1)S(1)}) custom-call(bf16[16,64,1024]{2,1,0:T(8,128)(2,1)S(1)} %get-tuple-element.32.hs, bf16[16,16,128]{2,1,0:T(8,128)(2,1)S(1)} %get-tuple-element.33.sq, bf16[1024,2048]{1,0:T(8,128)(2,1)S(1)} %copy-done.2, ...), custom_call_target="tpu_custom_call" | custom-call | tf_op jit(solution)/shard_map/project_last/pallas_call | solution.py:367
  41.2 12.8 %collective-permute-done.10.r3_ref = bf16[4,1168,128]{2,1,0:T(8,128)(2,1)} collective-permute-done((bf16[4,1168,128]{2,1,0:T(8,128)(2,1)}, bf16[4,1168,128]{2,1,0:T(8,128)(2,1)}, u32[]{:S(2)}, u32[]{:S(2)}) %collective-permute-start.10) | collective-permute-done | bytes 1196064 | tf_op jit(solution)/shard_map/ppermute | solution.py:50
  54.0 2.6 %first_sum.1 = (f32[1168,128]{1,0:T(8,128)S(1)}, bf16[1168,128]{1,0:T(8,128)(2,1)S(1)}, bf16[1168,128]{1,0:T(8,128)(2,1)S(1)}, bf16[1168,128]{1,0:T(8,128)(2,1)S(1)}) custom-call(bf16[4,1168,128]{2,1,0:T(8,128)(2,1)S(1)} %get-tuple-element.34.own_ref, bf16[4,1168,128]{2,1,0:T(8,128)(2,1)} %collective-permute-done.8.r1_ref, ...), custom_call_target="tpu_custom_call" | custom-call | tf_op jit(solution)/shard_map/first_sum/pallas_call | solution.py:375
  58.6 3.6 %collective-permute-start.12 = (bf16[1168,128]{1,0:T(8,128)(2,1)S(1)}, bf16[1168,128]{1,0:T(8,128)(2,1)S(1)}, u32[]{:S(2)}, u32[]{:S(2)}) collective-permute-start(bf16[1168,128]{1,0:T(8,128)(2,1)S(1)} %get-tuple-element.40), channel_id=1, source_target_pairs={{0,8},{1,9},{2,10},{3,11},{4,12},{5,13},{6,14},{7,15},{8,0},{9,1},... | collective-permute-start | bytes 897032 | tf_op jit(solution)/shard_map/ppermute | solution.py:57
  65.4 4.7 %collective-permute-done.12.r2_ref = bf16[1168,128]{1,0:T(8,128)(2,1)S(1)} collective-permute-done((bf16[1168,128]{1,0:T(8,128)(2,1)S(1)}, bf16[1168,128]{1,0:T(8,128)(2,1)S(1)}, u32[]{:S(2)}, u32[]{:S(2)}) %collective-permute-start.12) | collective-permute-done | bytes 299040 | tf_op jit(solution)/shard_map/ppermute | solution.py:57
  70.1 7.8 %attend.1 = (bf16[64,2048]{1,0:T(8,128)(2,1)S(1)}, bf16[64,128]{1,0:T(8,128)(2,1)}, bf16[64,128]{1,0:T(8,128)(2,1)}) custom-call(s32[32]{0:T(128)S(1)} %copy-done.3, f32[1168,128]{1,0:T(8,128)S(1)} %get-tuple-element.38.p0_ref, bf16[1168,128]{1,0:T(8,128)(2,1)S(1)} %collective-permute-done.11.r1_ref, bf16[1168,128]{1,0:T(8,128)(2,1)S(1)} %collective-permute-done.12.r2_ref, ...), custom_call_target="tpu_custom_call" | custom-call | tf_op jit(solution)/shard_map/attend/pallas_call | solution.py:384
  79.5 2.7 %collective-permute-start.15 = (bf16[64,2048]{1,0:T(8,128)(2,1)S(1)}, bf16[64,2048]{1,0:T(8,128)(2,1)S(1)}, u32[]{:S(2)}, u32[]{:S(2)}) collective-permute-start(bf16[64,2048]{1,0:T(8,128)(2,1)S(1)} %get-tuple-element.44), channel_id=1, source_target_pairs={{0,2},{1,3},{2,0},{3,1},{4,6},{5,7},{6,4},{7,5},{8,10},{9,11},{10,... | collective-permute-start | bytes 786440 | tf_op jit(solution)/shard_map/ppermute | solution.py:50
  85.7 3.6 %collective-permute-done.15 = bf16[64,2048]{1,0:T(8,128)(2,1)S(1)} collective-permute-done((bf16[64,2048]{1,0:T(8,128)(2,1)S(1)}, bf16[64,2048]{1,0:T(8,128)(2,1)S(1)}, u32[]{:S(2)}, u32[]{:S(2)}) %collective-permute-start.15) | collective-permute-done | bytes 262176 | tf_op jit(solution)/shard_map/ppermute | solution.py:50
  91.0 2.1 %collective-permute-start.18 = (bf16[256,2048]{1,0:T(8,128)(2,1)S(1)}, bf16[256,2048]{1,0:T(8,128)(2,1)S(1)}, u32[]{:S(2)}, u32[]{:S(2)}) collective-permute-start(bf16[256,2048]{1,0:T(8,128)(2,1)S(1)} %constant_dynamic-update-slice_fusion.refs_0_), channel_id=1, source_target_pairs={{0,8},{1,9},{2,10},{3,11},{4,12},{5,13},{6,14},{7,15},{8,0},{9,1},... | collective-permute-start | bytes 3145736 | tf_op jit(solution)/shard_map/ppermute | solution.py:57
  95.9 9.6 %collective-permute-done.17.refs_0_ = bf16[256,2048]{1,0:T(8,128)(2,1)S(1)} collective-permute-done((bf16[256,2048]{1,0:T(8,128)(2,1)S(1)}, bf16[256,2048]{1,0:T(8,128)(2,1)S(1)}, u32[]{:S(2)}, u32[]{:S(2)}) %collective-permute-start.17) | collective-permute-done | bytes 1048608 | tf_op jit(solution)/shard_map/ppermute | solution.py:57
  106.8 10.3 %collective-permute-done.18.refs_0_ = bf16[256,2048]{1,0:T(8,128)(2,1)S(1)} collective-permute-done((bf16[256,2048]{1,0:T(8,128)(2,1)S(1)}, bf16[256,2048]{1,0:T(8,128)(2,1)S(1)}, u32[]{:S(2)}, u32[]{:S(2)}) %collective-permute-start.18) | collective-permute-done | bytes 1048608 | tf_op jit(solution)/shard_map/ppermute | solution.py:57
  120.3 2.6 %collective-permute-done.20 = bf16[8,64,1024]{2,1,0:T(8,128)(2,1)S(1)} collective-permute-done((bf16[8,64,1024]{2,1,0:T(8,128)(2,1)S(1)}, bf16[8,64,1024]{2,1,0:T(8,128)(2,1)S(1)}, u32[]{:S(2)}, u32[]{:S(2)}) %collective-permute-start.20) | collective-permute-done | bytes 1048608 | tf_op jit(solution)/shard_map/ppermute | solution.py:39
  124.4 2.9 %collective-permute-start.22 = (bf16[128,1024]{1,0:T(8,128)(2,1)S(1)}, bf16[128,1024]{1,0:T(8,128)(2,1)S(1)}, u32[]{:S(2)}, u32[]{:S(2)}) collective-permute-start(bf16[128,1024]{1,0:T(8,128)(2,1)S(1)} %bitcast.16), channel_id=1, source_target_pairs={{0,64},{1,65},{2,66},{3,67},{4,68},{5,69},{6,70},{7,71},{8,72},{9,... | collective-permute-start | bytes 786440 | tf_op jit(solution)/shard_map/ppermute | solution.py:43
  127.3 2.5 %collective-permute-start.23 = (bf16[128,1024]{1,0:T(8,128)(2,1)S(1)}, bf16[128,1024]{1,0:T(8,128)(2,1)S(1)}, u32[]{:S(2)}, u32[]{:S(2)}) collective-permute-start(bf16[128,1024]{1,0:T(8,128)(2,1)S(1)} %bitcast.15), channel_id=1, source_target_pairs={{0,96},{1,97},{2,98},{3,99},{4,100},{5,101},{6,102},{7,103},{8,104... | collective-permute-start | bytes 786440 | tf_op jit(solution)/shard_map/ppermute | solution.py:43
  129.9 3.2 %collective-permute-done.21 = bf16[128,1024]{1,0:T(8,128)(2,1)S(1)} collective-permute-done((bf16[128,1024]{1,0:T(8,128)(2,1)S(1)}, bf16[128,1024]{1,0:T(8,128)(2,1)S(1)}, u32[]{:S(2)}, u32[]{:S(2)}) %collective-permute-start.21) | collective-permute-done | bytes 262176 | tf_op jit(solution)/shard_map/ppermute | solution.py:43
  133.1 6.3 %collective-permute-done.22 = bf16[128,1024]{1,0:T(8,128)(2,1)S(1)} collective-permute-done((bf16[128,1024]{1,0:T(8,128)(2,1)S(1)}, bf16[128,1024]{1,0:T(8,128)(2,1)S(1)}, u32[]{:S(2)}, u32[]{:S(2)}) %collective-permute-start.22) | collective-permute-done | bytes 262176 | tf_op jit(solution)/shard_map/ppermute | solution.py:43
  (59 shorter events, 30.1 us)
Async XLA Ops:
  0.6 9.7 %collective-permute-start = (bf16[128,1024]{1,0:T(8,128)(2,1)}, bf16[128,1024]{1,0:T(8,128)(2,1)S(1)}, u32[]{:S(2)}, u32[]{:S(2)}) collective-permute-start(bf16[128,1024]{1,0:T(8,128)(2,1)} %hidden_hbm.1), channel_id=1, source_target_pairs={{0,32},{1,33},{2,34},{3,35},{4,36},{5,37},{6,38},{7,39},{8,40},{9,... | collective-permute-start | bytes 786440 | tf_op jit(solution)/shard_map/ppermute | solution.py:43
  2.4 14.7 %collective-permute-start.3 = (bf16[128,1024]{1,0:T(8,128)(2,1)}, bf16[128,1024]{1,0:T(8,128)(2,1)S(1)}, u32[]{:S(2)}, u32[]{:S(2)}) collective-permute-start(bf16[128,1024]{1,0:T(8,128)(2,1)} %hidden_hbm.1), channel_id=1, source_target_pairs={{0,64},{1,65},{2,66},{3,67},{4,68},{5,69},{6,70},{7,71},{8,72},{9,... | collective-permute-start | bytes 786440 | tf_op jit(solution)/shard_map/ppermute | solution.py:43
  5.3 11.9 %collective-permute-start.5 = (bf16[128,1024]{1,0:T(8,128)(2,1)}, bf16[128,1024]{1,0:T(8,128)(2,1)S(1)}, u32[]{:S(2)}, u32[]{:S(2)}) collective-permute-start(bf16[128,1024]{1,0:T(8,128)(2,1)} %hidden_hbm.1), channel_id=1, source_target_pairs={{0,96},{1,97},{2,98},{3,99},{4,100},{5,101},{6,102},{7,103},{8,104... | collective-permute-start | bytes 786440 | tf_op jit(solution)/shard_map/ppermute | solution.py:43
  6.6 11.0 %collective-permute-start.1 = (bf16[128,1024]{1,0:T(8,128)(2,1)}, bf16[128,1024]{1,0:T(8,128)(2,1)S(1)}, u32[]{:S(2)}, u32[]{:S(2)}) collective-permute-start(bf16[128,1024]{1,0:T(8,128)(2,1)} %hidden_hbm.1), channel_id=1, source_target_pairs={{0,16},{1,17},{2,18},{3,19},{4,20},{5,21},{6,22},{7,23},{8,24},{9,... | collective-permute-start | bytes 786440 | tf_op jit(solution)/shard_map/ppermute | solution.py:39
  12.8 4.8 %collective-permute-start.2 = (bf16[128,1024]{1,0:T(8,128)(2,1)S(1)}, bf16[128,1024]{1,0:T(8,128)(2,1)S(1)}, u32[]{:S(2)}, u32[]{:S(2)}) collective-permute-start(bf16[128,1024]{1,0:T(8,128)(2,1)S(1)} %get-tuple-element.31.refs_2_), channel_id=1, source_target_pairs={{0,16},{1,17},{2,18},{3,19},{4,20},{5,21},{6,22},{7,23},{8,24},{9,... | collective-permute-start | bytes 786440 | tf_op jit(solution)/shard_map/ppermute | solution.py:39
  17.1 1.5 %collective-permute-start.4 = (bf16[128,1024]{1,0:T(8,128)(2,1)S(1)}, bf16[128,1024]{1,0:T(8,128)(2,1)S(1)}, u32[]{:S(2)}, u32[]{:S(2)}) collective-permute-start(bf16[128,1024]{1,0:T(8,128)(2,1)S(1)} %collective-permute-done.3.refs_4_), channel_id=1, source_target_pairs={{0,16},{1,17},{2,18},{3,19},{4,20},{5,21},{6,22},{7,23},{8,24},{9,... | collective-permute-start | bytes 786440 | tf_op jit(solution)/shard_map/ppermute | solution.py:39
  17.1 1.9 %collective-permute-start.6 = (bf16[128,1024]{1,0:T(8,128)(2,1)S(1)}, bf16[128,1024]{1,0:T(8,128)(2,1)S(1)}, u32[]{:S(2)}, u32[]{:S(2)}) collective-permute-start(bf16[128,1024]{1,0:T(8,128)(2,1)S(1)} %collective-permute-done.5.refs_6_), channel_id=1, source_target_pairs={{0,16},{1,17},{2,18},{3,19},{4,20},{5,21},{6,22},{7,23},{8,24},{9,... | collective-permute-start | bytes 786440 | tf_op jit(solution)/shard_map/ppermute | solution.py:39
  22.7 3.2 %collective-permute-start.7 = (bf16[16,128]{1,0:T(8,128)(2,1)S(1)}, bf16[16,128]{1,0:T(8,128)(2,1)S(1)}, u32[]{:S(2)}, u32[]{:S(2)}) collective-permute-start(bf16[16,128]{1,0:T(8,128)(2,1)S(1)} %slice_bitcast_fusion), channel_id=1, source_target_pairs={{0,16},{1,17},{2,18},{3,19},{4,20},{5,21},{6,22},{7,23},{8,24},{9,... | collective-permute-start | bytes 12296 | tf_op jit(solution)/shard_map/ppermute | solution.py:39
  22.9 18.3 %collective-permute-start.9 = (bf16[4,1168,128]{2,1,0:T(8,128)(2,1)}, bf16[4,1168,128]{2,1,0:T(8,128)(2,1)}, u32[]{:S(2)}, u32[]{:S(2)}) collective-permute-start(bf16[4,1168,128]{2,1,0:T(8,128)(2,1)} %get-tuple-element.36), channel_id=1, source_target_pairs={{0,2},{1,3},{2,0},{3,1},{4,6},{5,7},{6,4},{7,5},{8,10},{9,11},{10,... | collective-permute-start | bytes 3588104 | tf_op jit(solution)/shard_map/ppermute | solution.py:50
  29.9 24.1 %collective-permute-start.10 = (bf16[4,1168,128]{2,1,0:T(8,128)(2,1)}, bf16[4,1168,128]{2,1,0:T(8,128)(2,1)}, u32[]{:S(2)}, u32[]{:S(2)}) collective-permute-start(bf16[4,1168,128]{2,1,0:T(8,128)(2,1)} %get-tuple-element.37), channel_id=1, source_target_pairs={{0,3},{1,0},{2,1},{3,2},{4,7},{5,4},{6,5},{7,6},{8,11},{9,8},{10,9... | collective-permute-start | bytes 3588104 | tf_op jit(solution)/shard_map/ppermute | solution.py:50
  31.0 23.0 %collective-permute-start.8 = (bf16[4,1168,128]{2,1,0:T(8,128)(2,1)}, bf16[4,1168,128]{2,1,0:T(8,128)(2,1)}, u32[]{:S(2)}, u32[]{:S(2)}) collective-permute-start(bf16[4,1168,128]{2,1,0:T(8,128)(2,1)} %get-tuple-element.35), channel_id=1, source_target_pairs={{0,1},{1,2},{2,3},{3,0},{4,5},{5,6},{6,7},{7,4},{8,9},{9,10},{10,1... | collective-permute-start | bytes 3588104 | tf_op jit(solution)/shard_map/ppermute | solution.py:50
  56.6 8.9 %collective-permute-start.11 = (bf16[1168,128]{1,0:T(8,128)(2,1)S(1)}, bf16[1168,128]{1,0:T(8,128)(2,1)S(1)}, u32[]{:S(2)}, u32[]{:S(2)}) collective-permute-start(bf16[1168,128]{1,0:T(8,128)(2,1)S(1)} %get-tuple-element.39), channel_id=1, source_target_pairs={{0,4},{1,5},{2,6},{3,7},{4,8},{5,9},{6,10},{7,11},{8,12},{9,13},{1... | collective-permute-start | bytes 897032 | tf_op jit(solution)/shard_map/ppermute | solution.py:57
  58.6 11.5 %collective-permute-start.12 = (bf16[1168,128]{1,0:T(8,128)(2,1)S(1)}, bf16[1168,128]{1,0:T(8,128)(2,1)S(1)}, u32[]{:S(2)}, u32[]{:S(2)}) collective-permute-start(bf16[1168,128]{1,0:T(8,128)(2,1)S(1)} %get-tuple-element.40), channel_id=1, source_target_pairs={{0,8},{1,9},{2,10},{3,11},{4,12},{5,13},{6,14},{7,15},{8,0},{9,1},... | collective-permute-start | bytes 897032 | tf_op jit(solution)/shard_map/ppermute | solution.py:57
  62.2 7.9 %collective-permute-start.13 = (bf16[1168,128]{1,0:T(8,128)(2,1)S(1)}, bf16[1168,128]{1,0:T(8,128)(2,1)S(1)}, u32[]{:S(2)}, u32[]{:S(2)}) collective-permute-start(bf16[1168,128]{1,0:T(8,128)(2,1)S(1)} %get-tuple-element.41), channel_id=1, source_target_pairs={{0,12},{1,13},{2,14},{3,15},{4,0},{5,1},{6,2},{7,3},{8,4},{9,5},{1... | collective-permute-start | bytes 897032 | tf_op jit(solution)/shard_map/ppermute | solution.py:57
  77.9 7.7 %collective-permute-start.14 = (bf16[64,2048]{1,0:T(8,128)(2,1)S(1)}, bf16[64,2048]{1,0:T(8,128)(2,1)S(1)}, u32[]{:S(2)}, u32[]{:S(2)}) collective-permute-start(bf16[64,2048]{1,0:T(8,128)(2,1)S(1)} %get-tuple-element.44), channel_id=1, source_target_pairs={{0,1},{1,2},{2,3},{3,0},{4,5},{5,6},{6,7},{7,4},{8,9},{9,10},{10,1... | collective-permute-start | bytes 786440 | tf_op jit(solution)/shard_map/ppermute | solution.py:50
  79.5 9.8 %collective-permute-start.15 = (bf16[64,2048]{1,0:T(8,128)(2,1)S(1)}, bf16[64,2048]{1,0:T(8,128)(2,1)S(1)}, u32[]{:S(2)}, u32[]{:S(2)}) collective-permute-start(bf16[64,2048]{1,0:T(8,128)(2,1)S(1)} %get-tuple-element.44), channel_id=1, source_target_pairs={{0,2},{1,3},{2,0},{3,1},{4,6},{5,7},{6,4},{7,5},{8,10},{9,11},{10,... | collective-permute-start | bytes 786440 | tf_op jit(solution)/shard_map/ppermute | solution.py:50
  82.2 7.2 %collective-permute-start.16 = (bf16[64,2048]{1,0:T(8,128)(2,1)S(1)}, bf16[64,2048]{1,0:T(8,128)(2,1)S(1)}, u32[]{:S(2)}, u32[]{:S(2)}) collective-permute-start(bf16[64,2048]{1,0:T(8,128)(2,1)S(1)} %get-tuple-element.44), channel_id=1, source_target_pairs={{0,3},{1,0},{2,1},{3,2},{4,7},{5,4},{6,5},{7,6},{8,11},{9,8},{10,9... | collective-permute-start | bytes 786440 | tf_op jit(solution)/shard_map/ppermute | solution.py:50
  89.4 16.1 %collective-permute-start.17 = (bf16[256,2048]{1,0:T(8,128)(2,1)S(1)}, bf16[256,2048]{1,0:T(8,128)(2,1)S(1)}, u32[]{:S(2)}, u32[]{:S(2)}) collective-permute-start(bf16[256,2048]{1,0:T(8,128)(2,1)S(1)} %constant_dynamic-update-slice_fusion.refs_0_), channel_id=1, source_target_pairs={{0,4},{1,5},{2,6},{3,7},{4,8},{5,9},{6,10},{7,11},{8,12},{9,13},{1... | collective-permute-start | bytes 3145736 | tf_op jit(solution)/shard_map/ppermute | solution.py:57
  91.0 26.1 %collective-permute-start.18 = (bf16[256,2048]{1,0:T(8,128)(2,1)S(1)}, bf16[256,2048]{1,0:T(8,128)(2,1)S(1)}, u32[]{:S(2)}, u32[]{:S(2)}) collective-permute-start(bf16[256,2048]{1,0:T(8,128)(2,1)S(1)} %constant_dynamic-update-slice_fusion.refs_0_), channel_id=1, source_target_pairs={{0,8},{1,9},{2,10},{3,11},{4,12},{5,13},{6,14},{7,15},{8,0},{9,1},... | collective-permute-start | bytes 3145736 | tf_op jit(solution)/shard_map/ppermute | solution.py:57
  93.1 25.3 %collective-permute-start.19 = (bf16[256,2048]{1,0:T(8,128)(2,1)S(1)}, bf16[256,2048]{1,0:T(8,128)(2,1)S(1)}, u32[]{:S(2)}, u32[]{:S(2)}) collective-permute-start(bf16[256,2048]{1,0:T(8,128)(2,1)S(1)} %constant_dynamic-update-slice_fusion.refs_0_), channel_id=1, source_target_pairs={{0,12},{1,13},{2,14},{3,15},{4,0},{5,1},{6,2},{7,3},{8,4},{9,5},{1... | collective-permute-start | bytes 3145736 | tf_op jit(solution)/shard_map/ppermute | solution.py:57
  120.2 2.7 %collective-permute-start.20 = (bf16[8,64,1024]{2,1,0:T(8,128)(2,1)S(1)}, bf16[8,64,1024]{2,1,0:T(8,128)(2,1)S(1)}, u32[]{:S(2)}, u32[]{:S(2)}) collective-permute-start(bf16[8,64,1024]{2,1,0:T(8,128)(2,1)S(1)} %get-tuple-element.46), channel_id=1, source_target_pairs={{0,16},{1,17},{2,18},{3,19},{4,20},{5,21},{6,22},{7,23},{8,24},{9,... | collective-permute-start | bytes 3145736 | tf_op jit(solution)/shard_map/ppermute | solution.py:39
  123.5 9.6 %collective-permute-start.21 = (bf16[128,1024]{1,0:T(8,128)(2,1)S(1)}, bf16[128,1024]{1,0:T(8,128)(2,1)S(1)}, u32[]{:S(2)}, u32[]{:S(2)}) collective-permute-start(bf16[128,1024]{1,0:T(8,128)(2,1)S(1)} %bitcast.17), channel_id=1, source_target_pairs={{0,32},{1,33},{2,34},{3,35},{4,36},{5,37},{6,38},{7,39},{8,40},{9,... | collective-permute-start | bytes 786440 | tf_op jit(solution)/shard_map/ppermute | solution.py:43
  124.4 15.0 %collective-permute-start.22 = (bf16[128,1024]{1,0:T(8,128)(2,1)S(1)}, bf16[128,1024]{1,0:T(8,128)(2,1)S(1)}, u32[]{:S(2)}, u32[]{:S(2)}) collective-permute-start(bf16[128,1024]{1,0:T(8,128)(2,1)S(1)} %bitcast.16), channel_id=1, source_target_pairs={{0,64},{1,65},{2,66},{3,67},{4,68},{5,69},{6,70},{7,71},{8,72},{9,... | collective-permute-start | bytes 786440 | tf_op jit(solution)/shard_map/ppermute | solution.py:43
  127.3 12.1 %collective-permute-start.23 = (bf16[128,1024]{1,0:T(8,128)(2,1)S(1)}, bf16[128,1024]{1,0:T(8,128)(2,1)S(1)}, u32[]{:S(2)}, u32[]{:S(2)}) collective-permute-start(bf16[128,1024]{1,0:T(8,128)(2,1)S(1)} %bitcast.15), channel_id=1, source_target_pairs={{0,96},{1,97},{2,98},{3,99},{4,100},{5,101},{6,102},{7,103},{8,104... | collective-permute-start | bytes 786440 | tf_op jit(solution)/shard_map/ppermute | solution.py:43
  (5 other events, 61.9 us)

commit v3 on v2

--- a/solution.py
+++ b/solution.py
@@ -110,30 +110,25 @@
     first, count = group[0], len(group)
     depth = hs.shape[2]
     lhs = hs[4 * first : 4 * (first + count)].reshape(4 * count * rows, depth)
+    per = outs[0].shape[0]
     for n in range(heads // 2 + 1):
         if n == heads // 2:
             rhs = jnp.concatenate([wk_ref[...], wv_ref[...]], axis=1)
         else:
             rhs = wq_ref[:, n * 256 : (n + 1) * 256]
         acc = jnp.dot(lhs, rhs, preferred_element_type=F32).astype(BF16)
-        for i in range(count):
-            for f in range(4):
-                top = (4 * i + f) * rows
-                for hh in range(2):
-                    head = 2 * n + hh
-                    outs[i][f, head * rows : (head + 1) * rows, :] = acc[
-                        top : top + rows, hh * HD : (hh + 1) * HD
-                    ]
-    for i in range(count):
-        for f in range(4):
-            outs[i][f, (heads + 2) * rows :, :] = sq[4 * (first + i) + f]
-
-
-ORDER = (2, 1, 3, 0)
+        for i in range(4 * count):
+            for hh in range(2):
+                head = 2 * n + hh
+                outs[i // per][i % per, head * rows : (head + 1) * rows, :] = acc[
+                    i * rows : (i + 1) * rows, hh * HD : (hh + 1) * HD
+                ]
+    for i in range(4 * count):
+        outs[i // per][i % per, (heads + 2) * rows :, :] = sq[4 * first + i]
 
 
 def project_first_body(rows, heads, gain_ref, wq_ref, wk_ref, wv_ref, *refs):
-    blocks, (out_ref, hs, sq) = refs[:8], refs[8:]
+    blocks, outs, (hs, sq) = refs[:8], refs[8:10], refs[10:]
     y, c, z, x = place()
     gain = gain_ref[...].astype(F32).reshape(1, -1)
     depth = gain.shape[1]
@@ -160,7 +155,7 @@
                     preferred_element_type=F32,
                 )
             sq[slot] = split_high_low(total)
-    project_group(rows, heads, (0,), hs, sq, wq_ref, wk_ref, wv_ref, [out_ref])
+    project_group(rows, heads, (0,), hs, sq, wq_ref, wk_ref, wv_ref, outs)
 
 
 def project_middle_body(rows, heads, token_ref, hs, sq, wq_ref, wk_ref, wv_ref, *outs):
@@ -181,23 +176,18 @@
         copy.wait()
 
 
-def first_sum_body(main, own_ref, r1_ref, r2_ref, r3_ref, *outs):
-    for f in range(4):
-        total = (
-            own_ref[f].astype(F32)
-            + r1_ref[f].astype(F32)
-            + r2_ref[f].astype(F32)
-            + r3_ref[f].astype(F32)
-        )
-        if f == 0:
-            outs[0][...] = total
-        else:
-            outs[f][0:main, :] = total[:main].astype(BF16)
-            outs[f][main:, :] = split_high_low(total[main : main + 8] + total[main + 8 :])
+def add_body(main, terms, *refs):
+    ins, outs = refs[: len(refs) - len(terms)], refs[len(refs) - len(terms) :]
+    for out, picks in zip(outs, terms):
+        for i, pick in enumerate(picks):
+            total = sum(ins[ref][block].astype(F32) for ref, block in pick)
+            out[i, 0:main, :] = total[:main].astype(BF16)
+            out[i, main:, :] = split_high_low(total[main : main + 8] + total[main + 8 :])
 
 
 def attend_body(
-    rows, heads, len_ref, p0_ref, r1_ref, r2_ref, r3_ref, cos_ref, sin_ref, kbuf, vbuf,
+    rows, heads, len_ref, p0_ref, p1_ref, p2_ref, r1_ref, r2_ref, r3_ref,
+    cos_ref, sin_ref, kbuf, vbuf,
     ctx_ref, nk_ref, nv_ref, qs, os, kf, vf,
 ):
     seqs = rows // NEW
@@ -205,12 +195,8 @@
     main = (heads + 2) * rows
 
     def total(lo, hi):
-        return (
-            p0_ref[lo:hi, :]
-            + r1_ref[lo:hi, :].astype(F32)
-            + r2_ref[lo:hi, :].astype(F32)
-            + r3_ref[lo:hi, :].astype(F32)
-        )
+        refs = (p0_ref, p1_ref, p2_ref, r1_ref, r2_ref, r3_ref)
+        return sum(ref[0, lo:hi, :].astype(F32) for ref in refs)
 
     square = total(main, main + 16)
     column = jnp.transpose(square[:8] + square[8:])[:rows, 0:1]
@@ -286,32 +272,31 @@
         ctx_ref[:, head * HD : (head + 1) * HD] = os[pl.ds(head, rows, stride=heads), :].astype(BF16)
 
 
-def output_body(count, *refs):
-    a_refs, (w_ref, out_ref) = refs[:count], refs[count:]
-    lhs = jnp.concatenate([a[...] for a in a_refs], axis=0) if count > 1 else a_refs[0][...]
+def output_body(a_ref, b_ref, w_ref, out_ref):
+    lhs = jnp.concatenate([a_ref[...], b_ref[...]], axis=0)
     for n in range(w_ref.shape[1] // 256):
         cols = slice(n * 256, (n + 1) * 256)
         out_ref[:, cols] = jnp.dot(lhs, w_ref[:, cols], preferred_element_type=F32).astype(BF16)
 
 
-def arrange_body(rows, *refs):
-    y_refs, (mine_ref, theirs_ref) = refs[:4], refs[4:]
+def output_last_body(rows, a_ref, b_ref, w_ref, y0_ref, y1_ref, y3_ref, mine_ref, theirs_ref, y2):
     y, c, z, x = place()
-    for f in range(4):
+    output_body(a_ref, b_ref, w_ref, y2)
+    for f, source in enumerate((y0_ref, y1_ref, y2, y3_ref)):
         for e in range(4):
             zz = jnp.where(c == 0, z - f, z - e) % 4
             xx = jnp.where(c == 0, x - e, x - f) % 4
             slot = 2 * ((zz - y) % 4) + xx % 2
-            part = y_refs[f][e * rows : (e + 1) * rows, :]
+            top = e * rows
             own = xx // 2 == c
 
             @pl.when(own)
-            def _(slot=slot, part=part):
-                mine_ref[slot] = part
+            def _(slot=slot, source=source, top=top):
+                mine_ref[slot] = source[top : top + rows, :]
 
             @pl.when(jnp.logical_not(own))
-            def _(slot=slot, part=part):
-                theirs_ref[slot] = part
+            def _(slot=slot, source=source, top=top):
+                theirs_ref[slot] = source[top : top + rows, :]
 
 
 def local(hidden, gain, w_query, w_key, w_value, w_out, key_cache, value_cache, lengths):
@@ -344,47 +329,60 @@
     for value in [back] + received[1:]:
         blocks += [value, swap_core(value)]
 
-    group = shape((4, length, HD))
-    sent = {}
-    kept = {}
-    kept[2], scaled, squares = call(
+    half = shape((2, length, HD))
+    two_a, two_b, scaled, squares = call(
         functools.partial(project_first_body, rows, heads),
-        [group, shape((16, rows, depth)), shape((16, 16, HD))],
+        [half, half, shape((16, rows, depth)), shape((16, 16, HD))],
         [VSPEC] * 12,
         "project_first",
         12,
     )(scale, *weights, *blocks)
-    sent[2] = shift_first(kept[2], 2)
+    over_a, over_b = shift_first(two_a, 1), shift_first(two_b, 3)
     token = swap_core(squares[0])
-    kept[1], kept[3] = call(
+    one_a, one_b, three_a, three_b = call(
         functools.partial(project_middle_body, rows, heads),
-        [group, group],
+        [half] * 4,
         [VSPEC] * 6,
         "project_middle",
         12,
     )(token, scaled, squares, *weights)
-    sent[1], sent[3] = shift_first(kept[1], 1), shift_first(kept[3], 3)
-    kept[0], keys, values = call(
+    from_one_b, from_three_a = shift_first(one_b, 1), shift_first(three_a, 3)
+
+    def add(terms, *values):
+        return call(
+            functools.partial(add_body, main, terms),
+            [shape((len(picks), length, HD)) for picks in terms],
+            [VSPEC] * len(values),
+            "add",
+            8,
+        )(*values)
+
+    pairwise = [[[(0, 0), (1, 0)], [(0, 1), (1, 1)]]]
+    from_one_a = shift_first(add(pairwise, one_a, over_a)[0], 1)
+    from_three_b = shift_first(add(pairwise, three_b, over_b)[0], 3)
+    own_group, keys, values = call(
         functools.partial(project_last_body, rows, heads),
-        [group] + [pltpu.VMEM(v.shape, v.dtype) for v in (key_cache, value_cache)],
+        [shape((4, length, HD))] + [pltpu.VMEM(v.shape, v.dtype) for v in (key_cache, value_cache)],
         [VSPEC] * 5 + [HSPEC] * 2,
         "project_last",
         12,
         scratch=[pltpu.SemaphoreType.DMA((2,))],
     )(scaled, squares, *weights, in_hbm(key_cache), in_hbm(value_cache))
-    sums = call(
-        functools.partial(first_sum_body, main),
-        [shape((length, HD), F32)] + [shape((length, HD))] * 3,
-        [VSPEC] * 4,
-        "first_sum",
-        10,
-    )(kept[0], sent[1], sent[2], sent[3])
-    parts = [sums[0]] + [shift_second(sums[f], f) for f in (1, 2, 3)]
+    terms = [
+        [[(0, 2), (3, 0), (4, 0)]],
+        [[(0, 1), (1, 1), (2, 1)]],
+        [[(0, 3), (3, 1), (4, 1)]],
+    ]
+    two, one, three = add(
+        terms, own_group, from_one_a, from_three_a, from_one_b, from_three_b
+    )
+    arrived = [shift_second(two, 2), shift_second(one, 1), shift_second(three, 3)]
+    parts = [own_group, from_one_a, from_three_a] + arrived
 
     context, fresh_keys, fresh_values = call(
         functools.partial(attend_body, rows, heads),
         [shape((rows, heads * HD)), shape((rows, HD)), shape((rows, HD))],
-        [SSPEC] + [VSPEC] * 8,
+        [SSPEC] + [VSPEC] * 10,
         "attend",
         10,
         scratch=[
@@ -395,25 +393,36 @@
         ],
     )(lengths, *parts, cosine, sine, keys, values)
 
-    near = [context] + [shift_first(context, e) for e in (1, 2, 3)]
-    stacked = jnp.concatenate(near, axis=0)
-    far = [shift_second(stacked, f) for f in (1, 2, 3)]
-    partial = []
-    for rows_in in [stacked] + far:
-        partial += call(
-            functools.partial(output_body, 1),
+    one, three, two = shift_first(context, 1), shift_first(context, 3), shift_first(context, 2)
+    low, high = jnp.concatenate([context, one], 0), jnp.concatenate([two, three], 0)
+    one_low, three_high = shift_second(low, 1), shift_second(high, 3)
+    two_low, two_high = shift_second(one_low, 1), shift_second(three_high, 3)
+    one_high, three_low = shift_second(high, 1), shift_second(low, 3)
+
+    def project_out(a, b):
+        return call(
+            output_body,
             [shape((4 * rows, width))],
-            [VSPEC] * 2,
+            [VSPEC] * 3,
             "project_out",
             8,
-        )(rows_in, w_out)
+        )(a, b, w_out)[0]
+
     mine, theirs = call(
-        functools.partial(arrange_body, rows),
+        functools.partial(output_last_body, rows),
         [shape((8, rows, width)), shape((8, rows, width))],
-        [VSPEC] * 4,
-        "arrange",
-        8,
-    )(*partial)
+        [VSPEC] * 6,
+        "project_out_last",
+        12,
+        scratch=[pltpu.VMEM((4 * rows, width), BF16)],
+    )(
+        two_low,
+        two_high,
+        w_out,
+        project_out(low, high),
+        project_out(one_low, one_high),
+        project_out(three_low, three_high),
+    )
     both = mine.astype(F32) + swap_core(theirs).astype(F32)
     both = both.reshape(4, 2 * rows, width)
     result = hidden.astype(F32) + both[0]

time: 141 us -> 131 us (0.929)
  waiting for transfers between devices: 67.7 us -> 46.4 us
  starting transfers between devices: 35.7 us -> 43.3 us
  local copies, waits for them, and re-layouts: 2.47 us -> 5.51 us
    ppermute x6 -> x9, waiting for transfers between devices: 19.6 us -> 7.79 us  [shift_first(): return lax.ppermute(value, AXES, pairs(move))]
    ppermute x6 -> x9, waiting for transfers between devices: 26.6 us -> 16.3 us  [shift_second(): return lax.ppermute(value, AXES, pairs(move))]
    ppermute x6 -> x9, starting transfers between devices: 11.8 us -> 16.8 us  [shift_second(): return lax.ppermute(value, AXES, pairs(move))]
    unnamed x13 -> x24, local copies, waits for them, and re-layouts: 2.26 us -> 4.05 us
    ppermute x6 -> x9, starting transfers between devices: 10.8 us -> 12.3 us  [shift_first(): return lax.ppermute(value, AXES, pairs(move))]
    pallas_call x9 -> x10, Pallas kernels: 21.6 us -> 21.1 us  [the longest x1 5.81 us: local(): call(functools.partial(project_last_body, rows, heads), [shape((4, length...]
  transfers between devices with their start and end apart: 24 -> 30, of which waited for: 15 -> 20; matrix products, arithmetic and copies ran while one was open for 0% -> 2% of each run, Pallas kernels for 11% -> 14%
where the time goes in v3:
time: 131 us; the launch traced here: 130 us
  waiting for transfers between devices  46.4 us (35%)
  starting transfers between devices  43.3 us (33%)
  Pallas kernels  31.5 us (24%)
  local copies, waits for them, and re-layouts  5.51 us (4%)
  other arithmetic  2.36 us (2%)
    ppermute x6, waiting for transfers between devices, shift_y(): lax.ppermute(value, AXES, pairs(lambda y, c, z, x: (y + step, c, z, x)))  17.5 us
    ppermute x9, starting transfers between devices, shift_second(): return lax.ppermute(value, AXES, pairs(move))  16.8 us
    ppermute x9, waiting for transfers between devices, shift_second(): return lax.ppermute(value, AXES, pairs(move))  16.3 us
    ppermute x6, starting transfers between devices, shift_y(): lax.ppermute(value, AXES, pairs(lambda y, c, z, x: (y + step, c, z, x)))  12.4 us
    ppermute x9, starting transfers between devices, shift_first(): return lax.ppermute(value, AXES, pairs(move))  12.3 us
    pallas_call x1, Pallas kernels, local(): call(functools.partial(attend_body, rows, heads), [shape((rows, heads * H...  7.93 us
    ppermute x9, waiting for transfers between devices, shift_first(): return lax.ppermute(value, AXES, pairs(move))  7.79 us
    pallas_call x1, Pallas kernels, local(): call(functools.partial(project_last_body, rows, heads), [shape((4, length...  5.81 us
  transfers between devices with their start and end apart: 30, of which 20 were waited for; matrix products, arithmetic and copies ran while one was open for 2% of the time, Pallas kernels for 14%

profile of v3, /device:TPU:0, one launch (start us, length us, event | category | flops | bytes accessed | tf_op | source)
XLA Modules:
  0.0 130.0 jit_solution(17373592987341313093)
XLA Ops:
  2.4 2.9 %collective-permute-start.3 = (bf16[128,1024]{1,0:T(8,128)(2,1)}, bf16[128,1024]{1,0:T(8,128)(2,1)S(1)}, u32[]{:S(2)}, u32[]{:S(2)}) collective-permute-start(bf16[128,1024]{1,0:T(8,128)(2,1)} %hidden_hbm.1), channel_id=1, source_target_pairs={{0,64},{1,65},{2,66},{3,67},{4,68},{5,69},{6,70},{7,71},{8,72},{9,... | collective-permute-start | bytes 786440 | tf_op jit(solution)/shard_map/ppermute | solution.py:43
  6.6 3.7 %collective-permute-done.back_ref = bf16[128,1024]{1,0:T(8,128)(2,1)S(1)} collective-permute-done((bf16[128,1024]{1,0:T(8,128)(2,1)}, bf16[128,1024]{1,0:T(8,128)(2,1)S(1)}, u32[]{:S(2)}, u32[]{:S(2)}) %collective-permute-start) | collective-permute-done | bytes 262176 | tf_op jit(solution)/shard_map/ppermute | solution.py:43
  12.9 4.2 %collective-permute-done.3.refs_4_ = bf16[128,1024]{1,0:T(8,128)(2,1)S(1)} collective-permute-done((bf16[128,1024]{1,0:T(8,128)(2,1)}, bf16[128,1024]{1,0:T(8,128)(2,1)S(1)}, u32[]{:S(2)}, u32[]{:S(2)}) %collective-permute-start.3) | collective-permute-done | bytes 262176 | tf_op jit(solution)/shard_map/ppermute | solution.py:43
  19.0 2.6 %project_first.1 = (bf16[2,1168,128]{2,1,0:T(8,128)(2,1)S(1)}, bf16[2,1168,128]{2,1,0:T(8,128)(2,1)S(1)}, bf16[16,64,1024]{2,1,0:T(8,128)(2,1)S(1)}, bf16[16,16,128]{2,1,0:T(8,128)(2,1)S(1)}) custom-call(bf16[1024]{0:T(1024)(128)(2,1)S(1)} %get-tuple-element.28.gain_ref, bf16[1024,2048]{1,0:T(8,128)(2,1)S(1)} %get-tuple-element.29.wq_ref, ...), custom_call_target="tpu_custom_call" | custom-call | tf_op jit(solution)/shard_map/project_first/pallas_call | solution.py:333
  21.7 2.8 %collective-permute-start.12 = (bf16[2,1168,128]{2,1,0:T(8,128)(2,1)S(1)}, bf16[2,1168,128]{2,1,0:T(8,128)(2,1)S(1)}, u32[]{:S(2)}, u32[]{:S(2)}) collective-permute-start(bf16[2,1168,128]{2,1,0:T(8,128)(2,1)S(1)} %get-tuple-element.42), channel_id=1, source_target_pairs={{0,3},{1,0},{2,1},{3,2},{4,7},{5,4},{6,5},{7,6},{8,11},{9,8},{10,9... | collective-permute-start | bytes 1794056 | tf_op jit(solution)/shard_map/ppermute | solution.py:50
  26.5 3.6 %project_middle.1 = (bf16[2,1168,128]{2,1,0:T(8,128)(2,1)S(1)}, bf16[2,1168,128]{2,1,0:T(8,128)(2,1)}, bf16[2,1168,128]{2,1,0:T(8,128)(2,1)}, bf16[2,1168,128]{2,1,0:T(8,128)(2,1)S(1)}) custom-call(bf16[16,128]{1,0:T(8,128)(2,1)S(1)} %collective-permute-done.7.token_ref, bf16[16,64,1024]{2,1,0:T(8,128)(2,1)S(1)} %get-tuple-element.34.hs, ...), custom_call_target="tpu_custom_call" | custom-call | tf_op jit(solution)/shard_map/project_middle/pallas_call | solution.py:342
  30.1 2.8 %collective-permute-start.10 = (bf16[2,1168,128]{2,1,0:T(8,128)(2,1)}, bf16[2,1168,128]{2,1,0:T(8,128)(2,1)S(1)}, u32[]{:S(2)}, u32[]{:S(2)}) collective-permute-start(bf16[2,1168,128]{2,1,0:T(8,128)(2,1)} %get-tuple-element.39), channel_id=1, source_target_pairs={{0,3},{1,0},{2,1},{3,2},{4,7},{5,4},{6,5},{7,6},{8,11},{9,8},{10,9... | collective-permute-start | bytes 1794056 | tf_op jit(solution)/shard_map/ppermute | solution.py:50
  33.8 3.2 %collective-permute-start.13 = (bf16[2,1168,128]{2,1,0:T(8,128)(2,1)}, bf16[2,1168,128]{2,1,0:T(8,128)(2,1)}, u32[]{:S(2)}, u32[]{:S(2)}) collective-permute-start(bf16[2,1168,128]{2,1,0:T(8,128)(2,1)} %add.76), channel_id=1, source_target_pairs={{0,3},{1,0},{2,1},{3,2},{4,7},{5,4},{6,5},{7,6},{8,11},{9,8},{10,9... | collective-permute-start | bytes 1794056 | tf_op jit(solution)/shard_map/ppermute | solution.py:50
  44.1 5.8 %project_last.1 = (bf16[4,1168,128]{2,1,0:T(8,128)(2,1)S(1)}, bf16[32,1024,128]{2,1,0:T(8,128)(2,1)S(1)}, bf16[32,1024,128]{2,1,0:T(8,128)(2,1)S(1)}) custom-call(bf16[16,64,1024]{2,1,0:T(8,128)(2,1)S(1)} %get-tuple-element.34.hs, bf16[16,16,128]{2,1,0:T(8,128)(2,1)S(1)} %copy-done.6, bf16[1024,2048]{1,0:T(8,128)(2,1)S(1)} %copy-done.2, ...), custom_call_target="tpu_custom_call" | custom-call | tf_op jit(solution)/shard_map/project_last/pallas_call | solution.py:363
  52.2 3.6 %collective-permute-start.14 = (bf16[1,1168,128]{2,1,0:T(8,128)(2,1)S(1)}, bf16[1,1168,128]{2,1,0:T(8,128)(2,1)S(1)}, u32[]{:S(2)}, u32[]{:S(2)}) collective-permute-start(bf16[1,1168,128]{2,1,0:T(8,128)(2,1)S(1)} %get-tuple-element.43), channel_id=1, source_target_pairs={{0,8},{1,9},{2,10},{3,11},{4,12},{5,13},{6,14},{7,15},{8,0},{9,1},... | collective-permute-start | bytes 897032 | tf_op jit(solution)/shard_map/ppermute | solution.py:57
  60.6 3.2 %collective-permute-done.15.r2_ref = bf16[1,1168,128]{2,1,0:T(8,128)(2,1)S(1)} collective-permute-done((bf16[1,1168,128]{2,1,0:T(8,128)(2,1)S(1)}, bf16[1,1168,128]{2,1,0:T(8,128)(2,1)S(1)}, u32[]{:S(2)}, u32[]{:S(2)}) %collective-permute-start.15) | collective-permute-done | bytes 299040 | tf_op jit(solution)/shard_map/ppermute | solution.py:57
  64.8 7.9 %attend.1 = (bf16[64,2048]{1,0:T(8,128)(2,1)S(1)}, bf16[64,128]{1,0:T(8,128)(2,1)}, bf16[64,128]{1,0:T(8,128)(2,1)}) custom-call(s32[32]{0:T(128)S(1)} %copy-done.8, bf16[4,1168,128]{2,1,0:T(8,128)(2,1)S(1)} %get-tuple-element.36.refs_0_.p0_ref, bf16[2,1168,128]{2,1,0:T(8,128)(2,1)S(1)} %collective-permute-done.9.refs_1_.p1_ref, ...), custom_call_target="tpu_custom_call" | custom-call | tf_op jit(solution)/shard_map/attend/pallas_call | solution.py:382
  76.3 4.4 %collective-permute-done.20 = bf16[64,2048]{1,0:T(8,128)(2,1)S(1)} collective-permute-done((bf16[64,2048]{1,0:T(8,128)(2,1)S(1)}, bf16[64,2048]{1,0:T(8,128)(2,1)S(1)}, u32[]{:S(2)}, u32[]{:S(2)}) %collective-permute-start.20) | collective-permute-done | bytes 262176 | tf_op jit(solution)/shard_map/ppermute | solution.py:50
  80.7 2.7 %collective-permute-done.21 = bf16[64,2048]{1,0:T(8,128)(2,1)S(1)} collective-permute-done((bf16[64,2048]{1,0:T(8,128)(2,1)S(1)}, bf16[64,2048]{1,0:T(8,128)(2,1)S(1)}, u32[]{:S(2)}, u32[]{:S(2)}) %collective-permute-start.21) | collective-permute-done | bytes 262176 | tf_op jit(solution)/shard_map/ppermute | solution.py:50
  83.4 2.9 %collective-permute-start.22 = (bf16[128,2048]{1,0:T(8,128)(2,1)S(1)}, bf16[128,2048]{1,0:T(8,128)(2,1)S(1)}, u32[]{:S(2)}, u32[]{:S(2)}) collective-permute-start(bf16[128,2048]{1,0:T(8,128)(2,1)S(1)} %constant_dynamic-update-slice_fusion.2.b_ref), channel_id=1, source_target_pairs={{0,12},{1,13},{2,14},{3,15},{4,0},{5,1},{6,2},{7,3},{8,4},{9,5},{1... | collective-permute-start | bytes 1572872 | tf_op jit(solution)/shard_map/ppermute | solution.py:57
  86.4 3.2 %collective-permute-start.25 = (bf16[128,2048]{1,0:T(8,128)(2,1)S(1)}, bf16[128,2048]{1,0:T(8,128)(2,1)S(1)}, u32[]{:S(2)}, u32[]{:S(2)}) collective-permute-start(bf16[128,2048]{1,0:T(8,128)(2,1)S(1)} %constant_dynamic-update-slice_fusion.a_ref), channel_id=1, source_target_pairs={{0,12},{1,13},{2,14},{3,15},{4,0},{5,1},{6,2},{7,3},{8,4},{9,5},{1... | collective-permute-start | bytes 1572872 | tf_op jit(solution)/shard_map/ppermute | solution.py:57
  89.6 3.4 %collective-permute-done.22.b_ref = bf16[128,2048]{1,0:T(8,128)(2,1)S(1)} collective-permute-done((bf16[128,2048]{1,0:T(8,128)(2,1)S(1)}, bf16[128,2048]{1,0:T(8,128)(2,1)S(1)}, u32[]{:S(2)}, u32[]{:S(2)}) %collective-permute-start.22) | collective-permute-done | bytes 524320 | tf_op jit(solution)/shard_map/ppermute | solution.py:57
  93.0 3.7 %collective-permute-start.23 = (bf16[128,2048]{1,0:T(8,128)(2,1)S(1)}, bf16[128,2048]{1,0:T(8,128)(2,1)S(1)}, u32[]{:S(2)}, u32[]{:S(2)}) collective-permute-start(bf16[128,2048]{1,0:T(8,128)(2,1)S(1)} %collective-permute-done.22.b_ref), channel_id=1, source_target_pairs={{0,12},{1,13},{2,14},{3,15},{4,0},{5,1},{6,2},{7,3},{8,4},{9,5},{1... | collective-permute-start | bytes 1572872 | tf_op jit(solution)/shard_map/ppermute | solution.py:57
  104.2 3.8 %collective-permute-done.19.a_ref = bf16[128,2048]{1,0:T(8,128)(2,1)S(1)} collective-permute-done((bf16[128,2048]{1,0:T(8,128)(2,1)S(1)}, bf16[128,2048]{1,0:T(8,128)(2,1)S(1)}, u32[]{:S(2)}, u32[]{:S(2)}) %collective-permute-start.19) | collective-permute-done | bytes 524320 | tf_op jit(solution)/shard_map/ppermute | solution.py:57
  109.9 2.6 %collective-permute-done.26 = bf16[8,64,1024]{2,1,0:T(8,128)(2,1)S(1)} collective-permute-done((bf16[8,64,1024]{2,1,0:T(8,128)(2,1)S(1)}, bf16[8,64,1024]{2,1,0:T(8,128)(2,1)S(1)}, u32[]{:S(2)}, u32[]{:S(2)}) %collective-permute-start.26) | collective-permute-done | bytes 1048608 | tf_op jit(solution)/shard_map/ppermute | solution.py:39
  114.0 2.9 %collective-permute-start.28 = (bf16[128,1024]{1,0:T(8,128)(2,1)S(1)}, bf16[128,1024]{1,0:T(8,128)(2,1)S(1)}, u32[]{:S(2)}, u32[]{:S(2)}) collective-permute-start(bf16[128,1024]{1,0:T(8,128)(2,1)S(1)} %bitcast.16), channel_id=1, source_target_pairs={{0,64},{1,65},{2,66},{3,67},{4,68},{5,69},{6,70},{7,71},{8,72},{9,... | collective-permute-start | bytes 786440 | tf_op jit(solution)/shard_map/ppermute | solution.py:43
  116.9 2.5 %collective-permute-start.29 = (bf16[128,1024]{1,0:T(8,128)(2,1)S(1)}, bf16[128,1024]{1,0:T(8,128)(2,1)S(1)}, u32[]{:S(2)}, u32[]{:S(2)}) collective-permute-start(bf16[128,1024]{1,0:T(8,128)(2,1)S(1)} %bitcast.15), channel_id=1, source_target_pairs={{0,96},{1,97},{2,98},{3,99},{4,100},{5,101},{6,102},{7,103},{8,104... | collective-permute-start | bytes 786440 | tf_op jit(solution)/shard_map/ppermute | solution.py:43
  119.5 3.2 %collective-permute-done.27 = bf16[128,1024]{1,0:T(8,128)(2,1)S(1)} collective-permute-done((bf16[128,1024]{1,0:T(8,128)(2,1)S(1)}, bf16[128,1024]{1,0:T(8,128)(2,1)S(1)}, u32[]{:S(2)}, u32[]{:S(2)}) %collective-permute-start.27) | collective-permute-done | bytes 262176 | tf_op jit(solution)/shard_map/ppermute | solution.py:43
  122.7 6.4 %collective-permute-done.28 = bf16[128,1024]{1,0:T(8,128)(2,1)S(1)} collective-permute-done((bf16[128,1024]{1,0:T(8,128)(2,1)S(1)}, bf16[128,1024]{1,0:T(8,128)(2,1)S(1)}, u32[]{:S(2)}, u32[]{:S(2)}) %collective-permute-start.28) | collective-permute-done | bytes 262176 | tf_op jit(solution)/shard_map/ppermute | solution.py:43
  (84 shorter events, 40.9 us)
Async XLA Ops:
  0.6 9.7 %collective-permute-start = (bf16[128,1024]{1,0:T(8,128)(2,1)}, bf16[128,1024]{1,0:T(8,128)(2,1)S(1)}, u32[]{:S(2)}, u32[]{:S(2)}) collective-permute-start(bf16[128,1024]{1,0:T(8,128)(2,1)} %hidden_hbm.1), channel_id=1, source_target_pairs={{0,32},{1,33},{2,34},{3,35},{4,36},{5,37},{6,38},{7,39},{8,40},{9,... | collective-permute-start | bytes 786440 | tf_op jit(solution)/shard_map/ppermute | solution.py:43
  2.4 14.7 %collective-permute-start.3 = (bf16[128,1024]{1,0:T(8,128)(2,1)}, bf16[128,1024]{1,0:T(8,128)(2,1)S(1)}, u32[]{:S(2)}, u32[]{:S(2)}) collective-permute-start(bf16[128,1024]{1,0:T(8,128)(2,1)} %hidden_hbm.1), channel_id=1, source_target_pairs={{0,64},{1,65},{2,66},{3,67},{4,68},{5,69},{6,70},{7,71},{8,72},{9,... | collective-permute-start | bytes 786440 | tf_op jit(solution)/shard_map/ppermute | solution.py:43
  5.3 11.9 %collective-permute-start.5 = (bf16[128,1024]{1,0:T(8,128)(2,1)}, bf16[128,1024]{1,0:T(8,128)(2,1)S(1)}, u32[]{:S(2)}, u32[]{:S(2)}) collective-permute-start(bf16[128,1024]{1,0:T(8,128)(2,1)} %hidden_hbm.1), channel_id=1, source_target_pairs={{0,96},{1,97},{2,98},{3,99},{4,100},{5,101},{6,102},{7,103},{8,104... | collective-permute-start | bytes 786440 | tf_op jit(solution)/shard_map/ppermute | solution.py:43
  6.6 11.0 %collective-permute-start.1 = (bf16[128,1024]{1,0:T(8,128)(2,1)}, bf16[128,1024]{1,0:T(8,128)(2,1)S(1)}, u32[]{:S(2)}, u32[]{:S(2)}) collective-permute-start(bf16[128,1024]{1,0:T(8,128)(2,1)} %hidden_hbm.1), channel_id=1, source_target_pairs={{0,16},{1,17},{2,18},{3,19},{4,20},{5,21},{6,22},{7,23},{8,24},{9,... | collective-permute-start | bytes 786440 | tf_op jit(solution)/shard_map/ppermute | solution.py:39
  21.7 11.2 %collective-permute-start.12 = (bf16[2,1168,128]{2,1,0:T(8,128)(2,1)S(1)}, bf16[2,1168,128]{2,1,0:T(8,128)(2,1)S(1)}, u32[]{:S(2)}, u32[]{:S(2)}) collective-permute-start(bf16[2,1168,128]{2,1,0:T(8,128)(2,1)S(1)} %get-tuple-element.42), channel_id=1, source_target_pairs={{0,3},{1,0},{2,1},{3,2},{4,7},{5,4},{6,5},{7,6},{8,11},{9,8},{10,9... | collective-permute-start | bytes 1794056 | tf_op jit(solution)/shard_map/ppermute | solution.py:50
  24.5 12.6 %collective-permute-start.8 = (bf16[2,1168,128]{2,1,0:T(8,128)(2,1)S(1)}, bf16[2,1168,128]{2,1,0:T(8,128)(2,1)S(1)}, u32[]{:S(2)}, u32[]{:S(2)}) collective-permute-start(bf16[2,1168,128]{2,1,0:T(8,128)(2,1)S(1)} %get-tuple-element.38), channel_id=1, source_target_pairs={{0,1},{1,2},{2,3},{3,0},{4,5},{5,6},{6,7},{7,4},{8,9},{9,10},{10,1... | collective-permute-start | bytes 1794056 | tf_op jit(solution)/shard_map/ppermute | solution.py:50
  30.1 19.8 %collective-permute-start.10 = (bf16[2,1168,128]{2,1,0:T(8,128)(2,1)}, bf16[2,1168,128]{2,1,0:T(8,128)(2,1)S(1)}, u32[]{:S(2)}, u32[]{:S(2)}) collective-permute-start(bf16[2,1168,128]{2,1,0:T(8,128)(2,1)} %get-tuple-element.39), channel_id=1, source_target_pairs={{0,3},{1,0},{2,1},{3,2},{4,7},{5,4},{6,5},{7,6},{8,11},{9,8},{10,9... | collective-permute-start | bytes 1794056 | tf_op jit(solution)/shard_map/ppermute | solution.py:50
  32.8 17.1 %collective-permute-start.11 = (bf16[2,1168,128]{2,1,0:T(8,128)(2,1)}, bf16[2,1168,128]{2,1,0:T(8,128)(2,1)}, u32[]{:S(2)}, u32[]{:S(2)}) collective-permute-start(bf16[2,1168,128]{2,1,0:T(8,128)(2,1)} %get-tuple-element.40), channel_id=1, source_target_pairs={{0,1},{1,2},{2,3},{3,0},{4,5},{5,6},{6,7},{7,4},{8,9},{9,10},{10,1... | collective-permute-start | bytes 1794056 | tf_op jit(solution)/shard_map/ppermute | solution.py:50
  33.8 16.1 %collective-permute-start.13 = (bf16[2,1168,128]{2,1,0:T(8,128)(2,1)}, bf16[2,1168,128]{2,1,0:T(8,128)(2,1)}, u32[]{:S(2)}, u32[]{:S(2)}) collective-permute-start(bf16[2,1168,128]{2,1,0:T(8,128)(2,1)} %add.76), channel_id=1, source_target_pairs={{0,3},{1,0},{2,1},{3,2},{4,7},{5,4},{6,5},{7,6},{8,11},{9,8},{10,9... | collective-permute-start | bytes 1794056 | tf_op jit(solution)/shard_map/ppermute | solution.py:50
  38.1 12.6 %collective-permute-start.9 = (bf16[2,1168,128]{2,1,0:T(8,128)(2,1)}, bf16[2,1168,128]{2,1,0:T(8,128)(2,1)S(1)}, u32[]{:S(2)}, u32[]{:S(2)}) collective-permute-start(bf16[2,1168,128]{2,1,0:T(8,128)(2,1)} %add.75), channel_id=1, source_target_pairs={{0,1},{1,2},{2,3},{3,0},{4,5},{5,6},{6,7},{7,4},{8,9},{9,10},{10,1... | collective-permute-start | bytes 1794056 | tf_op jit(solution)/shard_map/ppermute | solution.py:50
  52.2 8.4 %collective-permute-start.14 = (bf16[1,1168,128]{2,1,0:T(8,128)(2,1)S(1)}, bf16[1,1168,128]{2,1,0:T(8,128)(2,1)S(1)}, u32[]{:S(2)}, u32[]{:S(2)}) collective-permute-start(bf16[1,1168,128]{2,1,0:T(8,128)(2,1)S(1)} %get-tuple-element.43), channel_id=1, source_target_pairs={{0,8},{1,9},{2,10},{3,11},{4,12},{5,13},{6,14},{7,15},{8,0},{9,1},... | collective-permute-start | bytes 897032 | tf_op jit(solution)/shard_map/ppermute | solution.py:57
  55.9 8.0 %collective-permute-start.15 = (bf16[1,1168,128]{2,1,0:T(8,128)(2,1)S(1)}, bf16[1,1168,128]{2,1,0:T(8,128)(2,1)S(1)}, u32[]{:S(2)}, u32[]{:S(2)}) collective-permute-start(bf16[1,1168,128]{2,1,0:T(8,128)(2,1)S(1)} %get-tuple-element.44), channel_id=1, source_target_pairs={{0,4},{1,5},{2,6},{3,7},{4,8},{5,9},{6,10},{7,11},{8,12},{9,13},{1... | collective-permute-start | bytes 897032 | tf_op jit(solution)/shard_map/ppermute | solution.py:57
  56.9 7.9 %collective-permute-start.16 = (bf16[1,1168,128]{2,1,0:T(8,128)(2,1)S(1)}, bf16[1,1168,128]{2,1,0:T(8,128)(2,1)S(1)}, u32[]{:S(2)}, u32[]{:S(2)}) collective-permute-start(bf16[1,1168,128]{2,1,0:T(8,128)(2,1)S(1)} %get-tuple-element.45), channel_id=1, source_target_pairs={{0,12},{1,13},{2,14},{3,15},{4,0},{5,1},{6,2},{7,3},{8,4},{9,5},{1... | collective-permute-start | bytes 897032 | tf_op jit(solution)/shard_map/ppermute | solution.py:57
  73.5 9.8 %collective-permute-start.21 = (bf16[64,2048]{1,0:T(8,128)(2,1)S(1)}, bf16[64,2048]{1,0:T(8,128)(2,1)S(1)}, u32[]{:S(2)}, u32[]{:S(2)}) collective-permute-start(bf16[64,2048]{1,0:T(8,128)(2,1)S(1)} %get-tuple-element.48), channel_id=1, source_target_pairs={{0,3},{1,0},{2,1},{3,2},{4,7},{5,4},{6,5},{7,6},{8,11},{9,8},{10,9... | collective-permute-start | bytes 786440 | tf_op jit(solution)/shard_map/ppermute | solution.py:50
  75.4 10.9 %collective-permute-start.17 = (bf16[64,2048]{1,0:T(8,128)(2,1)S(1)}, bf16[64,2048]{1,0:T(8,128)(2,1)S(1)}, u32[]{:S(2)}, u32[]{:S(2)}) collective-permute-start(bf16[64,2048]{1,0:T(8,128)(2,1)S(1)} %get-tuple-element.48), channel_id=1, source_target_pairs={{0,1},{1,2},{2,3},{3,0},{4,5},{5,6},{6,7},{7,4},{8,9},{9,10},{10,1... | collective-permute-start | bytes 786440 | tf_op jit(solution)/shard_map/ppermute | solution.py:50
  83.4 9.6 %collective-permute-start.22 = (bf16[128,2048]{1,0:T(8,128)(2,1)S(1)}, bf16[128,2048]{1,0:T(8,128)(2,1)S(1)}, u32[]{:S(2)}, u32[]{:S(2)}) collective-permute-start(bf16[128,2048]{1,0:T(8,128)(2,1)S(1)} %constant_dynamic-update-slice_fusion.2.b_ref), channel_id=1, source_target_pairs={{0,12},{1,13},{2,14},{3,15},{4,0},{5,1},{6,2},{7,3},{8,4},{9,5},{1... | collective-permute-start | bytes 1572872 | tf_op jit(solution)/shard_map/ppermute | solution.py:57
  86.3 10.5 %collective-permute-start.18 = (bf16[128,2048]{1,0:T(8,128)(2,1)S(1)}, bf16[128,2048]{1,0:T(8,128)(2,1)S(1)}, u32[]{:S(2)}, u32[]{:S(2)}) collective-permute-start(bf16[128,2048]{1,0:T(8,128)(2,1)S(1)} %constant_dynamic-update-slice_fusion.a_ref), channel_id=1, source_target_pairs={{0,4},{1,5},{2,6},{3,7},{4,8},{5,9},{6,10},{7,11},{8,12},{9,13},{1... | collective-permute-start | bytes 1572872 | tf_op jit(solution)/shard_map/ppermute | solution.py:57
  86.4 12.2 %collective-permute-start.25 = (bf16[128,2048]{1,0:T(8,128)(2,1)S(1)}, bf16[128,2048]{1,0:T(8,128)(2,1)S(1)}, u32[]{:S(2)}, u32[]{:S(2)}) collective-permute-start(bf16[128,2048]{1,0:T(8,128)(2,1)S(1)} %constant_dynamic-update-slice_fusion.a_ref), channel_id=1, source_target_pairs={{0,12},{1,13},{2,14},{3,15},{4,0},{5,1},{6,2},{7,3},{8,4},{9,5},{1... | collective-permute-start | bytes 1572872 | tf_op jit(solution)/shard_map/ppermute | solution.py:57
  89.6 12.8 %collective-permute-start.24 = (bf16[128,2048]{1,0:T(8,128)(2,1)S(1)}, bf16[128,2048]{1,0:T(8,128)(2,1)S(1)}, u32[]{:S(2)}, u32[]{:S(2)}) collective-permute-start(bf16[128,2048]{1,0:T(8,128)(2,1)S(1)} %constant_dynamic-update-slice_fusion.2.b_ref), channel_id=1, source_target_pairs={{0,4},{1,5},{2,6},{3,7},{4,8},{5,9},{6,10},{7,11},{8,12},{9,13},{1... | collective-permute-start | bytes 1572872 | tf_op jit(solution)/shard_map/ppermute | solution.py:57
  93.0 11.2 %collective-permute-start.23 = (bf16[128,2048]{1,0:T(8,128)(2,1)S(1)}, bf16[128,2048]{1,0:T(8,128)(2,1)S(1)}, u32[]{:S(2)}, u32[]{:S(2)}) collective-permute-start(bf16[128,2048]{1,0:T(8,128)(2,1)S(1)} %collective-permute-done.22.b_ref), channel_id=1, source_target_pairs={{0,12},{1,13},{2,14},{3,15},{4,0},{5,1},{6,2},{7,3},{8,4},{9,5},{1... | collective-permute-start | bytes 1572872 | tf_op jit(solution)/shard_map/ppermute | solution.py:57
  96.8 11.2 %collective-permute-start.19 = (bf16[128,2048]{1,0:T(8,128)(2,1)S(1)}, bf16[128,2048]{1,0:T(8,128)(2,1)S(1)}, u32[]{:S(2)}, u32[]{:S(2)}) collective-permute-start(bf16[128,2048]{1,0:T(8,128)(2,1)S(1)} %collective-permute-done.18.a_ref), channel_id=1, source_target_pairs={{0,4},{1,5},{2,6},{3,7},{4,8},{5,9},{6,10},{7,11},{8,12},{9,13},{1... | collective-permute-start | bytes 1572872 | tf_op jit(solution)/shard_map/ppermute | solution.py:57
  113.1 9.6 %collective-permute-start.27 = (bf16[128,1024]{1,0:T(8,128)(2,1)S(1)}, bf16[128,1024]{1,0:T(8,128)(2,1)S(1)}, u32[]{:S(2)}, u32[]{:S(2)}) collective-permute-start(bf16[128,1024]{1,0:T(8,128)(2,1)S(1)} %bitcast.17), channel_id=1, source_target_pairs={{0,32},{1,33},{2,34},{3,35},{4,36},{5,37},{6,38},{7,39},{8,40},{9,... | collective-permute-start | bytes 786440 | tf_op jit(solution)/shard_map/ppermute | solution.py:43
  114.0 15.1 %collective-permute-start.28 = (bf16[128,1024]{1,0:T(8,128)(2,1)S(1)}, bf16[128,1024]{1,0:T(8,128)(2,1)S(1)}, u32[]{:S(2)}, u32[]{:S(2)}) collective-permute-start(bf16[128,1024]{1,0:T(8,128)(2,1)S(1)} %bitcast.16), channel_id=1, source_target_pairs={{0,64},{1,65},{2,66},{3,67},{4,68},{5,69},{6,70},{7,71},{8,72},{9,... | collective-permute-start | bytes 786440 | tf_op jit(solution)/shard_map/ppermute | solution.py:43
  116.9 12.1 %collective-permute-start.29 = (bf16[128,1024]{1,0:T(8,128)(2,1)S(1)}, bf16[128,1024]{1,0:T(8,128)(2,1)S(1)}, u32[]{:S(2)}, u32[]{:S(2)}) collective-permute-start(bf16[128,1024]{1,0:T(8,128)(2,1)S(1)} %bitcast.15), channel_id=1, source_target_pairs={{0,96},{1,97},{2,98},{3,99},{4,100},{5,101},{6,102},{7,103},{8,104... | collective-permute-start | bytes 786440 | tf_op jit(solution)/shard_map/ppermute | solution.py:43
  (17 other events, 170.2 us)

commit v4 on v3

--- a/solution.py
+++ b/solution.py
@@ -19,7 +19,8 @@
 BF16 = jnp.bfloat16
 F32 = jnp.float32
 MIB = 1024 * 1024
-TOGETHER = 4
+TOGETHER = 8
+LOG2_E = 1.4426950408889634
 
 
 def pairs(move):
@@ -106,29 +107,28 @@
         copy.wait()
 
 
-def project_group(rows, heads, group, hs, sq, wq_ref, wk_ref, wv_ref, outs):
-    first, count = group[0], len(group)
-    depth = hs.shape[2]
-    lhs = hs[4 * first : 4 * (first + count)].reshape(4 * count * rows, depth)
+def project_blocks(rows, heads, first, hs, sq, wq_ref, wk_ref, wv_ref, outs):
     per = outs[0].shape[0]
+    count = per * len(outs)
+    lhs = hs[first : first + count].reshape(count * rows, hs.shape[2])
     for n in range(heads // 2 + 1):
         if n == heads // 2:
             rhs = jnp.concatenate([wk_ref[...], wv_ref[...]], axis=1)
         else:
             rhs = wq_ref[:, n * 256 : (n + 1) * 256]
         acc = jnp.dot(lhs, rhs, preferred_element_type=F32).astype(BF16)
-        for i in range(4 * count):
+        for i in range(count):
             for hh in range(2):
                 head = 2 * n + hh
                 outs[i // per][i % per, head * rows : (head + 1) * rows, :] = acc[
                     i * rows : (i + 1) * rows, hh * HD : (hh + 1) * HD
                 ]
-    for i in range(4 * count):
-        outs[i // per][i % per, (heads + 2) * rows :, :] = sq[4 * first + i]
+    for i in range(count):
+        outs[i // per][i % per, (heads + 2) * rows :, :] = sq[first + i]
 
 
 def project_first_body(rows, heads, gain_ref, wq_ref, wk_ref, wv_ref, *refs):
-    blocks, outs, (hs, sq) = refs[:8], refs[8:10], refs[10:]
+    blocks, outs, (hs, sq) = refs[:8], refs[8:12], refs[12:]
     y, c, z, x = place()
     gain = gain_ref[...].astype(F32).reshape(1, -1)
     depth = gain.shape[1]
@@ -140,8 +140,9 @@
             dz = (y - i // 2 - z) % 4
             dx = (2 * (c ^ (i % 2)) + j - x) % 4
             e, f = jnp.where(c == 0, dx, dz), jnp.where(c == 0, dz, dx)
-            at = jnp.where(e == 2, 0, jnp.where(e == 0, 3, (e + 1) // 2))
-            slot = 4 * at + f
+            slot = jnp.where(e == 2, f, 12 + f)
+            slot = jnp.where(e == 1, jnp.where(f >= 2, 2 + f, 8 + f), slot)
+            slot = jnp.where(e == 3, jnp.where(f < 2, 6 + f, 8 + f), slot)
             hs[slot] = (value * gain).astype(BF16)
             square = value * value
             high = square.astype(BF16)
@@ -155,23 +156,21 @@
                     preferred_element_type=F32,
                 )
             sq[slot] = split_high_low(total)
-    project_group(rows, heads, (0,), hs, sq, wq_ref, wk_ref, wv_ref, outs)
-
-
-def project_middle_body(rows, heads, token_ref, hs, sq, wq_ref, wk_ref, wv_ref, *outs):
-    project_group(rows, heads, (1, 2), hs, sq, wq_ref, wk_ref, wv_ref, outs)
-
-
-def project_last_body(
-    rows, heads, hs, sq, wq_ref, wk_ref, wv_ref, kc_hbm, vc_hbm, out_ref, kc_ref, vc_ref, sems
-):
+    project_blocks(rows, heads, 0, hs, sq, wq_ref, wk_ref, wv_ref, outs)
+
+
+def project_second_body(rows, heads, hs, sq, wq_ref, wk_ref, wv_ref, *outs):
+    project_blocks(rows, heads, 8, hs, sq, wq_ref, wk_ref, wv_ref, outs)
+
+
+def caches_body(after_ref, kc_hbm, vc_hbm, kc_ref, vc_ref, token_ref, sems):
     copies = [
         pltpu.make_async_copy(kc_hbm, kc_ref, sems.at[0]),
         pltpu.make_async_copy(vc_hbm, vc_ref, sems.at[1]),
     ]
     for copy in copies:
         copy.start()
-    project_group(rows, heads, (3,), hs, sq, wq_ref, wk_ref, wv_ref, [out_ref])
+    token_ref[...] = jnp.zeros_like(token_ref)
     for copy in copies:
         copy.wait()
 
@@ -217,8 +216,8 @@
     vf[...] = fresh.astype(F32)
 
     per = NEW * heads
-    scale = HD ** (-0.5)
-    slot_of = lax.broadcasted_iota(jnp.int32, (per, slots), 1)
+    scale = HD ** (-0.5) * LOG2_E
+    slot_of = lax.broadcasted_iota(jnp.int32, (1, slots), 1)
     second = lax.broadcasted_iota(jnp.int32, (per, 1), 0) >= heads
 
     def several(first, count):
@@ -231,37 +230,36 @@
             for q, s in zip(query, ids)
         ]
         scores = [
-            jnp.where(slot_of < len_ref[s], v * scale, -jnp.inf) for v, s in zip(scores, ids)
-        ]
-        s0 = [
-            jnp.sum(q * kf[pl.ds(2 * s, 1), :], axis=1, keepdims=True) * scale
+            v + jnp.where(slot_of < len_ref[s], 0.0, -jnp.inf) for v, s in zip(scores, ids)
+        ]
+        s0 = [jnp.sum(q * kf[pl.ds(2 * s, 1), :], axis=1, keepdims=True) for q, s in zip(query, ids)]
+        s1 = [
+            jnp.where(
+                second,
+                jnp.sum(q * kf[pl.ds(2 * s + 1, 1), :], axis=1, keepdims=True),
+                -jnp.inf,
+            )
             for q, s in zip(query, ids)
         ]
-        s1 = [
-            jnp.sum(q * kf[pl.ds(2 * s + 1, 1), :], axis=1, keepdims=True) * scale
-            for q, s in zip(query, ids)
-        ]
-        s1 = [jnp.where(second, v, -jnp.inf) for v in s1]
         highest = [
             jnp.maximum(jnp.max(v, axis=1, keepdims=True), jnp.maximum(a, b))
             for v, a, b in zip(scores, s0, s1)
         ]
-        probs = [jnp.exp(v - m) for v, m in zip(scores, highest)]
-        p0 = [jnp.exp(v - m) for v, m in zip(s0, highest)]
-        p1 = [jnp.exp(v - m) for v, m in zip(s1, highest)]
+        probs = [jnp.exp2((v - m) * scale) for v, m in zip(scores, highest)]
+        p0 = [jnp.exp2((v - m) * scale) for v, m in zip(s0, highest)]
+        p1 = [jnp.exp2((v - m) * scale) for v, m in zip(s1, highest)]
         norm = [
             1.0 / (jnp.sum(v, axis=1, keepdims=True) + a + b) for v, a, b in zip(probs, p0, p1)
         ]
         out = [
-            jnp.dot((v * n).astype(BF16), vbuf[s], preferred_element_type=F32)
-            for v, n, s in zip(probs, norm, ids)
+            jnp.dot(v.astype(BF16), vbuf[s], preferred_element_type=F32)
+            for v, s in zip(probs, ids)
         ]
         for u, s in enumerate(ids):
-            w0 = (p0[u] * norm[u]).astype(BF16).astype(F32)
-            w1 = (p1[u] * norm[u]).astype(BF16).astype(F32)
+            w0, w1 = p0[u].astype(BF16).astype(F32), p1[u].astype(BF16).astype(F32)
             os[pl.ds(pl.multiple_of(s * per, per), per), :] = (
                 out[u] + w0 * vf[pl.ds(2 * s, 1), :] + w1 * vf[pl.ds(2 * s + 1, 1), :]
-            )
+            ) * norm[u]
 
     def step(i, carry):
         several(TOGETHER * i, TOGETHER)
@@ -315,7 +313,8 @@
     cosine = jnp.concatenate([cosine, cosine], 1)
     sine = jnp.concatenate([-sine, sine], 1)
 
-    received = [shift_y(hidden, d) for d in (1, 2, 3)]
+    two, one, three = [shift_y(hidden, d) for d in (2, 1, 3)]
+    received = [one, two, three]
     sources = [hidden, gain, w_query, w_key, w_value]
     back, own, scale, *weights = call(
         load_body,
@@ -330,23 +329,22 @@
         blocks += [value, swap_core(value)]
 
     half = shape((2, length, HD))
-    two_a, two_b, scaled, squares = call(
+    two_a, two_b, one_b, three_a, scaled, squares = call(
         functools.partial(project_first_body, rows, heads),
-        [half, half, shape((16, rows, depth)), shape((16, 16, HD))],
+        [half] * 4 + [shape((16, rows, depth)), shape((16, 16, HD))],
         [VSPEC] * 12,
         "project_first",
-        12,
+        14,
     )(scale, *weights, *blocks)
     over_a, over_b = shift_first(two_a, 1), shift_first(two_b, 3)
-    token = swap_core(squares[0])
-    one_a, one_b, three_a, three_b = call(
-        functools.partial(project_middle_body, rows, heads),
+    from_one_b, from_three_a = shift_first(one_b, 1), shift_first(three_a, 3)
+    one_a, three_b, own_a, own_b = call(
+        functools.partial(project_second_body, rows, heads),
         [half] * 4,
-        [VSPEC] * 6,
-        "project_middle",
+        [VSPEC] * 5,
+        "project_second",
         12,
-    )(token, scaled, squares, *weights)
-    from_one_b, from_three_a = shift_first(one_b, 1), shift_first(three_a, 3)
+    )(scaled, squares, *weights)
 
     def add(terms, *values):
         return call(
@@ -358,26 +356,26 @@
         )(*values)
 
     pairwise = [[[(0, 0), (1, 0)], [(0, 1), (1, 1)]]]
-    from_one_a = shift_first(add(pairwise, one_a, over_a)[0], 1)
-    from_three_b = shift_first(add(pairwise, three_b, over_b)[0], 3)
-    own_group, keys, values = call(
-        functools.partial(project_last_body, rows, heads),
-        [shape((4, length, HD))] + [pltpu.VMEM(v.shape, v.dtype) for v in (key_cache, value_cache)],
-        [VSPEC] * 5 + [HSPEC] * 2,
-        "project_last",
-        12,
+    sum_one, sum_three = add(pairwise, one_a, over_a)[0], add(pairwise, three_b, over_b)[0]
+    from_one_a, from_three_b = shift_first(sum_one, 1), shift_first(sum_three, 3)
+    keys, values, token = call(
+        caches_body,
+        [pltpu.VMEM(v.shape, v.dtype) for v in (key_cache, value_cache)] + [shape((16, HD))],
+        [VSPEC, HSPEC, HSPEC],
+        "load_caches",
+        4,
         scratch=[pltpu.SemaphoreType.DMA((2,))],
-    )(scaled, squares, *weights, in_hbm(key_cache), in_hbm(value_cache))
+    )(sum_three, in_hbm(key_cache), in_hbm(value_cache))
     terms = [
-        [[(0, 2), (3, 0), (4, 0)]],
-        [[(0, 1), (1, 1), (2, 1)]],
-        [[(0, 3), (3, 1), (4, 1)]],
+        [[(1, 0), (4, 0), (5, 0)]],
+        [[(0, 1), (2, 1), (3, 1)]],
+        [[(1, 1), (4, 1), (5, 1)]],
     ]
     two, one, three = add(
-        terms, own_group, from_one_a, from_three_a, from_one_b, from_three_b
+        terms, own_a, own_b, from_one_a, from_three_a, from_one_b, from_three_b, token
     )
     arrived = [shift_second(two, 2), shift_second(one, 1), shift_second(three, 3)]
-    parts = [own_group, from_one_a, from_three_a] + arrived
+    parts = [own_a, from_one_a, from_three_a] + arrived
 
     context, fresh_keys, fresh_values = call(
         functools.partial(attend_body, rows, heads),
@@ -393,7 +391,7 @@
         ],
     )(lengths, *parts, cosine, sine, keys, values)
 
-    one, three, two = shift_first(context, 1), shift_first(context, 3), shift_first(context, 2)
+    two, one, three = [shift_first(context, e) for e in (2, 1, 3)]
     low, high = jnp.concatenate([context, one], 0), jnp.concatenate([two, three], 0)
     one_low, three_high = shift_second(low, 1), shift_second(high, 3)
     two_low, two_high = shift_second(one_low, 1), shift_second(three_high, 3)
@@ -424,10 +422,13 @@
         project_out(three_low, three_high),
     )
     both = mine.astype(F32) + swap_core(theirs).astype(F32)
-    both = both.reshape(4, 2 * rows, width)
-    result = hidden.astype(F32) + both[0]
-    for value in [shift_y(both[g].astype(BF16), g) for g in (1, 2, 3)]:
-        result = result + value.astype(F32)
+    over_a, over_b = shift_y(both[4].astype(BF16), 1), shift_y(both[5].astype(BF16), 3)
+    from_one_b, from_three_a = shift_y(both[3].astype(BF16), 1), shift_y(both[6].astype(BF16), 3)
+    from_one_a = shift_y((both[2] + over_a.astype(F32)).astype(BF16), 1)
+    from_three_b = shift_y((both[7] + over_b.astype(F32)).astype(BF16), 3)
+    upper = both[0] + from_one_a.astype(F32) + from_three_a.astype(F32)
+    lower = both[1] + from_one_b.astype(F32) + from_three_b.astype(F32)
+    result = hidden.astype(F32) + jnp.concatenate([upper, lower], axis=0)
     return result.astype(BF16), fresh_keys, fresh_values
 
 

time: 131 us -> 126 us (0.962)
  starting transfers between devices: 43.3 us -> 48.6 us
  local copies, waits for them, and re-layouts: 5.51 us -> 0.23 us
  Pallas kernels: 31.5 us -> 29.1 us
  waiting for transfers between devices: 46.4 us -> 44.8 us
    ppermute x9, waiting for transfers between devices: 7.79 us -> 13.7 us  [shift_first(): return lax.ppermute(value, AXES, pairs(move))]
    unnamed x24 -> x12, local copies, waits for them, and re-layouts: 4.05 us -> 0.06 us
    ppermute x9, waiting for transfers between devices: 16.3 us -> 12.6 us  [shift_second(): return lax.ppermute(value, AXES, pairs(move))]
    ppermute x6 -> x9, waiting for transfers between devices: 17.5 us -> 14.4 us  [shift_y(): lax.ppermute(value, AXES, pairs(lambda y, c, z, x: (y + step, c, z, x)))]
    ppermute x9, starting transfers between devices: 16.8 us -> 19.2 us  [shift_second(): return lax.ppermute(value, AXES, pairs(move))]
    ppermute x6 -> x9, starting transfers between devices: 12.4 us -> 14.6 us  [shift_y(): lax.ppermute(value, AXES, pairs(lambda y, c, z, x: (y + step, c, z, x)))]
    pallas_call x1, Pallas kernels: 7.93 us -> 5.89 us  [local(): call(functools.partial(attend_body, rows, heads), [shape((rows, heads * H...]
    ppermute x9, starting transfers between devices: 12.3 us -> 14.1 us  [shift_first(): return lax.ppermute(value, AXES, pairs(move))]
  transfers between devices with their start and end apart: 30 -> 32, of which waited for: 20 -> 20; matrix products, arithmetic and copies ran while one was open for 2% -> 0% of each run, Pallas kernels for 14% -> 12%
where the time goes in v4:
time: 126 us; the launch traced here: 125 us
  starting transfers between devices  48.6 us (39%)
  waiting for transfers between devices  44.8 us (36%)
  Pallas kernels  29.1 us (23%)
  other arithmetic  1.78 us (1%)
    ppermute x9, starting transfers between devices, shift_second(): return lax.ppermute(value, AXES, pairs(move))  19.2 us
    ppermute x9, starting transfers between devices, shift_y(): lax.ppermute(value, AXES, pairs(lambda y, c, z, x: (y + step, c, z, x)))  14.6 us
    ppermute x9, waiting for transfers between devices, shift_y(): lax.ppermute(value, AXES, pairs(lambda y, c, z, x: (y + step, c, z, x)))  14.4 us
    ppermute x9, starting transfers between devices, shift_first(): return lax.ppermute(value, AXES, pairs(move))  14.1 us
    ppermute x9, waiting for transfers between devices, shift_first(): return lax.ppermute(value, AXES, pairs(move))  13.7 us
    ppermute x9, waiting for transfers between devices, shift_second(): return lax.ppermute(value, AXES, pairs(move))  12.6 us
    pallas_call x1, Pallas kernels, local(): call(functools.partial(attend_body, rows, heads), [shape((rows, heads * H...  5.89 us
    pallas_call x1, Pallas kernels, local(): call(caches_body, [pltpu.VMEM(v.shape, v.dtype) for v in (key_cache, valu...  5.85 us
  transfers between devices with their start and end apart: 32, of which 20 were waited for; matrix products, arithmetic and copies ran while one was open for 0% of the time, Pallas kernels for 12%

profile of v4, /device:TPU:0, one launch (start us, length us, event | category | flops | bytes accessed | tf_op | source)
XLA Modules:
  0.0 125.4 jit_solution(14126399966032540750)
XLA Ops:
  2.4 2.9 %collective-permute-start.3 = (bf16[128,1024]{1,0:T(8,128)(2,1)}, bf16[128,1024]{1,0:T(8,128)(2,1)S(1)}, u32[]{:S(2)}, u32[]{:S(2)}) collective-permute-start(bf16[128,1024]{1,0:T(8,128)(2,1)} %hidden_hbm.1), channel_id=1, source_target_pairs={{0,64},{1,65},{2,66},{3,67},{4,68},{5,69},{6,70},{7,71},{8,72},{9,... | collective-permute-start | bytes 786440 | tf_op jit(solution)/shard_map/ppermute | solution.py:44
  6.6 3.7 %collective-permute-done.back_ref = bf16[128,1024]{1,0:T(8,128)(2,1)S(1)} collective-permute-done((bf16[128,1024]{1,0:T(8,128)(2,1)}, bf16[128,1024]{1,0:T(8,128)(2,1)S(1)}, u32[]{:S(2)}, u32[]{:S(2)}) %collective-permute-start) | collective-permute-done | bytes 262176 | tf_op jit(solution)/shard_map/ppermute | solution.py:44
  10.3 2.5 %load.1 = (bf16[128,1024]{1,0:T(8,128)(2,1)S(1)}, bf16[128,1024]{1,0:T(8,128)(2,1)S(1)}, bf16[1024]{0:T(1024)(128)(2,1)S(1)}, bf16[1024,2048]{1,0:T(8,128)(2,1)S...) custom-call(bf16[128,1024]{1,0:T(8,128)(2,1)S(1)} %collective-permute-done.back_ref, ...), custom_call_target="tpu_custom_call" | custom-call | tf_op jit(solution)/shard_map/load/pallas_call | solution.py:319
  12.9 4.2 %collective-permute-done.3.refs_4_ = bf16[128,1024]{1,0:T(8,128)(2,1)S(1)} collective-permute-done((bf16[128,1024]{1,0:T(8,128)(2,1)}, bf16[128,1024]{1,0:T(8,128)(2,1)S(1)}, u32[]{:S(2)}, u32[]{:S(2)}) %collective-permute-start.3) | collective-permute-done | bytes 262176 | tf_op jit(solution)/shard_map/ppermute | solution.py:44
  19.0 4.9 %project_first.1 = (bf16[2,1168,128]{2,1,0:T(8,128)(2,1)S(1)}, bf16[2,1168,128]{2,1,0:T(8,128)(2,1)S(1)}, bf16[2,1168,128]{2,1,0:T(8,128)(2,1)}, bf16[2,1168,128...) custom-call(bf16[1024]{0:T(1024)(128)(2,1)S(1)} %get-tuple-element.30.gain_ref, ...), custom_call_target="tpu_custom_call" | custom-call | tf_op jit(solution)/shard_map/project_first/pallas_call | solution.py:332
  29.1 2.6 %project_second.1 = (bf16[2,1168,128]{2,1,0:T(8,128)(2,1)S(1)}, bf16[2,1168,128]{2,1,0:T(8,128)(2,1)S(1)}, bf16[2,1168,128]{2,1,0:T(8,128)(2,1)S(1)}, bf16[2,1168,128]{2,1,0:T(8,128)(2,1)S(1)}) custom-call(bf16[16,64,1024]{2,1,0:T(8,128)(2,1)S(1)} %get-tuple-element.36.hs, bf16[16,16,128]{2,1,0:T(8,128)(2,1)S(1)} %get-tuple-element.37.sq, ...), custom_call_target="tpu_custom_call" | custom-call | tf_op jit(solution)/shard_map/project_second/pallas_call | solution.py:341
  31.8 3.3 %collective-permute-done.7.refs_1_ = bf16[2,1168,128]{2,1,0:T(8,128)(2,1)S(1)} collective-permute-done((bf16[2,1168,128]{2,1,0:T(8,128)(2,1)S(1)}, bf16[2,1168,128]{2,1,0:T(8,128)(2,1)S(1)}, u32[]{:S(2)}, u32[]{:S(2)}) %collective-permute-start.7) | collective-permute-done | bytes 598048 | tf_op jit(solution)/shard_map/ppermute | solution.py:51
  35.7 3.0 %collective-permute-start.12 = (bf16[2,1168,128]{2,1,0:T(8,128)(2,1)S(1)}, bf16[2,1168,128]{2,1,0:T(8,128)(2,1)}, u32[]{:S(2)}, u32[]{:S(2)}) collective-permute-start(bf16[2,1168,128]{2,1,0:T(8,128)(2,1)S(1)} %add.81.after_ref), channel_id=1, source_target_pairs={{0,3},{1,0},{2,1},{3,2},{4,7},{5,4},{6,5},{7,6},{8,11},{9,8},{10,9... | collective-permute-start | bytes 1794056 | tf_op jit(solution)/shard_map/ppermute | solution.py:51
  38.9 5.9 %load_caches.1 = (bf16[32,1024,128]{2,1,0:T(8,128)(2,1)S(1)}, bf16[32,1024,128]{2,1,0:T(8,128)(2,1)S(1)}, bf16[16,128]{1,0:T(8,128)(2,1)S(1)}) custom-call(bf16[2,1168,128]{2,1,0:T(8,128)(2,1)S(1)} %add.81.after_ref, bf16[32,1024,128]{2,1,0:T(8,128)(2,1)} %kc_hbm.1, bf16[32,1024,128]{2,1,0:T(8,128)(2,1)} %vc_hbm.1), custom_call_target="tpu_custom_call" | custom-call | tf_op jit(solution)/shard_map/load_caches/pallas_call | solution.py:361
  44.8 3.0 %collective-permute-done.8.refs_2_.p1_ref = bf16[2,1168,128]{2,1,0:T(8,128)(2,1)S(1)} collective-permute-done((bf16[2,1168,128]{2,1,0:T(8,128)(2,1)S(1)}, bf16[2,1168,128]{2,1,0:T(8,128)(2,1)S(1)}, u32[]{:S(2)}, u32[]{:S(2)}) %collective-permute-start.8) | collective-permute-done | bytes 598048 | tf_op jit(solution)/shard_map/ppermute | solution.py:51
  49.8 4.0 %collective-permute-start.13 = (bf16[1,1168,128]{2,1,0:T(8,128)(2,1)S(1)}, bf16[1,1168,128]{2,1,0:T(8,128)(2,1)S(1)}, u32[]{:S(2)}, u32[]{:S(2)}) collective-permute-start(bf16[1,1168,128]{2,1,0:T(8,128)(2,1)S(1)} %get-tuple-element.47), channel_id=1, source_target_pairs={{0,8},{1,9},{2,10},{3,11},{4,12},{5,13},{6,14},{7,15},{8,0},{9,1},... | collective-permute-start | bytes 897032 | tf_op jit(solution)/shard_map/ppermute | solution.py:58
  54.8 2.2 %collective-permute-start.15 = (bf16[1,1168,128]{2,1,0:T(8,128)(2,1)S(1)}, bf16[1,1168,128]{2,1,0:T(8,128)(2,1)S(1)}, u32[]{:S(2)}, u32[]{:S(2)}) collective-permute-start(bf16[1,1168,128]{2,1,0:T(8,128)(2,1)S(1)} %get-tuple-element.49), channel_id=1, source_target_pairs={{0,12},{1,13},{2,14},{3,15},{4,0},{5,1},{6,2},{7,3},{8,4},{9,5},{1... | collective-permute-start | bytes 897032 | tf_op jit(solution)/shard_map/ppermute | solution.py:58
  58.5 3.2 %collective-permute-done.14.r2_ref = bf16[1,1168,128]{2,1,0:T(8,128)(2,1)S(1)} collective-permute-done((bf16[1,1168,128]{2,1,0:T(8,128)(2,1)S(1)}, bf16[1,1168,128]{2,1,0:T(8,128)(2,1)S(1)}, u32[]{:S(2)}, u32[]{:S(2)}) %collective-permute-start.14) | collective-permute-done | bytes 299040 | tf_op jit(solution)/shard_map/ppermute | solution.py:58
  62.8 5.9 %attend.1 = (bf16[64,2048]{1,0:T(8,128)(2,1)S(1)}, bf16[64,128]{1,0:T(8,128)(2,1)}, bf16[64,128]{1,0:T(8,128)(2,1)}) custom-call(s32[32]{0:T(128)S(1)} %copy-done.3, bf16[2,1168,128]{2,1,0:T(8,128)(2,1)S(1)} %get-tuple-element.38.refs_0_.p0_ref, bf16[2,1168,128]{2,1,0:T(8,128)(2,1)S(1)} %collective-permute-done.8.refs_2_.p1_ref, ...), custom_call_target="tpu_custom_call" | custom-call | tf_op jit(solution)/shard_map/attend/pallas_call | solution.py:380
  70.2 2.9 %collective-permute-start.19 = (bf16[64,2048]{1,0:T(8,128)(2,1)S(1)}, bf16[64,2048]{1,0:T(8,128)(2,1)S(1)}, u32[]{:S(2)}, u32[]{:S(2)}) collective-permute-start(bf16[64,2048]{1,0:T(8,128)(2,1)S(1)} %get-tuple-element.52), channel_id=1, source_target_pairs={{0,2},{1,3},{2,0},{3,1},{4,6},{5,7},{6,4},{7,5},{8,10},{9,11},{10,... | collective-permute-start | bytes 786440 | tf_op jit(solution)/shard_map/ppermute | solution.py:51
  77.7 4.9 %collective-permute-done.19 = bf16[64,2048]{1,0:T(8,128)(2,1)S(1)} collective-permute-done((bf16[64,2048]{1,0:T(8,128)(2,1)S(1)}, bf16[64,2048]{1,0:T(8,128)(2,1)S(1)}, u32[]{:S(2)}, u32[]{:S(2)}) %collective-permute-start.19) | collective-permute-done | bytes 262176 | tf_op jit(solution)/shard_map/ppermute | solution.py:51
  82.7 3.7 %collective-permute-start.21 = (bf16[128,2048]{1,0:T(8,128)(2,1)S(1)}, bf16[128,2048]{1,0:T(8,128)(2,1)S(1)}, u32[]{:S(2)}, u32[]{:S(2)}) collective-permute-start(bf16[128,2048]{1,0:T(8,128)(2,1)S(1)} %constant_dynamic-update-slice_fusion.2.b_ref), channel_id=1, source_target_pairs={{0,12},{1,13},{2,14},{3,15},{4,0},{5,1},{6,2},{7,3},{8,4},{9,5},{1... | collective-permute-start | bytes 1572872 | tf_op jit(solution)/shard_map/ppermute | solution.py:58
  86.4 3.2 %collective-permute-start.24 = (bf16[128,2048]{1,0:T(8,128)(2,1)S(1)}, bf16[128,2048]{1,0:T(8,128)(2,1)S(1)}, u32[]{:S(2)}, u32[]{:S(2)}) collective-permute-start(bf16[128,2048]{1,0:T(8,128)(2,1)S(1)} %constant_dynamic-update-slice_fusion.a_ref), channel_id=1, source_target_pairs={{0,12},{1,13},{2,14},{3,15},{4,0},{5,1},{6,2},{7,3},{8,4},{9,5},{1... | collective-permute-start | bytes 1572872 | tf_op jit(solution)/shard_map/ppermute | solution.py:58
  89.6 3.5 %collective-permute-done.21.b_ref = bf16[128,2048]{1,0:T(8,128)(2,1)S(1)} collective-permute-done((bf16[128,2048]{1,0:T(8,128)(2,1)S(1)}, bf16[128,2048]{1,0:T(8,128)(2,1)S(1)}, u32[]{:S(2)}, u32[]{:S(2)}) %collective-permute-start.21) | collective-permute-done | bytes 524320 | tf_op jit(solution)/shard_map/ppermute | solution.py:58
  93.1 3.7 %collective-permute-start.22 = (bf16[128,2048]{1,0:T(8,128)(2,1)S(1)}, bf16[128,2048]{1,0:T(8,128)(2,1)S(1)}, u32[]{:S(2)}, u32[]{:S(2)}) collective-permute-start(bf16[128,2048]{1,0:T(8,128)(2,1)S(1)} %collective-permute-done.21.b_ref), channel_id=1, source_target_pairs={{0,12},{1,13},{2,14},{3,15},{4,0},{5,1},{6,2},{7,3},{8,4},{9,5},{1... | collective-permute-start | bytes 1572872 | tf_op jit(solution)/shard_map/ppermute | solution.py:58
  106.1 2.6 %collective-permute-done.25 = bf16[8,64,1024]{2,1,0:T(8,128)(2,1)S(1)} collective-permute-done((bf16[8,64,1024]{2,1,0:T(8,128)(2,1)S(1)}, bf16[8,64,1024]{2,1,0:T(8,128)(2,1)S(1)}, u32[]{:S(2)}, u32[]{:S(2)}) %collective-permute-start.25) | collective-permute-done | bytes 1048608 | tf_op jit(solution)/shard_map/ppermute | solution.py:40
  110.3 2.4 %collective-permute-start.30 = (bf16[64,1024]{1,0:T(8,128)(2,1)S(1)}, bf16[64,1024]{1,0:T(8,128)(2,1)S(1)}, u32[]{:S(2)}, u32[]{:S(2)}) collective-permute-start(bf16[64,1024]{1,0:T(8,128)(2,1)S(1)} %get-tuple-element.64), channel_id=1, source_target_pairs={{0,96},{1,97},{2,98},{3,99},{4,100},{5,101},{6,102},{7,103},{8,104... | collective-permute-start | bytes 393224 | tf_op jit(solution)/shard_map/ppermute | solution.py:44
  117.4 2.1 %collective-permute-start.27 = (bf16[64,1024]{1,0:T(8,128)(2,1)S(1)}, bf16[64,1024]{1,0:T(8,128)(2,1)S(1)}, u32[]{:S(2)}, u32[]{:S(2)}) collective-permute-start(bf16[64,1024]{1,0:T(8,128)(2,1)S(1)} %get-tuple-element.59), channel_id=1, source_target_pairs={{0,32},{1,33},{2,34},{3,35},{4,36},{5,37},{6,38},{7,39},{8,40},{9,... | collective-permute-start | bytes 393224 | tf_op jit(solution)/shard_map/ppermute | solution.py:44
  120.7 2.9 %collective-permute-done.27 = bf16[64,1024]{1,0:T(8,128)(2,1)S(1)} collective-permute-done((bf16[64,1024]{1,0:T(8,128)(2,1)S(1)}, bf16[64,1024]{1,0:T(8,128)(2,1)S(1)}, u32[]{:S(2)}, u32[]{:S(2)}) %collective-permute-start.27) | collective-permute-done | bytes 131104 | tf_op jit(solution)/shard_map/ppermute | solution.py:44
  (76 shorter events, 41.2 us)
Async XLA Ops:
  0.6 9.7 %collective-permute-start = (bf16[128,1024]{1,0:T(8,128)(2,1)}, bf16[128,1024]{1,0:T(8,128)(2,1)S(1)}, u32[]{:S(2)}, u32[]{:S(2)}) collective-permute-start(bf16[128,1024]{1,0:T(8,128)(2,1)} %hidden_hbm.1), channel_id=1, source_target_pairs={{0,32},{1,33},{2,34},{3,35},{4,36},{5,37},{6,38},{7,39},{8,40},{9,... | collective-permute-start | bytes 786440 | tf_op jit(solution)/shard_map/ppermute | solution.py:44
  2.4 14.7 %collective-permute-start.3 = (bf16[128,1024]{1,0:T(8,128)(2,1)}, bf16[128,1024]{1,0:T(8,128)(2,1)S(1)}, u32[]{:S(2)}, u32[]{:S(2)}) collective-permute-start(bf16[128,1024]{1,0:T(8,128)(2,1)} %hidden_hbm.1), channel_id=1, source_target_pairs={{0,64},{1,65},{2,66},{3,67},{4,68},{5,69},{6,70},{7,71},{8,72},{9,... | collective-permute-start | bytes 786440 | tf_op jit(solution)/shard_map/ppermute | solution.py:44
  5.3 11.9 %collective-permute-start.5 = (bf16[128,1024]{1,0:T(8,128)(2,1)}, bf16[128,1024]{1,0:T(8,128)(2,1)S(1)}, u32[]{:S(2)}, u32[]{:S(2)}) collective-permute-start(bf16[128,1024]{1,0:T(8,128)(2,1)} %hidden_hbm.1), channel_id=1, source_target_pairs={{0,96},{1,97},{2,98},{3,99},{4,100},{5,101},{6,102},{7,103},{8,104... | collective-permute-start | bytes 786440 | tf_op jit(solution)/shard_map/ppermute | solution.py:44
  6.6 11.0 %collective-permute-start.1 = (bf16[128,1024]{1,0:T(8,128)(2,1)}, bf16[128,1024]{1,0:T(8,128)(2,1)S(1)}, u32[]{:S(2)}, u32[]{:S(2)}) collective-permute-start(bf16[128,1024]{1,0:T(8,128)(2,1)} %hidden_hbm.1), channel_id=1, source_target_pairs={{0,16},{1,17},{2,18},{3,19},{4,20},{5,21},{6,22},{7,23},{8,24},{9,... | collective-permute-start | bytes 786440 | tf_op jit(solution)/shard_map/ppermute | solution.py:40
  23.9 11.2 %collective-permute-start.7 = (bf16[2,1168,128]{2,1,0:T(8,128)(2,1)S(1)}, bf16[2,1168,128]{2,1,0:T(8,128)(2,1)S(1)}, u32[]{:S(2)}, u32[]{:S(2)}) collective-permute-start(bf16[2,1168,128]{2,1,0:T(8,128)(2,1)S(1)} %get-tuple-element.40), channel_id=1, source_target_pairs={{0,1},{1,2},{2,3},{3,0},{4,5},{5,6},{6,7},{7,4},{8,9},{9,10},{10,1... | collective-permute-start | bytes 1794056 | tf_op jit(solution)/shard_map/ppermute | solution.py:51
  25.4 10.2 %collective-permute-start.11 = (bf16[2,1168,128]{2,1,0:T(8,128)(2,1)S(1)}, bf16[2,1168,128]{2,1,0:T(8,128)(2,1)S(1)}, u32[]{:S(2)}, u32[]{:S(2)}) collective-permute-start(bf16[2,1168,128]{2,1,0:T(8,128)(2,1)S(1)} %get-tuple-element.45), channel_id=1, source_target_pairs={{0,3},{1,0},{2,1},{3,2},{4,7},{5,4},{6,5},{7,6},{8,11},{9,8},{10,9... | collective-permute-start | bytes 1794056 | tf_op jit(solution)/shard_map/ppermute | solution.py:51
  27.1 17.7 %collective-permute-start.9 = (bf16[2,1168,128]{2,1,0:T(8,128)(2,1)}, bf16[2,1168,128]{2,1,0:T(8,128)(2,1)S(1)}, u32[]{:S(2)}, u32[]{:S(2)}) collective-permute-start(bf16[2,1168,128]{2,1,0:T(8,128)(2,1)} %get-tuple-element.41), channel_id=1, source_target_pairs={{0,3},{1,0},{2,1},{3,2},{4,7},{5,4},{6,5},{7,6},{8,11},{9,8},{10,9... | collective-permute-start | bytes 1794056 | tf_op jit(solution)/shard_map/ppermute | solution.py:51
  28.7 16.2 %collective-permute-start.10 = (bf16[2,1168,128]{2,1,0:T(8,128)(2,1)}, bf16[2,1168,128]{2,1,0:T(8,128)(2,1)}, u32[]{:S(2)}, u32[]{:S(2)}) collective-permute-start(bf16[2,1168,128]{2,1,0:T(8,128)(2,1)} %get-tuple-element.43), channel_id=1, source_target_pairs={{0,1},{1,2},{2,3},{3,0},{4,5},{5,6},{6,7},{7,4},{8,9},{9,10},{10,1... | collective-permute-start | bytes 1794056 | tf_op jit(solution)/shard_map/ppermute | solution.py:51
  35.2 12.7 %collective-permute-start.8 = (bf16[2,1168,128]{2,1,0:T(8,128)(2,1)S(1)}, bf16[2,1168,128]{2,1,0:T(8,128)(2,1)S(1)}, u32[]{:S(2)}, u32[]{:S(2)}) collective-permute-start(bf16[2,1168,128]{2,1,0:T(8,128)(2,1)S(1)} %add.80), channel_id=1, source_target_pairs={{0,1},{1,2},{2,3},{3,0},{4,5},{5,6},{6,7},{7,4},{8,9},{9,10},{10,1... | collective-permute-start | bytes 1794056 | tf_op jit(solution)/shard_map/ppermute | solution.py:51
  35.7 12.5 %collective-permute-start.12 = (bf16[2,1168,128]{2,1,0:T(8,128)(2,1)S(1)}, bf16[2,1168,128]{2,1,0:T(8,128)(2,1)}, u32[]{:S(2)}, u32[]{:S(2)}) collective-permute-start(bf16[2,1168,128]{2,1,0:T(8,128)(2,1)S(1)} %add.81.after_ref), channel_id=1, source_target_pairs={{0,3},{1,0},{2,1},{3,2},{4,7},{5,4},{6,5},{7,6},{8,11},{9,8},{10,9... | collective-permute-start | bytes 1794056 | tf_op jit(solution)/shard_map/ppermute | solution.py:51
  49.8 8.7 %collective-permute-start.13 = (bf16[1,1168,128]{2,1,0:T(8,128)(2,1)S(1)}, bf16[1,1168,128]{2,1,0:T(8,128)(2,1)S(1)}, u32[]{:S(2)}, u32[]{:S(2)}) collective-permute-start(bf16[1,1168,128]{2,1,0:T(8,128)(2,1)S(1)} %get-tuple-element.47), channel_id=1, source_target_pairs={{0,8},{1,9},{2,10},{3,11},{4,12},{5,13},{6,14},{7,15},{8,0},{9,1},... | collective-permute-start | bytes 897032 | tf_op jit(solution)/shard_map/ppermute | solution.py:58
  53.8 8.0 %collective-permute-start.14 = (bf16[1,1168,128]{2,1,0:T(8,128)(2,1)S(1)}, bf16[1,1168,128]{2,1,0:T(8,128)(2,1)S(1)}, u32[]{:S(2)}, u32[]{:S(2)}) collective-permute-start(bf16[1,1168,128]{2,1,0:T(8,128)(2,1)S(1)} %get-tuple-element.48), channel_id=1, source_target_pairs={{0,4},{1,5},{2,6},{3,7},{4,8},{5,9},{6,10},{7,11},{8,12},{9,13},{1... | collective-permute-start | bytes 897032 | tf_op jit(solution)/shard_map/ppermute | solution.py:58
  54.8 7.9 %collective-permute-start.15 = (bf16[1,1168,128]{2,1,0:T(8,128)(2,1)S(1)}, bf16[1,1168,128]{2,1,0:T(8,128)(2,1)S(1)}, u32[]{:S(2)}, u32[]{:S(2)}) collective-permute-start(bf16[1,1168,128]{2,1,0:T(8,128)(2,1)S(1)} %get-tuple-element.49), channel_id=1, source_target_pairs={{0,12},{1,13},{2,14},{3,15},{4,0},{5,1},{6,2},{7,3},{8,4},{9,5},{1... | collective-permute-start | bytes 897032 | tf_op jit(solution)/shard_map/ppermute | solution.py:58
  68.7 7.7 %collective-permute-start.16 = (bf16[64,2048]{1,0:T(8,128)(2,1)S(1)}, bf16[64,2048]{1,0:T(8,128)(2,1)S(1)}, u32[]{:S(2)}, u32[]{:S(2)}) collective-permute-start(bf16[64,2048]{1,0:T(8,128)(2,1)S(1)} %get-tuple-element.52), channel_id=1, source_target_pairs={{0,1},{1,2},{2,3},{3,0},{4,5},{5,6},{6,7},{7,4},{8,9},{9,10},{10,1... | collective-permute-start | bytes 786440 | tf_op jit(solution)/shard_map/ppermute | solution.py:51
  70.2 12.4 %collective-permute-start.19 = (bf16[64,2048]{1,0:T(8,128)(2,1)S(1)}, bf16[64,2048]{1,0:T(8,128)(2,1)S(1)}, u32[]{:S(2)}, u32[]{:S(2)}) collective-permute-start(bf16[64,2048]{1,0:T(8,128)(2,1)S(1)} %get-tuple-element.52), channel_id=1, source_target_pairs={{0,2},{1,3},{2,0},{3,1},{4,6},{5,7},{6,4},{7,5},{8,10},{9,11},{10,... | collective-permute-start | bytes 786440 | tf_op jit(solution)/shard_map/ppermute | solution.py:51
  73.2 9.5 %collective-permute-start.20 = (bf16[64,2048]{1,0:T(8,128)(2,1)S(1)}, bf16[64,2048]{1,0:T(8,128)(2,1)S(1)}, u32[]{:S(2)}, u32[]{:S(2)}) collective-permute-start(bf16[64,2048]{1,0:T(8,128)(2,1)S(1)} %get-tuple-element.52), channel_id=1, source_target_pairs={{0,3},{1,0},{2,1},{3,2},{4,7},{5,4},{6,5},{7,6},{8,11},{9,8},{10,9... | collective-permute-start | bytes 786440 | tf_op jit(solution)/shard_map/ppermute | solution.py:51
  76.3 13.3 %collective-permute-start.17 = (bf16[128,2048]{1,0:T(8,128)(2,1)S(1)}, bf16[128,2048]{1,0:T(8,128)(2,1)S(1)}, u32[]{:S(2)}, u32[]{:S(2)}) collective-permute-start(bf16[128,2048]{1,0:T(8,128)(2,1)S(1)} %constant_dynamic-update-slice_fusion.a_ref), channel_id=1, source_target_pairs={{0,4},{1,5},{2,6},{3,7},{4,8},{5,9},{6,10},{7,11},{8,12},{9,13},{1... | collective-permute-start | bytes 1572872 | tf_op jit(solution)/shard_map/ppermute | solution.py:58
  82.7 10.4 %collective-permute-start.21 = (bf16[128,2048]{1,0:T(8,128)(2,1)S(1)}, bf16[128,2048]{1,0:T(8,128)(2,1)S(1)}, u32[]{:S(2)}, u32[]{:S(2)}) collective-permute-start(bf16[128,2048]{1,0:T(8,128)(2,1)S(1)} %constant_dynamic-update-slice_fusion.2.b_ref), channel_id=1, source_target_pairs={{0,12},{1,13},{2,14},{3,15},{4,0},{5,1},{6,2},{7,3},{8,4},{9,5},{1... | collective-permute-start | bytes 1572872 | tf_op jit(solution)/shard_map/ppermute | solution.py:58
  86.4 11.7 %collective-permute-start.23 = (bf16[128,2048]{1,0:T(8,128)(2,1)S(1)}, bf16[128,2048]{1,0:T(8,128)(2,1)S(1)}, u32[]{:S(2)}, u32[]{:S(2)}) collective-permute-start(bf16[128,2048]{1,0:T(8,128)(2,1)S(1)} %constant_dynamic-update-slice_fusion.2.b_ref), channel_id=1, source_target_pairs={{0,4},{1,5},{2,6},{3,7},{4,8},{5,9},{6,10},{7,11},{8,12},{9,13},{1... | collective-permute-start | bytes 1572872 | tf_op jit(solution)/shard_map/ppermute | solution.py:58
  86.4 13.0 %collective-permute-start.24 = (bf16[128,2048]{1,0:T(8,128)(2,1)S(1)}, bf16[128,2048]{1,0:T(8,128)(2,1)S(1)}, u32[]{:S(2)}, u32[]{:S(2)}) collective-permute-start(bf16[128,2048]{1,0:T(8,128)(2,1)S(1)} %constant_dynamic-update-slice_fusion.a_ref), channel_id=1, source_target_pairs={{0,12},{1,13},{2,14},{3,15},{4,0},{5,1},{6,2},{7,3},{8,4},{9,5},{1... | collective-permute-start | bytes 1572872 | tf_op jit(solution)/shard_map/ppermute | solution.py:58
  89.6 12.8 %collective-permute-start.18 = (bf16[128,2048]{1,0:T(8,128)(2,1)S(1)}, bf16[128,2048]{1,0:T(8,128)(2,1)S(1)}, u32[]{:S(2)}, u32[]{:S(2)}) collective-permute-start(bf16[128,2048]{1,0:T(8,128)(2,1)S(1)} %collective-permute-done.17.a_ref), channel_id=1, source_target_pairs={{0,4},{1,5},{2,6},{3,7},{4,8},{5,9},{6,10},{7,11},{8,12},{9,13},{1... | collective-permute-start | bytes 1572872 | tf_op jit(solution)/shard_map/ppermute | solution.py:58
  93.1 11.2 %collective-permute-start.22 = (bf16[128,2048]{1,0:T(8,128)(2,1)S(1)}, bf16[128,2048]{1,0:T(8,128)(2,1)S(1)}, u32[]{:S(2)}, u32[]{:S(2)}) collective-permute-start(bf16[128,2048]{1,0:T(8,128)(2,1)S(1)} %collective-permute-done.21.b_ref), channel_id=1, source_target_pairs={{0,12},{1,13},{2,14},{3,15},{4,0},{5,1},{6,2},{7,3},{8,4},{9,5},{1... | collective-permute-start | bytes 1572872 | tf_op jit(solution)/shard_map/ppermute | solution.py:58
  110.3 7.1 %collective-permute-start.30 = (bf16[64,1024]{1,0:T(8,128)(2,1)S(1)}, bf16[64,1024]{1,0:T(8,128)(2,1)S(1)}, u32[]{:S(2)}, u32[]{:S(2)}) collective-permute-start(bf16[64,1024]{1,0:T(8,128)(2,1)S(1)} %get-tuple-element.64), channel_id=1, source_target_pairs={{0,96},{1,97},{2,98},{3,99},{4,100},{5,101},{6,102},{7,103},{8,104... | collective-permute-start | bytes 393224 | tf_op jit(solution)/shard_map/ppermute | solution.py:44
  112.6 8.1 %collective-permute-start.28 = (bf16[64,1024]{1,0:T(8,128)(2,1)S(1)}, bf16[64,1024]{1,0:T(8,128)(2,1)S(1)}, u32[]{:S(2)}, u32[]{:S(2)}) collective-permute-start(bf16[64,1024]{1,0:T(8,128)(2,1)S(1)} %get-tuple-element.66), channel_id=1, source_target_pairs={{0,96},{1,97},{2,98},{3,99},{4,100},{5,101},{6,102},{7,103},{8,104... | collective-permute-start | bytes 393224 | tf_op jit(solution)/shard_map/ppermute | solution.py:44
  (13 other events, 108.8 us)

commit v5 on v4

--- a/solution.py
+++ b/solution.py
@@ -132,8 +132,7 @@
     y, c, z, x = place()
     gain = gain_ref[...].astype(F32).reshape(1, -1)
     depth = gain.shape[1]
-    ones = jnp.ones((8, depth), BF16)
-    pad = jnp.zeros((HD - rows, depth), BF16)
+    pad = jnp.zeros((HD - rows, HD), F32)
     for i, block in enumerate(blocks):
         for j in range(2):
             value = block[j * rows : (j + 1) * rows, :].astype(F32)
@@ -144,17 +143,9 @@
             slot = jnp.where(e == 1, jnp.where(f >= 2, 2 + f, 8 + f), slot)
             slot = jnp.where(e == 3, jnp.where(f < 2, 6 + f, 8 + f), slot)
             hs[slot] = (value * gain).astype(BF16)
-            square = value * value
-            high = square.astype(BF16)
-            low = (square - high.astype(F32)).astype(BF16)
-            total = jnp.zeros((8, HD), F32)
-            for part in (high, low):
-                total += lax.dot_general(
-                    ones,
-                    jnp.concatenate([part, pad], axis=0),
-                    (((1,), (1,)), ((), ())),
-                    preferred_element_type=F32,
-                )
+            part = sum(value[:, n : n + HD] * value[:, n : n + HD] for n in range(0, depth, HD))
+            turned = jnp.transpose(jnp.concatenate([part, pad], axis=0))
+            total = jnp.broadcast_to(jnp.sum(turned, axis=0, keepdims=True), (8, HD))
             sq[slot] = split_high_low(total)
     project_blocks(rows, heads, 0, hs, sq, wq_ref, wk_ref, wv_ref, outs)
 
@@ -270,6 +261,10 @@
         ctx_ref[:, head * HD : (head + 1) * HD] = os[pl.ds(head, rows, stride=heads), :].astype(BF16)
 
 
+def together_body(token_ref, a_ref, out_ref):
+    out_ref[...] = a_ref[...]
+
+
 def output_body(a_ref, b_ref, w_ref, out_ref):
     lhs = jnp.concatenate([a_ref[...], b_ref[...]], axis=0)
     for n in range(w_ref.shape[1] // 256):
@@ -281,11 +276,11 @@
     y, c, z, x = place()
     output_body(a_ref, b_ref, w_ref, y2)
     for f, source in enumerate((y0_ref, y1_ref, y2, y3_ref)):
-        for e in range(4):
+        for place_of, e in enumerate((0, 2, 1, 3)):
             zz = jnp.where(c == 0, z - f, z - e) % 4
             xx = jnp.where(c == 0, x - e, x - f) % 4
             slot = 2 * ((zz - y) % 4) + xx % 2
-            top = e * rows
+            top = place_of * rows
             own = xx // 2 == c
 
             @pl.when(own)
@@ -391,8 +386,15 @@
         ],
     )(lengths, *parts, cosine, sine, keys, values)
 
+    context = call(
+        together_body,
+        [shape(context.shape)],
+        [VSPEC] * 2,
+        "together",
+        4,
+    )(swap_core(fresh_keys), context)[0]
     two, one, three = [shift_first(context, e) for e in (2, 1, 3)]
-    low, high = jnp.concatenate([context, one], 0), jnp.concatenate([two, three], 0)
+    low, high = jnp.concatenate([context, two], 0), jnp.concatenate([one, three], 0)
     one_low, three_high = shift_second(low, 1), shift_second(high, 3)
     two_low, two_high = shift_second(one_low, 1), shift_second(three_high, 3)
     one_high, three_low = shift_second(high, 1), shift_second(low, 3)

time: 126 us -> 123 us (0.976)
  waiting for transfers between devices: 44.8 us -> 42.9 us
    ppermute x9, waiting for transfers between devices: 13.7 us -> 10.5 us  [shift_first(): return lax.ppermute(value, AXES, pairs(move))]
    ppermute x5 -> x6, waiting for transfers between devices: 4.04 us -> 5.42 us  [swap_core(): return lax.ppermute(value, AXES, pairs(lambda y, c, z, x: (y, c + 1, z, x)))]
  transfers between devices with their start and end apart: 32 -> 33, of which waited for: 20 -> 23; matrix products, arithmetic and copies ran while one was open for 0% -> 1% of each run, Pallas kernels for 12% -> 12%
where the time goes in v5:
time: 123 us; the launch traced here: 122 us
  starting transfers between devices  48.1 us (39%)
  waiting for transfers between devices  42.9 us (35%)
  Pallas kernels  28.6 us (23%)
  other arithmetic  1.82 us (1%)
    ppermute x9, starting transfers between devices, shift_second(): return lax.ppermute(value, AXES, pairs(move))  18 us
    ppermute x9, starting transfers between devices, shift_first(): return lax.ppermute(value, AXES, pairs(move))  14.7 us
    ppermute x9, starting transfers between devices, shift_y(): lax.ppermute(value, AXES, pairs(lambda y, c, z, x: (y + step, c, z, x)))  14.6 us
    ppermute x9, waiting for transfers between devices, shift_y(): lax.ppermute(value, AXES, pairs(lambda y, c, z, x: (y + step, c, z, x)))  14.4 us
    ppermute x9, waiting for transfers between devices, shift_second(): return lax.ppermute(value, AXES, pairs(move))  12.6 us
    ppermute x9, waiting for transfers between devices, shift_first(): return lax.ppermute(value, AXES, pairs(move))  10.5 us
    pallas_call x1, Pallas kernels, local(): call(functools.partial(attend_body, rows, heads), [shape((rows, heads * H...  5.89 us
    pallas_call x1, Pallas kernels, local(): call(caches_body, [pltpu.VMEM(v.shape, v.dtype) for v in (key_cache, valu...  5.85 us
  transfers between devices with their start and end apart: 33, of which 23 were waited for; matrix products, arithmetic and copies ran while one was open for 1% of the time, Pallas kernels for 12%

profile of v5, /device:TPU:0, one launch (start us, length us, event | category | flops | bytes accessed | tf_op | source)
XLA Modules:
  0.0 122.4 jit_solution(17630115397633206513)
XLA Ops:
  2.4 2.9 %collective-permute-start.3 = (bf16[128,1024]{1,0:T(8,128)(2,1)}, bf16[128,1024]{1,0:T(8,128)(2,1)S(1)}, u32[]{:S(2)}, u32[]{:S(2)}) collective-permute-start(bf16[128,1024]{1,0:T(8,128)(2,1)} %hidden_hbm.1), channel_id=1, source_target_pairs={{0,64},{1,65},{2,66},{3,67},{4,68},{5,69},{6,70},{7,71},{8,72},{9,... | collective-permute-start | bytes 786440 | tf_op jit(solution)/shard_map/ppermute | solution.py:44
  6.6 3.7 %collective-permute-done.back_ref = bf16[128,1024]{1,0:T(8,128)(2,1)S(1)} collective-permute-done((bf16[128,1024]{1,0:T(8,128)(2,1)}, bf16[128,1024]{1,0:T(8,128)(2,1)S(1)}, u32[]{:S(2)}, u32[]{:S(2)}) %collective-permute-start) | collective-permute-done | bytes 262176 | tf_op jit(solution)/shard_map/ppermute | solution.py:44
  10.3 2.5 %load.1 = (bf16[128,1024]{1,0:T(8,128)(2,1)S(1)}, bf16[128,1024]{1,0:T(8,128)(2,1)S(1)}, bf16[1024]{0:T(1024)(128)(2,1)S(1)}, bf16[1024,2048]{1,0:T(8,128)(2,1)S...) custom-call(bf16[128,1024]{1,0:T(8,128)(2,1)S(1)} %collective-permute-done.back_ref, ...), custom_call_target="tpu_custom_call" | custom-call | tf_op jit(solution)/shard_map/load/pallas_call | solution.py:314
  12.9 4.2 %collective-permute-done.3.refs_4_ = bf16[128,1024]{1,0:T(8,128)(2,1)S(1)} collective-permute-done((bf16[128,1024]{1,0:T(8,128)(2,1)}, bf16[128,1024]{1,0:T(8,128)(2,1)S(1)}, u32[]{:S(2)}, u32[]{:S(2)}) %collective-permute-start.3) | collective-permute-done | bytes 262176 | tf_op jit(solution)/shard_map/ppermute | solution.py:44
  19.0 4.3 %project_first.1 = (bf16[2,1168,128]{2,1,0:T(8,128)(2,1)S(1)}, bf16[2,1168,128]{2,1,0:T(8,128)(2,1)S(1)}, bf16[2,1168,128]{2,1,0:T(8,128)(2,1)}, bf16[2,1168,128...) custom-call(bf16[1024]{0:T(1024)(128)(2,1)S(1)} %get-tuple-element.30.gain_ref, ...), custom_call_target="tpu_custom_call" | custom-call | tf_op jit(solution)/shard_map/project_first/pallas_call | solution.py:327
  28.6 2.6 %project_second.1 = (bf16[2,1168,128]{2,1,0:T(8,128)(2,1)S(1)}, bf16[2,1168,128]{2,1,0:T(8,128)(2,1)S(1)}, bf16[2,1168,128]{2,1,0:T(8,128)(2,1)S(1)}, bf16[2,1168,128]{2,1,0:T(8,128)(2,1)S(1)}) custom-call(bf16[16,64,1024]{2,1,0:T(8,128)(2,1)S(1)} %get-tuple-element.36.hs, bf16[16,16,128]{2,1,0:T(8,128)(2,1)S(1)} %get-tuple-element.37.sq, ...), custom_call_target="tpu_custom_call" | custom-call | tf_op jit(solution)/shard_map/project_second/pallas_call | solution.py:336
  31.2 3.3 %collective-permute-done.7.refs_1_ = bf16[2,1168,128]{2,1,0:T(8,128)(2,1)S(1)} collective-permute-done((bf16[2,1168,128]{2,1,0:T(8,128)(2,1)S(1)}, bf16[2,1168,128]{2,1,0:T(8,128)(2,1)S(1)}, u32[]{:S(2)}, u32[]{:S(2)}) %collective-permute-start.7) | collective-permute-done | bytes 598048 | tf_op jit(solution)/shard_map/ppermute | solution.py:51
  35.2 3.0 %collective-permute-start.12 = (bf16[2,1168,128]{2,1,0:T(8,128)(2,1)S(1)}, bf16[2,1168,128]{2,1,0:T(8,128)(2,1)}, u32[]{:S(2)}, u32[]{:S(2)}) collective-permute-start(bf16[2,1168,128]{2,1,0:T(8,128)(2,1)S(1)} %add.81.after_ref), channel_id=1, source_target_pairs={{0,3},{1,0},{2,1},{3,2},{4,7},{5,4},{6,5},{7,6},{8,11},{9,8},{10,9... | collective-permute-start | bytes 1794056 | tf_op jit(solution)/shard_map/ppermute | solution.py:51
  38.4 5.9 %load_caches.1 = (bf16[32,1024,128]{2,1,0:T(8,128)(2,1)S(1)}, bf16[32,1024,128]{2,1,0:T(8,128)(2,1)S(1)}, bf16[16,128]{1,0:T(8,128)(2,1)S(1)}) custom-call(bf16[2,1168,128]{2,1,0:T(8,128)(2,1)S(1)} %add.81.after_ref, bf16[32,1024,128]{2,1,0:T(8,128)(2,1)} %kc_hbm.1, bf16[32,1024,128]{2,1,0:T(8,128)(2,1)} %vc_hbm.1), custom_call_target="tpu_custom_call" | custom-call | tf_op jit(solution)/shard_map/load_caches/pallas_call | solution.py:356
  44.3 3.0 %collective-permute-done.8.refs_2_.p1_ref = bf16[2,1168,128]{2,1,0:T(8,128)(2,1)S(1)} collective-permute-done((bf16[2,1168,128]{2,1,0:T(8,128)(2,1)S(1)}, bf16[2,1168,128]{2,1,0:T(8,128)(2,1)S(1)}, u32[]{:S(2)}, u32[]{:S(2)}) %collective-permute-start.8) | collective-permute-done | bytes 598048 | tf_op jit(solution)/shard_map/ppermute | solution.py:51
  49.3 4.0 %collective-permute-start.13 = (bf16[1,1168,128]{2,1,0:T(8,128)(2,1)S(1)}, bf16[1,1168,128]{2,1,0:T(8,128)(2,1)S(1)}, u32[]{:S(2)}, u32[]{:S(2)}) collective-permute-start(bf16[1,1168,128]{2,1,0:T(8,128)(2,1)S(1)} %get-tuple-element.47), channel_id=1, source_target_pairs={{0,8},{1,9},{2,10},{3,11},{4,12},{5,13},{6,14},{7,15},{8,0},{9,1},... | collective-permute-start | bytes 897032 | tf_op jit(solution)/shard_map/ppermute | solution.py:58
  54.3 2.2 %collective-permute-start.15 = (bf16[1,1168,128]{2,1,0:T(8,128)(2,1)S(1)}, bf16[1,1168,128]{2,1,0:T(8,128)(2,1)S(1)}, u32[]{:S(2)}, u32[]{:S(2)}) collective-permute-start(bf16[1,1168,128]{2,1,0:T(8,128)(2,1)S(1)} %get-tuple-element.49), channel_id=1, source_target_pairs={{0,12},{1,13},{2,14},{3,15},{4,0},{5,1},{6,2},{7,3},{8,4},{9,5},{1... | collective-permute-start | bytes 897032 | tf_op jit(solution)/shard_map/ppermute | solution.py:58
  58.0 3.2 %collective-permute-done.14.r2_ref = bf16[1,1168,128]{2,1,0:T(8,128)(2,1)S(1)} collective-permute-done((bf16[1,1168,128]{2,1,0:T(8,128)(2,1)S(1)}, bf16[1,1168,128]{2,1,0:T(8,128)(2,1)S(1)}, u32[]{:S(2)}, u32[]{:S(2)}) %collective-permute-start.14) | collective-permute-done | bytes 299040 | tf_op jit(solution)/shard_map/ppermute | solution.py:58
  62.2 5.9 %attend.1 = (bf16[64,2048]{1,0:T(8,128)(2,1)S(1)}, bf16[64,128]{1,0:T(8,128)(2,1)}, bf16[64,128]{1,0:T(8,128)(2,1)}) custom-call(s32[32]{0:T(128)S(1)} %copy-done.3, bf16[2,1168,128]{2,1,0:T(8,128)(2,1)S(1)} %get-tuple-element.38.refs_0_.p0_ref, bf16[2,1168,128]{2,1,0:T(8,128)(2,1)S(1)} %collective-permute-done.8.refs_2_.p1_ref, ...), custom_call_target="tpu_custom_call" | custom-call | tf_op jit(solution)/shard_map/attend/pallas_call | solution.py:375
  69.6 2.8 %collective-permute-start.17 = (bf16[64,2048]{1,0:T(8,128)(2,1)S(1)}, bf16[64,2048]{1,0:T(8,128)(2,1)S(1)}, u32[]{:S(2)}, u32[]{:S(2)}) collective-permute-start(bf16[64,2048]{1,0:T(8,128)(2,1)S(1)} %together.1), channel_id=1, source_target_pairs={{0,2},{1,3},{2,0},{3,1},{4,6},{5,7},{6,4},{7,5},{8,10},{9,11},{10,... | collective-permute-start | bytes 786440 | tf_op jit(solution)/shard_map/ppermute | solution.py:51
  73.5 2.2 %collective-permute-start.21 = (bf16[64,2048]{1,0:T(8,128)(2,1)S(1)}, bf16[64,2048]{1,0:T(8,128)(2,1)S(1)}, u32[]{:S(2)}, u32[]{:S(2)}) collective-permute-start(bf16[64,2048]{1,0:T(8,128)(2,1)S(1)} %together.1), channel_id=1, source_target_pairs={{0,3},{1,0},{2,1},{3,2},{4,7},{5,4},{6,5},{7,6},{8,11},{9,8},{10,9... | collective-permute-start | bytes 786440 | tf_op jit(solution)/shard_map/ppermute | solution.py:51
  80.7 2.8 %collective-permute-start.22 = (bf16[128,2048]{1,0:T(8,128)(2,1)S(1)}, bf16[128,2048]{1,0:T(8,128)(2,1)S(1)}, u32[]{:S(2)}, u32[]{:S(2)}) collective-permute-start(bf16[128,2048]{1,0:T(8,128)(2,1)S(1)} %constant_dynamic-update-slice_fusion.b_ref), channel_id=1, source_target_pairs={{0,12},{1,13},{2,14},{3,15},{4,0},{5,1},{6,2},{7,3},{8,4},{9,5},{1... | collective-permute-start | bytes 1572872 | tf_op jit(solution)/shard_map/ppermute | solution.py:58
  83.4 3.2 %collective-permute-start.25 = (bf16[128,2048]{1,0:T(8,128)(2,1)S(1)}, bf16[128,2048]{1,0:T(8,128)(2,1)S(1)}, u32[]{:S(2)}, u32[]{:S(2)}) collective-permute-start(bf16[128,2048]{1,0:T(8,128)(2,1)S(1)} %pad_maximum_fusion.a_ref), channel_id=1, source_target_pairs={{0,12},{1,13},{2,14},{3,15},{4,0},{5,1},{6,2},{7,3},{8,4},{9,5},{1... | collective-permute-start | bytes 1572872 | tf_op jit(solution)/shard_map/ppermute | solution.py:58
  88.1 2.0 %collective-permute-done.22.b_ref = bf16[128,2048]{1,0:T(8,128)(2,1)S(1)} collective-permute-done((bf16[128,2048]{1,0:T(8,128)(2,1)S(1)}, bf16[128,2048]{1,0:T(8,128)(2,1)S(1)}, u32[]{:S(2)}, u32[]{:S(2)}) %collective-permute-start.22) | collective-permute-done | bytes 524320 | tf_op jit(solution)/shard_map/ppermute | solution.py:58
  90.1 3.7 %collective-permute-start.23 = (bf16[128,2048]{1,0:T(8,128)(2,1)S(1)}, bf16[128,2048]{1,0:T(8,128)(2,1)S(1)}, u32[]{:S(2)}, u32[]{:S(2)}) collective-permute-start(bf16[128,2048]{1,0:T(8,128)(2,1)S(1)} %collective-permute-done.22.b_ref), channel_id=1, source_target_pairs={{0,12},{1,13},{2,14},{3,15},{4,0},{5,1},{6,2},{7,3},{8,4},{9,5},{1... | collective-permute-start | bytes 1572872 | tf_op jit(solution)/shard_map/ppermute | solution.py:58
  103.2 2.6 %collective-permute-done.26 = bf16[8,64,1024]{2,1,0:T(8,128)(2,1)S(1)} collective-permute-done((bf16[8,64,1024]{2,1,0:T(8,128)(2,1)S(1)}, bf16[8,64,1024]{2,1,0:T(8,128)(2,1)S(1)}, u32[]{:S(2)}, u32[]{:S(2)}) %collective-permute-start.26) | collective-permute-done | bytes 1048608 | tf_op jit(solution)/shard_map/ppermute | solution.py:40
  107.3 2.4 %collective-permute-start.31 = (bf16[64,1024]{1,0:T(8,128)(2,1)S(1)}, bf16[64,1024]{1,0:T(8,128)(2,1)S(1)}, u32[]{:S(2)}, u32[]{:S(2)}) collective-permute-start(bf16[64,1024]{1,0:T(8,128)(2,1)S(1)} %get-tuple-element.64), channel_id=1, source_target_pairs={{0,96},{1,97},{2,98},{3,99},{4,100},{5,101},{6,102},{7,103},{8,104... | collective-permute-start | bytes 393224 | tf_op jit(solution)/shard_map/ppermute | solution.py:44
  114.5 2.1 %collective-permute-start.28 = (bf16[64,1024]{1,0:T(8,128)(2,1)S(1)}, bf16[64,1024]{1,0:T(8,128)(2,1)S(1)}, u32[]{:S(2)}, u32[]{:S(2)}) collective-permute-start(bf16[64,1024]{1,0:T(8,128)(2,1)S(1)} %get-tuple-element.59), channel_id=1, source_target_pairs={{0,32},{1,33},{2,34},{3,35},{4,36},{5,37},{6,38},{7,39},{8,40},{9,... | collective-permute-start | bytes 393224 | tf_op jit(solution)/shard_map/ppermute | solution.py:44
  117.8 2.9 %collective-permute-done.28 = bf16[64,1024]{1,0:T(8,128)(2,1)S(1)} collective-permute-done((bf16[64,1024]{1,0:T(8,128)(2,1)S(1)}, bf16[64,1024]{1,0:T(8,128)(2,1)S(1)}, u32[]{:S(2)}, u32[]{:S(2)}) %collective-permute-start.28) | collective-permute-done | bytes 131104 | tf_op jit(solution)/shard_map/ppermute | solution.py:44
  (78 shorter events, 44.1 us)
Async XLA Ops:
  0.6 9.7 %collective-permute-start = (bf16[128,1024]{1,0:T(8,128)(2,1)}, bf16[128,1024]{1,0:T(8,128)(2,1)S(1)}, u32[]{:S(2)}, u32[]{:S(2)}) collective-permute-start(bf16[128,1024]{1,0:T(8,128)(2,1)} %hidden_hbm.1), channel_id=1, source_target_pairs={{0,32},{1,33},{2,34},{3,35},{4,36},{5,37},{6,38},{7,39},{8,40},{9,... | collective-permute-start | bytes 786440 | tf_op jit(solution)/shard_map/ppermute | solution.py:44
  2.4 14.7 %collective-permute-start.3 = (bf16[128,1024]{1,0:T(8,128)(2,1)}, bf16[128,1024]{1,0:T(8,128)(2,1)S(1)}, u32[]{:S(2)}, u32[]{:S(2)}) collective-permute-start(bf16[128,1024]{1,0:T(8,128)(2,1)} %hidden_hbm.1), channel_id=1, source_target_pairs={{0,64},{1,65},{2,66},{3,67},{4,68},{5,69},{6,70},{7,71},{8,72},{9,... | collective-permute-start | bytes 786440 | tf_op jit(solution)/shard_map/ppermute | solution.py:44
  5.3 11.9 %collective-permute-start.5 = (bf16[128,1024]{1,0:T(8,128)(2,1)}, bf16[128,1024]{1,0:T(8,128)(2,1)S(1)}, u32[]{:S(2)}, u32[]{:S(2)}) collective-permute-start(bf16[128,1024]{1,0:T(8,128)(2,1)} %hidden_hbm.1), channel_id=1, source_target_pairs={{0,96},{1,97},{2,98},{3,99},{4,100},{5,101},{6,102},{7,103},{8,104... | collective-permute-start | bytes 786440 | tf_op jit(solution)/shard_map/ppermute | solution.py:44
  6.6 11.0 %collective-permute-start.1 = (bf16[128,1024]{1,0:T(8,128)(2,1)}, bf16[128,1024]{1,0:T(8,128)(2,1)S(1)}, u32[]{:S(2)}, u32[]{:S(2)}) collective-permute-start(bf16[128,1024]{1,0:T(8,128)(2,1)} %hidden_hbm.1), channel_id=1, source_target_pairs={{0,16},{1,17},{2,18},{3,19},{4,20},{5,21},{6,22},{7,23},{8,24},{9,... | collective-permute-start | bytes 786440 | tf_op jit(solution)/shard_map/ppermute | solution.py:40
  23.3 11.2 %collective-permute-start.7 = (bf16[2,1168,128]{2,1,0:T(8,128)(2,1)S(1)}, bf16[2,1168,128]{2,1,0:T(8,128)(2,1)S(1)}, u32[]{:S(2)}, u32[]{:S(2)}) collective-permute-start(bf16[2,1168,128]{2,1,0:T(8,128)(2,1)S(1)} %get-tuple-element.40), channel_id=1, source_target_pairs={{0,1},{1,2},{2,3},{3,0},{4,5},{5,6},{6,7},{7,4},{8,9},{9,10},{10,1... | collective-permute-start | bytes 1794056 | tf_op jit(solution)/shard_map/ppermute | solution.py:51
  24.8 10.2 %collective-permute-start.11 = (bf16[2,1168,128]{2,1,0:T(8,128)(2,1)S(1)}, bf16[2,1168,128]{2,1,0:T(8,128)(2,1)S(1)}, u32[]{:S(2)}, u32[]{:S(2)}) collective-permute-start(bf16[2,1168,128]{2,1,0:T(8,128)(2,1)S(1)} %get-tuple-element.45), channel_id=1, source_target_pairs={{0,3},{1,0},{2,1},{3,2},{4,7},{5,4},{6,5},{7,6},{8,11},{9,8},{10,9... | collective-permute-start | bytes 1794056 | tf_op jit(solution)/shard_map/ppermute | solution.py:51
  26.6 17.7 %collective-permute-start.9 = (bf16[2,1168,128]{2,1,0:T(8,128)(2,1)}, bf16[2,1168,128]{2,1,0:T(8,128)(2,1)S(1)}, u32[]{:S(2)}, u32[]{:S(2)}) collective-permute-start(bf16[2,1168,128]{2,1,0:T(8,128)(2,1)} %get-tuple-element.41), channel_id=1, source_target_pairs={{0,3},{1,0},{2,1},{3,2},{4,7},{5,4},{6,5},{7,6},{8,11},{9,8},{10,9... | collective-permute-start | bytes 1794056 | tf_op jit(solution)/shard_map/ppermute | solution.py:51
  28.1 16.2 %collective-permute-start.10 = (bf16[2,1168,128]{2,1,0:T(8,128)(2,1)}, bf16[2,1168,128]{2,1,0:T(8,128)(2,1)}, u32[]{:S(2)}, u32[]{:S(2)}) collective-permute-start(bf16[2,1168,128]{2,1,0:T(8,128)(2,1)} %get-tuple-element.43), channel_id=1, source_target_pairs={{0,1},{1,2},{2,3},{3,0},{4,5},{5,6},{6,7},{7,4},{8,9},{9,10},{10,1... | collective-permute-start | bytes 1794056 | tf_op jit(solution)/shard_map/ppermute | solution.py:51
  34.6 12.7 %collective-permute-start.8 = (bf16[2,1168,128]{2,1,0:T(8,128)(2,1)S(1)}, bf16[2,1168,128]{2,1,0:T(8,128)(2,1)S(1)}, u32[]{:S(2)}, u32[]{:S(2)}) collective-permute-start(bf16[2,1168,128]{2,1,0:T(8,128)(2,1)S(1)} %add.80), channel_id=1, source_target_pairs={{0,1},{1,2},{2,3},{3,0},{4,5},{5,6},{6,7},{7,4},{8,9},{9,10},{10,1... | collective-permute-start | bytes 1794056 | tf_op jit(solution)/shard_map/ppermute | solution.py:51
  35.2 12.5 %collective-permute-start.12 = (bf16[2,1168,128]{2,1,0:T(8,128)(2,1)S(1)}, bf16[2,1168,128]{2,1,0:T(8,128)(2,1)}, u32[]{:S(2)}, u32[]{:S(2)}) collective-permute-start(bf16[2,1168,128]{2,1,0:T(8,128)(2,1)S(1)} %add.81.after_ref), channel_id=1, source_target_pairs={{0,3},{1,0},{2,1},{3,2},{4,7},{5,4},{6,5},{7,6},{8,11},{9,8},{10,9... | collective-permute-start | bytes 1794056 | tf_op jit(solution)/shard_map/ppermute | solution.py:51
  49.3 8.7 %collective-permute-start.13 = (bf16[1,1168,128]{2,1,0:T(8,128)(2,1)S(1)}, bf16[1,1168,128]{2,1,0:T(8,128)(2,1)S(1)}, u32[]{:S(2)}, u32[]{:S(2)}) collective-permute-start(bf16[1,1168,128]{2,1,0:T(8,128)(2,1)S(1)} %get-tuple-element.47), channel_id=1, source_target_pairs={{0,8},{1,9},{2,10},{3,11},{4,12},{5,13},{6,14},{7,15},{8,0},{9,1},... | collective-permute-start | bytes 897032 | tf_op jit(solution)/shard_map/ppermute | solution.py:58
  53.2 8.0 %collective-permute-start.14 = (bf16[1,1168,128]{2,1,0:T(8,128)(2,1)S(1)}, bf16[1,1168,128]{2,1,0:T(8,128)(2,1)S(1)}, u32[]{:S(2)}, u32[]{:S(2)}) collective-permute-start(bf16[1,1168,128]{2,1,0:T(8,128)(2,1)S(1)} %get-tuple-element.48), channel_id=1, source_target_pairs={{0,4},{1,5},{2,6},{3,7},{4,8},{5,9},{6,10},{7,11},{8,12},{9,13},{1... | collective-permute-start | bytes 897032 | tf_op jit(solution)/shard_map/ppermute | solution.py:58
  54.3 7.9 %collective-permute-start.15 = (bf16[1,1168,128]{2,1,0:T(8,128)(2,1)S(1)}, bf16[1,1168,128]{2,1,0:T(8,128)(2,1)S(1)}, u32[]{:S(2)}, u32[]{:S(2)}) collective-permute-start(bf16[1,1168,128]{2,1,0:T(8,128)(2,1)S(1)} %get-tuple-element.49), channel_id=1, source_target_pairs={{0,12},{1,13},{2,14},{3,15},{4,0},{5,1},{6,2},{7,3},{8,4},{9,5},{1... | collective-permute-start | bytes 897032 | tf_op jit(solution)/shard_map/ppermute | solution.py:58
  69.6 8.0 %collective-permute-start.17 = (bf16[64,2048]{1,0:T(8,128)(2,1)S(1)}, bf16[64,2048]{1,0:T(8,128)(2,1)S(1)}, u32[]{:S(2)}, u32[]{:S(2)}) collective-permute-start(bf16[64,2048]{1,0:T(8,128)(2,1)S(1)} %together.1), channel_id=1, source_target_pairs={{0,2},{1,3},{2,0},{3,1},{4,6},{5,7},{6,4},{7,5},{8,10},{9,11},{10,... | collective-permute-start | bytes 786440 | tf_op jit(solution)/shard_map/ppermute | solution.py:51
  72.4 8.0 %collective-permute-start.20 = (bf16[64,2048]{1,0:T(8,128)(2,1)S(1)}, bf16[64,2048]{1,0:T(8,128)(2,1)S(1)}, u32[]{:S(2)}, u32[]{:S(2)}) collective-permute-start(bf16[64,2048]{1,0:T(8,128)(2,1)S(1)} %together.1), channel_id=1, source_target_pairs={{0,1},{1,2},{2,3},{3,0},{4,5},{5,6},{6,7},{7,4},{8,9},{9,10},{10,1... | collective-permute-start | bytes 786440 | tf_op jit(solution)/shard_map/ppermute | solution.py:51
  73.5 7.2 %collective-permute-start.21 = (bf16[64,2048]{1,0:T(8,128)(2,1)S(1)}, bf16[64,2048]{1,0:T(8,128)(2,1)S(1)}, u32[]{:S(2)}, u32[]{:S(2)}) collective-permute-start(bf16[64,2048]{1,0:T(8,128)(2,1)S(1)} %together.1), channel_id=1, source_target_pairs={{0,3},{1,0},{2,1},{3,2},{4,7},{5,4},{6,5},{7,6},{8,11},{9,8},{10,9... | collective-permute-start | bytes 786440 | tf_op jit(solution)/shard_map/ppermute | solution.py:51
  77.6 10.5 %collective-permute-start.18 = (bf16[128,2048]{1,0:T(8,128)(2,1)S(1)}, bf16[128,2048]{1,0:T(8,128)(2,1)S(1)}, u32[]{:S(2)}, u32[]{:S(2)}) collective-permute-start(bf16[128,2048]{1,0:T(8,128)(2,1)S(1)} %pad_maximum_fusion.a_ref), channel_id=1, source_target_pairs={{0,4},{1,5},{2,6},{3,7},{4,8},{5,9},{6,10},{7,11},{8,12},{9,13},{1... | collective-permute-start | bytes 1572872 | tf_op jit(solution)/shard_map/ppermute | solution.py:58
  80.7 9.5 %collective-permute-start.22 = (bf16[128,2048]{1,0:T(8,128)(2,1)S(1)}, bf16[128,2048]{1,0:T(8,128)(2,1)S(1)}, u32[]{:S(2)}, u32[]{:S(2)}) collective-permute-start(bf16[128,2048]{1,0:T(8,128)(2,1)S(1)} %constant_dynamic-update-slice_fusion.b_ref), channel_id=1, source_target_pairs={{0,12},{1,13},{2,14},{3,15},{4,0},{5,1},{6,2},{7,3},{8,4},{9,5},{1... | collective-permute-start | bytes 1572872 | tf_op jit(solution)/shard_map/ppermute | solution.py:58
  83.4 11.7 %collective-permute-start.24 = (bf16[128,2048]{1,0:T(8,128)(2,1)S(1)}, bf16[128,2048]{1,0:T(8,128)(2,1)S(1)}, u32[]{:S(2)}, u32[]{:S(2)}) collective-permute-start(bf16[128,2048]{1,0:T(8,128)(2,1)S(1)} %constant_dynamic-update-slice_fusion.b_ref), channel_id=1, source_target_pairs={{0,4},{1,5},{2,6},{3,7},{4,8},{5,9},{6,10},{7,11},{8,12},{9,13},{1... | collective-permute-start | bytes 1572872 | tf_op jit(solution)/shard_map/ppermute | solution.py:58
  83.4 13.0 %collective-permute-start.25 = (bf16[128,2048]{1,0:T(8,128)(2,1)S(1)}, bf16[128,2048]{1,0:T(8,128)(2,1)S(1)}, u32[]{:S(2)}, u32[]{:S(2)}) collective-permute-start(bf16[128,2048]{1,0:T(8,128)(2,1)S(1)} %pad_maximum_fusion.a_ref), channel_id=1, source_target_pairs={{0,12},{1,13},{2,14},{3,15},{4,0},{5,1},{6,2},{7,3},{8,4},{9,5},{1... | collective-permute-start | bytes 1572872 | tf_op jit(solution)/shard_map/ppermute | solution.py:58
  88.1 11.3 %collective-permute-start.19 = (bf16[128,2048]{1,0:T(8,128)(2,1)S(1)}, bf16[128,2048]{1,0:T(8,128)(2,1)S(1)}, u32[]{:S(2)}, u32[]{:S(2)}) collective-permute-start(bf16[128,2048]{1,0:T(8,128)(2,1)S(1)} %collective-permute-done.18.a_ref), channel_id=1, source_target_pairs={{0,4},{1,5},{2,6},{3,7},{4,8},{5,9},{6,10},{7,11},{8,12},{9,13},{1... | collective-permute-start | bytes 1572872 | tf_op jit(solution)/shard_map/ppermute | solution.py:58
  90.1 11.2 %collective-permute-start.23 = (bf16[128,2048]{1,0:T(8,128)(2,1)S(1)}, bf16[128,2048]{1,0:T(8,128)(2,1)S(1)}, u32[]{:S(2)}, u32[]{:S(2)}) collective-permute-start(bf16[128,2048]{1,0:T(8,128)(2,1)S(1)} %collective-permute-done.22.b_ref), channel_id=1, source_target_pairs={{0,12},{1,13},{2,14},{3,15},{4,0},{5,1},{6,2},{7,3},{8,4},{9,5},{1... | collective-permute-start | bytes 1572872 | tf_op jit(solution)/shard_map/ppermute | solution.py:58
  107.3 7.1 %collective-permute-start.31 = (bf16[64,1024]{1,0:T(8,128)(2,1)S(1)}, bf16[64,1024]{1,0:T(8,128)(2,1)S(1)}, u32[]{:S(2)}, u32[]{:S(2)}) collective-permute-start(bf16[64,1024]{1,0:T(8,128)(2,1)S(1)} %get-tuple-element.64), channel_id=1, source_target_pairs={{0,96},{1,97},{2,98},{3,99},{4,100},{5,101},{6,102},{7,103},{8,104... | collective-permute-start | bytes 393224 | tf_op jit(solution)/shard_map/ppermute | solution.py:44
  109.7 8.1 %collective-permute-start.29 = (bf16[64,1024]{1,0:T(8,128)(2,1)S(1)}, bf16[64,1024]{1,0:T(8,128)(2,1)S(1)}, u32[]{:S(2)}, u32[]{:S(2)}) collective-permute-start(bf16[64,1024]{1,0:T(8,128)(2,1)S(1)} %get-tuple-element.66), channel_id=1, source_target_pairs={{0,96},{1,97},{2,98},{3,99},{4,100},{5,101},{6,102},{7,103},{8,104... | collective-permute-start | bytes 393224 | tf_op jit(solution)/shard_map/ppermute | solution.py:44
  (14 other events, 107.9 us)

commit v6 on v5

--- a/solution.py
+++ b/solution.py
@@ -20,6 +20,7 @@
 F32 = jnp.float32
 MIB = 1024 * 1024
 TOGETHER = 8
+STEP = 64
 LOG2_E = 1.4426950408889634
 
 
@@ -63,7 +64,7 @@
 HSPEC = pl.BlockSpec(memory_space=pltpu.HBM)
 
 
-def call(body, outs, in_specs, name, vmem, scratch=(), flops=0, moved=0):
+def call(body, outs, in_specs, name, vmem, scratch=(), aliases={}):
     return pl.pallas_call(
         body,
         out_shape=outs,
@@ -71,7 +72,8 @@
         out_specs=[VSPEC] * len(outs),
         scratch_shapes=list(scratch),
         compiler_params=pltpu.CompilerParams(vmem_limit_bytes=vmem * MIB),
-        cost_estimate=pl.CostEstimate(flops=flops, bytes_accessed=moved, transcendentals=0),
+        cost_estimate=pl.CostEstimate(flops=0, bytes_accessed=0, transcendentals=0),
+        input_output_aliases=aliases,
         name=name,
     )
 
@@ -135,16 +137,20 @@
     pad = jnp.zeros((HD - rows, HD), F32)
     for i, block in enumerate(blocks):
         for j in range(2):
-            value = block[j * rows : (j + 1) * rows, :].astype(F32)
             dz = (y - i // 2 - z) % 4
             dx = (2 * (c ^ (i % 2)) + j - x) % 4
             e, f = jnp.where(c == 0, dx, dz), jnp.where(c == 0, dz, dx)
             slot = jnp.where(e == 2, f, 12 + f)
             slot = jnp.where(e == 1, jnp.where(f >= 2, 2 + f, 8 + f), slot)
             slot = jnp.where(e == 3, jnp.where(f < 2, 6 + f, 8 + f), slot)
-            hs[slot] = (value * gain).astype(BF16)
-            part = sum(value[:, n : n + HD] * value[:, n : n + HD] for n in range(0, depth, HD))
-            turned = jnp.transpose(jnp.concatenate([part, pad], axis=0))
+            parts = []
+            for top in range(0, rows, 16):
+                value = block[j * rows + top : j * rows + top + 16, :].astype(F32)
+                hs[slot, top : top + 16, :] = (value * gain).astype(BF16)
+                parts.append(
+                    sum(value[:, n : n + HD] * value[:, n : n + HD] for n in range(0, depth, HD))
+                )
+            turned = jnp.transpose(jnp.concatenate(parts + [pad], axis=0))
             total = jnp.broadcast_to(jnp.sum(turned, axis=0, keepdims=True), (8, HD))
             sq[slot] = split_high_low(total)
     project_blocks(rows, heads, 0, hs, sq, wq_ref, wk_ref, wv_ref, outs)
@@ -170,13 +176,21 @@
     ins, outs = refs[: len(refs) - len(terms)], refs[len(refs) - len(terms) :]
     for out, picks in zip(outs, terms):
         for i, pick in enumerate(picks):
-            total = sum(ins[ref][block].astype(F32) for ref, block in pick)
-            out[i, 0:main, :] = total[:main].astype(BF16)
-            out[i, main:, :] = split_high_low(total[main : main + 8] + total[main + 8 :])
+            for top in range(0, main, STEP):
+                total = sum(ins[ref][block, top : top + STEP, :].astype(F32) for ref, block in pick)
+                out[i, top : top + STEP, :] = total.astype(BF16)
+            total = sum(ins[ref][block, main:, :].astype(F32) for ref, block in pick)
+            out[i, main:, :] = split_high_low(total[:8] + total[8:])
+
+
+def early_sum_body(picks, *refs):
+    ins, outs = refs[:4], refs[4:]
+    for (out, at), pick in zip(((outs[0], 0), (outs[1], 0), (outs[1], 1), (outs[1], 2)), picks):
+        out[at] = sum(ins[ref][block].astype(F32) for ref, block in pick)
 
 
 def attend_body(
-    rows, heads, len_ref, p0_ref, p1_ref, p2_ref, r1_ref, r2_ref, r3_ref,
+    rows, heads, len_ref, p0_ref, p1_ref, r1_ref, r2_ref, r3_ref,
     cos_ref, sin_ref, kbuf, vbuf,
     ctx_ref, nk_ref, nv_ref, qs, os, kf, vf,
 ):
@@ -185,7 +199,7 @@
     main = (heads + 2) * rows
 
     def total(lo, hi):
-        refs = (p0_ref, p1_ref, p2_ref, r1_ref, r2_ref, r3_ref)
+        refs = (p0_ref, p1_ref, r1_ref, r2_ref, r3_ref)
         return sum(ref[0, lo:hi, :].astype(F32) for ref in refs)
 
     square = total(main, main + 16)
@@ -272,24 +286,32 @@
         out_ref[:, cols] = jnp.dot(lhs, w_ref[:, cols], preferred_element_type=F32).astype(BF16)
 
 
-def output_last_body(rows, a_ref, b_ref, w_ref, y0_ref, y1_ref, y3_ref, mine_ref, theirs_ref, y2):
+def arrange(rows, f, source, mine_ref, theirs_ref):
     y, c, z, x = place()
+    for place_of, e in enumerate((0, 2, 1, 3)):
+        zz = jnp.where(c == 0, z - f, z - e) % 4
+        xx = jnp.where(c == 0, x - e, x - f) % 4
+        slot = 2 * ((zz - y) % 4) + xx % 2
+        top = place_of * rows
+        own = xx // 2 == c
+
+        @pl.when(own)
+        def _(slot=slot, top=top):
+            mine_ref[slot] = source[top : top + rows, :]
+
+        @pl.when(jnp.logical_not(own))
+        def _(slot=slot, top=top):
+            theirs_ref[slot] = source[top : top + rows, :]
+
+
+def arrange_body(rows, y0_ref, y1_ref, y3_ref, mine_ref, theirs_ref):
+    for f, source in ((0, y0_ref), (1, y1_ref), (3, y3_ref)):
+        arrange(rows, f, source, mine_ref, theirs_ref)
+
+
+def output_last_body(rows, a_ref, b_ref, w_ref, mine_in, theirs_in, mine_ref, theirs_ref, y2):
     output_body(a_ref, b_ref, w_ref, y2)
-    for f, source in enumerate((y0_ref, y1_ref, y2, y3_ref)):
-        for place_of, e in enumerate((0, 2, 1, 3)):
-            zz = jnp.where(c == 0, z - f, z - e) % 4
-            xx = jnp.where(c == 0, x - e, x - f) % 4
-            slot = 2 * ((zz - y) % 4) + xx % 2
-            top = place_of * rows
-            own = xx // 2 == c
-
-            @pl.when(own)
-            def _(slot=slot, source=source, top=top):
-                mine_ref[slot] = source[top : top + rows, :]
-
-            @pl.when(jnp.logical_not(own))
-            def _(slot=slot, source=source, top=top):
-                theirs_ref[slot] = source[top : top + rows, :]
+    arrange(rows, 2, y2, mine_ref, theirs_ref)
 
 
 def local(hidden, gain, w_query, w_key, w_value, w_out, key_cache, value_cache, lengths):
@@ -361,21 +383,25 @@
         4,
         scratch=[pltpu.SemaphoreType.DMA((2,))],
     )(sum_three, in_hbm(key_cache), in_hbm(value_cache))
-    terms = [
-        [[(1, 0), (4, 0), (5, 0)]],
-        [[(0, 1), (2, 1), (3, 1)]],
-        [[(1, 1), (4, 1), (5, 1)]],
-    ]
-    two, one, three = add(
-        terms, own_a, own_b, from_one_a, from_three_a, from_one_b, from_three_b, token
-    )
+    early, early_rest = call(
+        functools.partial(
+            early_sum_body,
+            [[(0, 0), (3, 0)], [(0, 1), (3, 1)], [(1, 0), (2, 0)], [(1, 1), (2, 1)]],
+        ),
+        [shape((1, length, HD), F32), shape((3, length, HD), F32)],
+        [VSPEC] * 4,
+        "early_sum",
+        8,
+    )(own_a, own_b, from_one_b, from_three_a)
+    terms = [[[(0, 1), (2, 0)]], [[(0, 0), (1, 1)]], [[(0, 2), (2, 1)]]]
+    two, one, three = add(terms, early_rest, from_one_a, from_three_b, token)
     arrived = [shift_second(two, 2), shift_second(one, 1), shift_second(three, 3)]
-    parts = [own_a, from_one_a, from_three_a] + arrived
+    parts = [early, from_one_a] + arrived
 
     context, fresh_keys, fresh_values = call(
         functools.partial(attend_body, rows, heads),
         [shape((rows, heads * HD)), shape((rows, HD)), shape((rows, HD))],
-        [SSPEC] + [VSPEC] * 10,
+        [SSPEC] + [VSPEC] * 9,
         "attend",
         10,
         scratch=[
@@ -408,21 +434,21 @@
             8,
         )(a, b, w_out)[0]
 
-    mine, theirs = call(
-        functools.partial(output_last_body, rows),
-        [shape((8, rows, width)), shape((8, rows, width))],
-        [VSPEC] * 6,
-        "project_out_last",
-        12,
-        scratch=[pltpu.VMEM((4 * rows, width), BF16)],
-    )(
-        two_low,
-        two_high,
-        w_out,
+    arranged = [shape((8, rows, width)), shape((8, rows, width))]
+    near = call(functools.partial(arrange_body, rows), arranged, [VSPEC] * 3, "arrange", 8)(
         project_out(low, high),
         project_out(one_low, one_high),
         project_out(three_low, three_high),
     )
+    mine, theirs = call(
+        functools.partial(output_last_body, rows),
+        arranged,
+        [VSPEC] * 5,
+        "project_out_last",
+        12,
+        scratch=[pltpu.VMEM((4 * rows, width), BF16)],
+        aliases={3: 0, 4: 1},
+    )(two_low, two_high, w_out, *near)
     both = mine.astype(F32) + swap_core(theirs).astype(F32)
     over_a, over_b = shift_y(both[4].astype(BF16), 1), shift_y(both[5].astype(BF16), 3)
     from_one_b, from_three_a = shift_y(both[3].astype(BF16), 1), shift_y(both[6].astype(BF16), 3)

time: 123 us -> 122 us (level)
  waiting for transfers between devices: 42.9 us -> 41 us
    ppermute x9, waiting for transfers between devices: 10.5 us -> 8.92 us  [shift_first(): return lax.ppermute(value, AXES, pairs(move))]
  transfers between devices with their start and end apart: 33 -> 33, of which waited for: 23 -> 23; matrix products, arithmetic and copies ran while one was open for 1% -> 0% of each run, Pallas kernels for 12% -> 13%
where the time goes in v6:
time: 122 us; the launch traced here: 121 us
  starting transfers between devices  49.2 us (40%)
  waiting for transfers between devices  41 us (34%)
  Pallas kernels  28.1 us (23%)
  other arithmetic  1.81 us (1%)
    ppermute x9, starting transfers between devices, shift_second(): return lax.ppermute(value, AXES, pairs(move))  18 us
    ppermute x9, starting transfers between devices, shift_first(): return lax.ppermute(value, AXES, pairs(move))  15.9 us
    ppermute x9, starting transfers between devices, shift_y(): lax.ppermute(value, AXES, pairs(lambda y, c, z, x: (y + step, c, z, x)))  14.6 us
    ppermute x9, waiting for transfers between devices, shift_y(): lax.ppermute(value, AXES, pairs(lambda y, c, z, x: (y + step, c, z, x)))  14.4 us
    ppermute x9, waiting for transfers between devices, shift_second(): return lax.ppermute(value, AXES, pairs(move))  12.3 us
    ppermute x9, waiting for transfers between devices, shift_first(): return lax.ppermute(value, AXES, pairs(move))  8.92 us
    pallas_call x1, Pallas kernels, local(): call(caches_body, [pltpu.VMEM(v.shape, v.dtype) for v in (key_cache, valu...  5.88 us
    pallas_call x1, Pallas kernels, local(): call(functools.partial(attend_body, rows, heads), [shape((rows, heads * H...  5.8 us
  transfers between devices with their start and end apart: 33, of which 23 were waited for; matrix products, arithmetic and copies ran while one was open for 0% of the time, Pallas kernels for 13%

profile of v6, /device:TPU:0, one launch (start us, length us, event | category | flops | bytes accessed | tf_op | source)
XLA Modules:
  0.0 121.4 jit_solution(13719089522237691178)
XLA Ops:
  2.4 2.9 %collective-permute-start.3 = (bf16[128,1024]{1,0:T(8,128)(2,1)}, bf16[128,1024]{1,0:T(8,128)(2,1)S(1)}, u32[]{:S(2)}, u32[]{:S(2)}) collective-permute-start(bf16[128,1024]{1,0:T(8,128)(2,1)} %hidden_hbm.1), channel_id=1, source_target_pairs={{0,64},{1,65},{2,66},{3,67},{4,68},{5,69},{6,70},{7,71},{8,72},{9,... | collective-permute-start | bytes 786440 | tf_op jit(solution)/shard_map/ppermute | solution.py:45
  6.6 3.7 %collective-permute-done.back_ref = bf16[128,1024]{1,0:T(8,128)(2,1)S(1)} collective-permute-done((bf16[128,1024]{1,0:T(8,128)(2,1)}, bf16[128,1024]{1,0:T(8,128)(2,1)S(1)}, u32[]{:S(2)}, u32[]{:S(2)}) %collective-permute-start) | collective-permute-done | bytes 262176 | tf_op jit(solution)/shard_map/ppermute | solution.py:45
  10.3 2.5 %load.1 = (bf16[128,1024]{1,0:T(8,128)(2,1)S(1)}, bf16[128,1024]{1,0:T(8,128)(2,1)S(1)}, bf16[1024]{0:T(1024)(128)(2,1)S(1)}, bf16[1024,2048]{1,0:T(8,128)(2,1)S...) custom-call(bf16[128,1024]{1,0:T(8,128)(2,1)S(1)} %collective-permute-done.back_ref, ...), custom_call_target="tpu_custom_call" | custom-call | tf_op jit(solution)/shard_map/load/pallas_call | solution.py:336
  12.9 4.2 %collective-permute-done.3.refs_4_ = bf16[128,1024]{1,0:T(8,128)(2,1)S(1)} collective-permute-done((bf16[128,1024]{1,0:T(8,128)(2,1)}, bf16[128,1024]{1,0:T(8,128)(2,1)S(1)}, u32[]{:S(2)}, u32[]{:S(2)}) %collective-permute-start.3) | collective-permute-done | bytes 262176 | tf_op jit(solution)/shard_map/ppermute | solution.py:45
  19.0 4.1 %project_first.1 = (bf16[2,1168,128]{2,1,0:T(8,128)(2,1)S(1)}, bf16[2,1168,128]{2,1,0:T(8,128)(2,1)S(1)}, bf16[2,1168,128]{2,1,0:T(8,128)(2,1)}, bf16[2,1168,128...) custom-call(bf16[1024]{0:T(1024)(128)(2,1)S(1)} %get-tuple-element.34.gain_ref, ...), custom_call_target="tpu_custom_call" | custom-call | tf_op jit(solution)/shard_map/project_first/pallas_call | solution.py:349
  26.7 3.0 %collective-permute-start.8 = (bf16[2,1168,128]{2,1,0:T(8,128)(2,1)}, bf16[2,1168,128]{2,1,0:T(8,128)(2,1)S(1)}, u32[]{:S(2)}, u32[]{:S(2)}) collective-permute-start(bf16[2,1168,128]{2,1,0:T(8,128)(2,1)} %get-tuple-element.45), channel_id=1, source_target_pairs={{0,3},{1,0},{2,1},{3,2},{4,7},{5,4},{6,5},{7,6},{8,11},{9,8},{10,9... | collective-permute-start | bytes 1794056 | tf_op jit(solution)/shard_map/ppermute | solution.py:52
  29.6 2.6 %project_second.1 = (bf16[2,1168,128]{2,1,0:T(8,128)(2,1)S(1)}, bf16[2,1168,128]{2,1,0:T(8,128)(2,1)S(1)}, bf16[2,1168,128]{2,1,0:T(8,128)(2,1)S(1)}, bf16[2,1168,128]{2,1,0:T(8,128)(2,1)S(1)}) custom-call(bf16[16,64,1024]{2,1,0:T(8,128)(2,1)S(1)} %get-tuple-element.40.hs, bf16[16,16,128]{2,1,0:T(8,128)(2,1)S(1)} %get-tuple-element.41.sq, ...), custom_call_target="tpu_custom_call" | custom-call | tf_op jit(solution)/shard_map/project_second/pallas_call | solution.py:358
  32.3 2.0 %collective-permute-done.9.refs_1_ = bf16[2,1168,128]{2,1,0:T(8,128)(2,1)S(1)} collective-permute-done((bf16[2,1168,128]{2,1,0:T(8,128)(2,1)S(1)}, bf16[2,1168,128]{2,1,0:T(8,128)(2,1)S(1)}, u32[]{:S(2)}, u32[]{:S(2)}) %collective-permute-start.9) | collective-permute-done | bytes 598048 | tf_op jit(solution)/shard_map/ppermute | solution.py:52
  35.0 3.0 %collective-permute-start.12 = (bf16[2,1168,128]{2,1,0:T(8,128)(2,1)S(1)}, bf16[2,1168,128]{2,1,0:T(8,128)(2,1)}, u32[]{:S(2)}, u32[]{:S(2)}) collective-permute-start(bf16[2,1168,128]{2,1,0:T(8,128)(2,1)S(1)} %add.81.after_ref), channel_id=1, source_target_pairs={{0,3},{1,0},{2,1},{3,2},{4,7},{5,4},{6,5},{7,6},{8,11},{9,8},{10,9... | collective-permute-start | bytes 1794056 | tf_op jit(solution)/shard_map/ppermute | solution.py:52
  38.2 5.9 %load_caches.1 = (bf16[32,1024,128]{2,1,0:T(8,128)(2,1)S(1)}, bf16[32,1024,128]{2,1,0:T(8,128)(2,1)S(1)}, bf16[16,128]{1,0:T(8,128)(2,1)S(1)}) custom-call(bf16[2,1168,128]{2,1,0:T(8,128)(2,1)S(1)} %add.81.after_ref, bf16[32,1024,128]{2,1,0:T(8,128)(2,1)} %kc_hbm.1, bf16[32,1024,128]{2,1,0:T(8,128)(2,1)} %vc_hbm.1), custom_call_target="tpu_custom_call" | custom-call | tf_op jit(solution)/shard_map/load_caches/pallas_call | solution.py:378
  44.5 2.7 %collective-permute-done.10.refs_1_.p1_ref = bf16[2,1168,128]{2,1,0:T(8,128)(2,1)S(1)} collective-permute-done((bf16[2,1168,128]{2,1,0:T(8,128)(2,1)S(1)}, bf16[2,1168,128]{2,1,0:T(8,128)(2,1)S(1)}, u32[]{:S(2)}, u32[]{:S(2)}) %collective-permute-start.10) | collective-permute-done | bytes 598048 | tf_op jit(solution)/shard_map/ppermute | solution.py:52
  48.8 4.0 %collective-permute-start.13 = (bf16[1,1168,128]{2,1,0:T(8,128)(2,1)S(1)}, bf16[1,1168,128]{2,1,0:T(8,128)(2,1)S(1)}, u32[]{:S(2)}, u32[]{:S(2)}) collective-permute-start(bf16[1,1168,128]{2,1,0:T(8,128)(2,1)S(1)} %get-tuple-element.53), channel_id=1, source_target_pairs={{0,8},{1,9},{2,10},{3,11},{4,12},{5,13},{6,14},{7,15},{8,0},{9,1},... | collective-permute-start | bytes 897032 | tf_op jit(solution)/shard_map/ppermute | solution.py:59
  53.7 2.2 %collective-permute-start.15 = (bf16[1,1168,128]{2,1,0:T(8,128)(2,1)S(1)}, bf16[1,1168,128]{2,1,0:T(8,128)(2,1)S(1)}, u32[]{:S(2)}, u32[]{:S(2)}) collective-permute-start(bf16[1,1168,128]{2,1,0:T(8,128)(2,1)S(1)} %get-tuple-element.55), channel_id=1, source_target_pairs={{0,12},{1,13},{2,14},{3,15},{4,0},{5,1},{6,2},{7,3},{8,4},{9,5},{1... | collective-permute-start | bytes 897032 | tf_op jit(solution)/shard_map/ppermute | solution.py:59
  57.5 3.2 %collective-permute-done.14.r2_ref = bf16[1,1168,128]{2,1,0:T(8,128)(2,1)S(1)} collective-permute-done((bf16[1,1168,128]{2,1,0:T(8,128)(2,1)S(1)}, bf16[1,1168,128]{2,1,0:T(8,128)(2,1)S(1)}, u32[]{:S(2)}, u32[]{:S(2)}) %collective-permute-start.14) | collective-permute-done | bytes 299040 | tf_op jit(solution)/shard_map/ppermute | solution.py:59
  61.7 5.8 %attend.1 = (bf16[64,2048]{1,0:T(8,128)(2,1)S(1)}, bf16[64,128]{1,0:T(8,128)(2,1)}, bf16[64,128]{1,0:T(8,128)(2,1)}) custom-call(s32[32]{0:T(128)S(1)} %copy-done.5, f32[1,1168,128]{2,1,0:T(8,128)S(1)} %get-tuple-element.46.p0_ref, bf16[2,1168,128]{2,1,0:T(8,128)(2,1)S(1)} %collective-permute-done.10.refs_1_.p1_ref, ...), custom_call_target="tpu_custom_call" | custom-call | tf_op jit(solution)/shard_map/attend/pallas_call | solution.py:401
  69.0 2.8 %collective-permute-start.17 = (bf16[64,2048]{1,0:T(8,128)(2,1)S(1)}, bf16[64,2048]{1,0:T(8,128)(2,1)S(1)}, u32[]{:S(2)}, u32[]{:S(2)}) collective-permute-start(bf16[64,2048]{1,0:T(8,128)(2,1)S(1)} %together.1), channel_id=1, source_target_pairs={{0,2},{1,3},{2,0},{3,1},{4,6},{5,7},{6,4},{7,5},{8,10},{9,11},{10,... | collective-permute-start | bytes 786440 | tf_op jit(solution)/shard_map/ppermute | solution.py:52
  72.9 2.2 %collective-permute-start.21 = (bf16[64,2048]{1,0:T(8,128)(2,1)S(1)}, bf16[64,2048]{1,0:T(8,128)(2,1)S(1)}, u32[]{:S(2)}, u32[]{:S(2)}) collective-permute-start(bf16[64,2048]{1,0:T(8,128)(2,1)S(1)} %together.1), channel_id=1, source_target_pairs={{0,3},{1,0},{2,1},{3,2},{4,7},{5,4},{6,5},{7,6},{8,11},{9,8},{10,9... | collective-permute-start | bytes 786440 | tf_op jit(solution)/shard_map/ppermute | solution.py:52
  80.0 2.7 %collective-permute-start.22 = (bf16[128,2048]{1,0:T(8,128)(2,1)S(1)}, bf16[128,2048]{1,0:T(8,128)(2,1)S(1)}, u32[]{:S(2)}, u32[]{:S(2)}) collective-permute-start(bf16[128,2048]{1,0:T(8,128)(2,1)S(1)} %constant_dynamic-update-slice_fusion.b_ref), channel_id=1, source_target_pairs={{0,12},{1,13},{2,14},{3,15},{4,0},{5,1},{6,2},{7,3},{8,4},{9,5},{1... | collective-permute-start | bytes 1572872 | tf_op jit(solution)/shard_map/ppermute | solution.py:59
  82.8 3.2 %collective-permute-start.25 = (bf16[128,2048]{1,0:T(8,128)(2,1)S(1)}, bf16[128,2048]{1,0:T(8,128)(2,1)S(1)}, u32[]{:S(2)}, u32[]{:S(2)}) collective-permute-start(bf16[128,2048]{1,0:T(8,128)(2,1)S(1)} %pad_maximum_fusion.a_ref), channel_id=1, source_target_pairs={{0,12},{1,13},{2,14},{3,15},{4,0},{5,1},{6,2},{7,3},{8,4},{9,5},{1... | collective-permute-start | bytes 1572872 | tf_op jit(solution)/shard_map/ppermute | solution.py:59
  89.5 3.7 %collective-permute-start.23 = (bf16[128,2048]{1,0:T(8,128)(2,1)S(1)}, bf16[128,2048]{1,0:T(8,128)(2,1)S(1)}, u32[]{:S(2)}, u32[]{:S(2)}) collective-permute-start(bf16[128,2048]{1,0:T(8,128)(2,1)S(1)} %collective-permute-done.22.b_ref), channel_id=1, source_target_pairs={{0,12},{1,13},{2,14},{3,15},{4,0},{5,1},{6,2},{7,3},{8,4},{9,5},{1... | collective-permute-start | bytes 1572872 | tf_op jit(solution)/shard_map/ppermute | solution.py:59
  102.2 2.6 %collective-permute-done.26 = bf16[8,64,1024]{2,1,0:T(8,128)(2,1)S(1)} collective-permute-done((bf16[8,64,1024]{2,1,0:T(8,128)(2,1)S(1)}, bf16[8,64,1024]{2,1,0:T(8,128)(2,1)S(1)}, u32[]{:S(2)}, u32[]{:S(2)}) %collective-permute-start.26) | collective-permute-done | bytes 1048608 | tf_op jit(solution)/shard_map/ppermute | solution.py:41
  106.3 2.4 %collective-permute-start.31 = (bf16[64,1024]{1,0:T(8,128)(2,1)S(1)}, bf16[64,1024]{1,0:T(8,128)(2,1)S(1)}, u32[]{:S(2)}, u32[]{:S(2)}) collective-permute-start(bf16[64,1024]{1,0:T(8,128)(2,1)S(1)} %get-tuple-element.72), channel_id=1, source_target_pairs={{0,96},{1,97},{2,98},{3,99},{4,100},{5,101},{6,102},{7,103},{8,104... | collective-permute-start | bytes 393224 | tf_op jit(solution)/shard_map/ppermute | solution.py:45
  113.4 2.1 %collective-permute-start.28 = (bf16[64,1024]{1,0:T(8,128)(2,1)S(1)}, bf16[64,1024]{1,0:T(8,128)(2,1)S(1)}, u32[]{:S(2)}, u32[]{:S(2)}) collective-permute-start(bf16[64,1024]{1,0:T(8,128)(2,1)S(1)} %get-tuple-element.67), channel_id=1, source_target_pairs={{0,32},{1,33},{2,34},{3,35},{4,36},{5,37},{6,38},{7,39},{8,40},{9,... | collective-permute-start | bytes 393224 | tf_op jit(solution)/shard_map/ppermute | solution.py:45
  116.8 2.9 %collective-permute-done.28 = bf16[64,1024]{1,0:T(8,128)(2,1)S(1)} collective-permute-done((bf16[64,1024]{1,0:T(8,128)(2,1)S(1)}, bf16[64,1024]{1,0:T(8,128)(2,1)S(1)}, u32[]{:S(2)}, u32[]{:S(2)}) %collective-permute-start.28) | collective-permute-done | bytes 131104 | tf_op jit(solution)/shard_map/ppermute | solution.py:45
  (84 shorter events, 44.0 us)
Async XLA Ops:
  0.6 9.7 %collective-permute-start = (bf16[128,1024]{1,0:T(8,128)(2,1)}, bf16[128,1024]{1,0:T(8,128)(2,1)S(1)}, u32[]{:S(2)}, u32[]{:S(2)}) collective-permute-start(bf16[128,1024]{1,0:T(8,128)(2,1)} %hidden_hbm.1), channel_id=1, source_target_pairs={{0,32},{1,33},{2,34},{3,35},{4,36},{5,37},{6,38},{7,39},{8,40},{9,... | collective-permute-start | bytes 786440 | tf_op jit(solution)/shard_map/ppermute | solution.py:45
  2.4 14.7 %collective-permute-start.3 = (bf16[128,1024]{1,0:T(8,128)(2,1)}, bf16[128,1024]{1,0:T(8,128)(2,1)S(1)}, u32[]{:S(2)}, u32[]{:S(2)}) collective-permute-start(bf16[128,1024]{1,0:T(8,128)(2,1)} %hidden_hbm.1), channel_id=1, source_target_pairs={{0,64},{1,65},{2,66},{3,67},{4,68},{5,69},{6,70},{7,71},{8,72},{9,... | collective-permute-start | bytes 786440 | tf_op jit(solution)/shard_map/ppermute | solution.py:45
  5.3 11.9 %collective-permute-start.5 = (bf16[128,1024]{1,0:T(8,128)(2,1)}, bf16[128,1024]{1,0:T(8,128)(2,1)S(1)}, u32[]{:S(2)}, u32[]{:S(2)}) collective-permute-start(bf16[128,1024]{1,0:T(8,128)(2,1)} %hidden_hbm.1), channel_id=1, source_target_pairs={{0,96},{1,97},{2,98},{3,99},{4,100},{5,101},{6,102},{7,103},{8,104... | collective-permute-start | bytes 786440 | tf_op jit(solution)/shard_map/ppermute | solution.py:45
  6.6 11.0 %collective-permute-start.1 = (bf16[128,1024]{1,0:T(8,128)(2,1)}, bf16[128,1024]{1,0:T(8,128)(2,1)S(1)}, u32[]{:S(2)}, u32[]{:S(2)}) collective-permute-start(bf16[128,1024]{1,0:T(8,128)(2,1)} %hidden_hbm.1), channel_id=1, source_target_pairs={{0,16},{1,17},{2,18},{3,19},{4,20},{5,21},{6,22},{7,23},{8,24},{9,... | collective-permute-start | bytes 786440 | tf_op jit(solution)/shard_map/ppermute | solution.py:41
  23.1 11.2 %collective-permute-start.9 = (bf16[2,1168,128]{2,1,0:T(8,128)(2,1)S(1)}, bf16[2,1168,128]{2,1,0:T(8,128)(2,1)S(1)}, u32[]{:S(2)}, u32[]{:S(2)}) collective-permute-start(bf16[2,1168,128]{2,1,0:T(8,128)(2,1)S(1)} %get-tuple-element.48), channel_id=1, source_target_pairs={{0,1},{1,2},{2,3},{3,0},{4,5},{5,6},{6,7},{7,4},{8,9},{9,10},{10,1... | collective-permute-start | bytes 1794056 | tf_op jit(solution)/shard_map/ppermute | solution.py:52
  24.6 10.2 %collective-permute-start.11 = (bf16[2,1168,128]{2,1,0:T(8,128)(2,1)S(1)}, bf16[2,1168,128]{2,1,0:T(8,128)(2,1)S(1)}, u32[]{:S(2)}, u32[]{:S(2)}) collective-permute-start(bf16[2,1168,128]{2,1,0:T(8,128)(2,1)S(1)} %get-tuple-element.51), channel_id=1, source_target_pairs={{0,3},{1,0},{2,1},{3,2},{4,7},{5,4},{6,5},{7,6},{8,11},{9,8},{10,9... | collective-permute-start | bytes 1794056 | tf_op jit(solution)/shard_map/ppermute | solution.py:52
  26.4 17.7 %collective-permute-start.7 = (bf16[2,1168,128]{2,1,0:T(8,128)(2,1)}, bf16[2,1168,128]{2,1,0:T(8,128)(2,1)S(1)}, u32[]{:S(2)}, u32[]{:S(2)}) collective-permute-start(bf16[2,1168,128]{2,1,0:T(8,128)(2,1)} %get-tuple-element.44), channel_id=1, source_target_pairs={{0,1},{1,2},{2,3},{3,0},{4,5},{5,6},{6,7},{7,4},{8,9},{9,10},{10,1... | collective-permute-start | bytes 1794056 | tf_op jit(solution)/shard_map/ppermute | solution.py:52
  26.7 17.5 %collective-permute-start.8 = (bf16[2,1168,128]{2,1,0:T(8,128)(2,1)}, bf16[2,1168,128]{2,1,0:T(8,128)(2,1)S(1)}, u32[]{:S(2)}, u32[]{:S(2)}) collective-permute-start(bf16[2,1168,128]{2,1,0:T(8,128)(2,1)} %get-tuple-element.45), channel_id=1, source_target_pairs={{0,3},{1,0},{2,1},{3,2},{4,7},{5,4},{6,5},{7,6},{8,11},{9,8},{10,9... | collective-permute-start | bytes 1794056 | tf_op jit(solution)/shard_map/ppermute | solution.py:52
  34.5 12.7 %collective-permute-start.10 = (bf16[2,1168,128]{2,1,0:T(8,128)(2,1)S(1)}, bf16[2,1168,128]{2,1,0:T(8,128)(2,1)S(1)}, u32[]{:S(2)}, u32[]{:S(2)}) collective-permute-start(bf16[2,1168,128]{2,1,0:T(8,128)(2,1)S(1)} %add.80), channel_id=1, source_target_pairs={{0,1},{1,2},{2,3},{3,0},{4,5},{5,6},{6,7},{7,4},{8,9},{9,10},{10,1... | collective-permute-start | bytes 1794056 | tf_op jit(solution)/shard_map/ppermute | solution.py:52
  35.0 12.5 %collective-permute-start.12 = (bf16[2,1168,128]{2,1,0:T(8,128)(2,1)S(1)}, bf16[2,1168,128]{2,1,0:T(8,128)(2,1)}, u32[]{:S(2)}, u32[]{:S(2)}) collective-permute-start(bf16[2,1168,128]{2,1,0:T(8,128)(2,1)S(1)} %add.81.after_ref), channel_id=1, source_target_pairs={{0,3},{1,0},{2,1},{3,2},{4,7},{5,4},{6,5},{7,6},{8,11},{9,8},{10,9... | collective-permute-start | bytes 1794056 | tf_op jit(solution)/shard_map/ppermute | solution.py:52
  48.8 8.7 %collective-permute-start.13 = (bf16[1,1168,128]{2,1,0:T(8,128)(2,1)S(1)}, bf16[1,1168,128]{2,1,0:T(8,128)(2,1)S(1)}, u32[]{:S(2)}, u32[]{:S(2)}) collective-permute-start(bf16[1,1168,128]{2,1,0:T(8,128)(2,1)S(1)} %get-tuple-element.53), channel_id=1, source_target_pairs={{0,8},{1,9},{2,10},{3,11},{4,12},{5,13},{6,14},{7,15},{8,0},{9,1},... | collective-permute-start | bytes 897032 | tf_op jit(solution)/shard_map/ppermute | solution.py:59
  52.7 8.0 %collective-permute-start.14 = (bf16[1,1168,128]{2,1,0:T(8,128)(2,1)S(1)}, bf16[1,1168,128]{2,1,0:T(8,128)(2,1)S(1)}, u32[]{:S(2)}, u32[]{:S(2)}) collective-permute-start(bf16[1,1168,128]{2,1,0:T(8,128)(2,1)S(1)} %get-tuple-element.54), channel_id=1, source_target_pairs={{0,4},{1,5},{2,6},{3,7},{4,8},{5,9},{6,10},{7,11},{8,12},{9,13},{1... | collective-permute-start | bytes 897032 | tf_op jit(solution)/shard_map/ppermute | solution.py:59
  53.7 7.9 %collective-permute-start.15 = (bf16[1,1168,128]{2,1,0:T(8,128)(2,1)S(1)}, bf16[1,1168,128]{2,1,0:T(8,128)(2,1)S(1)}, u32[]{:S(2)}, u32[]{:S(2)}) collective-permute-start(bf16[1,1168,128]{2,1,0:T(8,128)(2,1)S(1)} %get-tuple-element.55), channel_id=1, source_target_pairs={{0,12},{1,13},{2,14},{3,15},{4,0},{5,1},{6,2},{7,3},{8,4},{9,5},{1... | collective-permute-start | bytes 897032 | tf_op jit(solution)/shard_map/ppermute | solution.py:59
  69.0 8.0 %collective-permute-start.17 = (bf16[64,2048]{1,0:T(8,128)(2,1)S(1)}, bf16[64,2048]{1,0:T(8,128)(2,1)S(1)}, u32[]{:S(2)}, u32[]{:S(2)}) collective-permute-start(bf16[64,2048]{1,0:T(8,128)(2,1)S(1)} %together.1), channel_id=1, source_target_pairs={{0,2},{1,3},{2,0},{3,1},{4,6},{5,7},{6,4},{7,5},{8,10},{9,11},{10,... | collective-permute-start | bytes 786440 | tf_op jit(solution)/shard_map/ppermute | solution.py:52
  71.8 8.0 %collective-permute-start.20 = (bf16[64,2048]{1,0:T(8,128)(2,1)S(1)}, bf16[64,2048]{1,0:T(8,128)(2,1)S(1)}, u32[]{:S(2)}, u32[]{:S(2)}) collective-permute-start(bf16[64,2048]{1,0:T(8,128)(2,1)S(1)} %together.1), channel_id=1, source_target_pairs={{0,1},{1,2},{2,3},{3,0},{4,5},{5,6},{6,7},{7,4},{8,9},{9,10},{10,1... | collective-permute-start | bytes 786440 | tf_op jit(solution)/shard_map/ppermute | solution.py:52
  72.9 7.2 %collective-permute-start.21 = (bf16[64,2048]{1,0:T(8,128)(2,1)S(1)}, bf16[64,2048]{1,0:T(8,128)(2,1)S(1)}, u32[]{:S(2)}, u32[]{:S(2)}) collective-permute-start(bf16[64,2048]{1,0:T(8,128)(2,1)S(1)} %together.1), channel_id=1, source_target_pairs={{0,3},{1,0},{2,1},{3,2},{4,7},{5,4},{6,5},{7,6},{8,11},{9,8},{10,9... | collective-permute-start | bytes 786440 | tf_op jit(solution)/shard_map/ppermute | solution.py:52
  77.0 10.5 %collective-permute-start.18 = (bf16[128,2048]{1,0:T(8,128)(2,1)S(1)}, bf16[128,2048]{1,0:T(8,128)(2,1)S(1)}, u32[]{:S(2)}, u32[]{:S(2)}) collective-permute-start(bf16[128,2048]{1,0:T(8,128)(2,1)S(1)} %pad_maximum_fusion.a_ref), channel_id=1, source_target_pairs={{0,4},{1,5},{2,6},{3,7},{4,8},{5,9},{6,10},{7,11},{8,12},{9,13},{1... | collective-permute-start | bytes 1572872 | tf_op jit(solution)/shard_map/ppermute | solution.py:59
  80.0 9.4 %collective-permute-start.22 = (bf16[128,2048]{1,0:T(8,128)(2,1)S(1)}, bf16[128,2048]{1,0:T(8,128)(2,1)S(1)}, u32[]{:S(2)}, u32[]{:S(2)}) collective-permute-start(bf16[128,2048]{1,0:T(8,128)(2,1)S(1)} %constant_dynamic-update-slice_fusion.b_ref), channel_id=1, source_target_pairs={{0,12},{1,13},{2,14},{3,15},{4,0},{5,1},{6,2},{7,3},{8,4},{9,5},{1... | collective-permute-start | bytes 1572872 | tf_op jit(solution)/shard_map/ppermute | solution.py:59
  82.8 11.7 %collective-permute-start.24 = (bf16[128,2048]{1,0:T(8,128)(2,1)S(1)}, bf16[128,2048]{1,0:T(8,128)(2,1)S(1)}, u32[]{:S(2)}, u32[]{:S(2)}) collective-permute-start(bf16[128,2048]{1,0:T(8,128)(2,1)S(1)} %constant_dynamic-update-slice_fusion.b_ref), channel_id=1, source_target_pairs={{0,4},{1,5},{2,6},{3,7},{4,8},{5,9},{6,10},{7,11},{8,12},{9,13},{1... | collective-permute-start | bytes 1572872 | tf_op jit(solution)/shard_map/ppermute | solution.py:59
  82.8 12.9 %collective-permute-start.25 = (bf16[128,2048]{1,0:T(8,128)(2,1)S(1)}, bf16[128,2048]{1,0:T(8,128)(2,1)S(1)}, u32[]{:S(2)}, u32[]{:S(2)}) collective-permute-start(bf16[128,2048]{1,0:T(8,128)(2,1)S(1)} %pad_maximum_fusion.a_ref), channel_id=1, source_target_pairs={{0,12},{1,13},{2,14},{3,15},{4,0},{5,1},{6,2},{7,3},{8,4},{9,5},{1... | collective-permute-start | bytes 1572872 | tf_op jit(solution)/shard_map/ppermute | solution.py:59
  87.5 11.3 %collective-permute-start.19 = (bf16[128,2048]{1,0:T(8,128)(2,1)S(1)}, bf16[128,2048]{1,0:T(8,128)(2,1)S(1)}, u32[]{:S(2)}, u32[]{:S(2)}) collective-permute-start(bf16[128,2048]{1,0:T(8,128)(2,1)S(1)} %collective-permute-done.18.a_ref), channel_id=1, source_target_pairs={{0,4},{1,5},{2,6},{3,7},{4,8},{5,9},{6,10},{7,11},{8,12},{9,13},{1... | collective-permute-start | bytes 1572872 | tf_op jit(solution)/shard_map/ppermute | solution.py:59
  89.5 11.2 %collective-permute-start.23 = (bf16[128,2048]{1,0:T(8,128)(2,1)S(1)}, bf16[128,2048]{1,0:T(8,128)(2,1)S(1)}, u32[]{:S(2)}, u32[]{:S(2)}) collective-permute-start(bf16[128,2048]{1,0:T(8,128)(2,1)S(1)} %collective-permute-done.22.b_ref), channel_id=1, source_target_pairs={{0,12},{1,13},{2,14},{3,15},{4,0},{5,1},{6,2},{7,3},{8,4},{9,5},{1... | collective-permute-start | bytes 1572872 | tf_op jit(solution)/shard_map/ppermute | solution.py:59
  106.3 7.1 %collective-permute-start.31 = (bf16[64,1024]{1,0:T(8,128)(2,1)S(1)}, bf16[64,1024]{1,0:T(8,128)(2,1)S(1)}, u32[]{:S(2)}, u32[]{:S(2)}) collective-permute-start(bf16[64,1024]{1,0:T(8,128)(2,1)S(1)} %get-tuple-element.72), channel_id=1, source_target_pairs={{0,96},{1,97},{2,98},{3,99},{4,100},{5,101},{6,102},{7,103},{8,104... | collective-permute-start | bytes 393224 | tf_op jit(solution)/shard_map/ppermute | solution.py:45
  108.7 8.1 %collective-permute-start.29 = (bf16[64,1024]{1,0:T(8,128)(2,1)S(1)}, bf16[64,1024]{1,0:T(8,128)(2,1)S(1)}, u32[]{:S(2)}, u32[]{:S(2)}) collective-permute-start(bf16[64,1024]{1,0:T(8,128)(2,1)S(1)} %get-tuple-element.74), channel_id=1, source_target_pairs={{0,96},{1,97},{2,98},{3,99},{4,100},{5,101},{6,102},{7,103},{8,104... | collective-permute-start | bytes 393224 | tf_op jit(solution)/shard_map/ppermute | solution.py:45
  (16 other events, 110.5 us)

commit v7 on v6

--- a/solution.py
+++ b/solution.py
@@ -314,6 +314,14 @@
     arrange(rows, 2, y2, mine_ref, theirs_ref)
 
 
+def base_body(hidden_ref, mine_ref, swapped_ref, upper_ref, lower_ref, out_ref):
+    rows = upper_ref.shape[0]
+    for j, sent in enumerate((upper_ref, lower_ref)):
+        part = slice(j * rows, (j + 1) * rows)
+        total = mine_ref[j].astype(F32) + swapped_ref[j].astype(F32) + sent[...].astype(F32)
+        out_ref[part, :] = hidden_ref[part, :].astype(F32) + total
+
+
 def local(hidden, gain, w_query, w_key, w_value, w_out, key_cache, value_cache, lengths):
     heads = w_query.shape[1] // HD
     depth = hidden.shape[1]
@@ -449,14 +457,20 @@
         scratch=[pltpu.VMEM((4 * rows, width), BF16)],
         aliases={3: 0, 4: 1},
     )(two_low, two_high, w_out, *near)
-    both = mine.astype(F32) + swap_core(theirs).astype(F32)
+    swapped = swap_core(theirs)
+    both = mine.astype(F32) + swapped.astype(F32)
     over_a, over_b = shift_y(both[4].astype(BF16), 1), shift_y(both[5].astype(BF16), 3)
     from_one_b, from_three_a = shift_y(both[3].astype(BF16), 1), shift_y(both[6].astype(BF16), 3)
     from_one_a = shift_y((both[2] + over_a.astype(F32)).astype(BF16), 1)
     from_three_b = shift_y((both[7] + over_b.astype(F32)).astype(BF16), 3)
-    upper = both[0] + from_one_a.astype(F32) + from_three_a.astype(F32)
-    lower = both[1] + from_one_b.astype(F32) + from_three_b.astype(F32)
-    result = hidden.astype(F32) + jnp.concatenate([upper, lower], axis=0)
+    base = call(
+        base_body,
+        [shape(hidden.shape, F32)],
+        [VSPEC] * 5,
+        "base",
+        8,
+    )(hidden, mine, swapped, from_three_a, from_one_b)[0]
+    result = base + jnp.concatenate([from_one_a, from_three_b], axis=0).astype(F32)
     return result.astype(BF16), fresh_keys, fresh_values
 
 

time: 122 us -> 124 us (1.016)
  waiting for transfers between devices: 41 us -> 43.2 us
    ppermute x9, waiting for transfers between devices: 14.4 us -> 16.6 us  [shift_y(): lax.ppermute(value, AXES, pairs(lambda y, c, z, x: (y + step, c, z, x)))]
where the time goes in v7:
time: 124 us; the launch traced here: 123 us
  starting transfers between devices  48.9 us (39%)
  waiting for transfers between devices  43.2 us (35%)
  Pallas kernels  28.3 us (23%)
  other arithmetic  1.71 us (1%)
    ppermute x9, starting transfers between devices, shift_second(): return lax.ppermute(value, AXES, pairs(move))  18 us
    ppermute x9, waiting for transfers between devices, shift_y(): lax.ppermute(value, AXES, pairs(lambda y, c, z, x: (y + step, c, z, x)))  16.6 us
    ppermute x9, starting transfers between devices, shift_first(): return lax.ppermute(value, AXES, pairs(move))  15.9 us
    ppermute x9, starting transfers between devices, shift_y(): lax.ppermute(value, AXES, pairs(lambda y, c, z, x: (y + step, c, z, x)))  14.3 us
    ppermute x9, waiting for transfers between devices, shift_second(): return lax.ppermute(value, AXES, pairs(move))  12.3 us
    ppermute x9, waiting for transfers between devices, shift_first(): return lax.ppermute(value, AXES, pairs(move))  8.91 us
    pallas_call x1, Pallas kernels, local(): call(caches_body, [pltpu.VMEM(v.shape, v.dtype) for v in (key_cache, valu...  5.88 us
    pallas_call x1, Pallas kernels, local(): call(functools.partial(attend_body, rows, heads), [shape((rows, heads * H...  5.8 us
  transfers between devices with their start and end apart: 33, of which 23 were waited for; matrix products, arithmetic and copies ran while one was open for 0% of the time, Pallas kernels for 13%

profile of v7, /device:TPU:0, one launch (start us, length us, event | category | flops | bytes accessed | tf_op | source)
XLA Modules:
  0.0 123.4 jit_solution(2787274587631857455)
XLA Ops:
  2.4 2.9 %collective-permute-start.3 = (bf16[128,1024]{1,0:T(8,128)(2,1)}, bf16[128,1024]{1,0:T(8,128)(2,1)S(1)}, u32[]{:S(2)}, u32[]{:S(2)}) collective-permute-start(bf16[128,1024]{1,0:T(8,128)(2,1)} %hidden_ref.1), channel_id=1, source_target_pairs={{0,64},{1,65},{2,66},{3,67},{4,68},{5,69},{6,70},{7,71},{8,72},{9,... | collective-permute-start | bytes 786440 | tf_op jit(solution)/shard_map/ppermute | solution.py:45
  6.6 3.7 %collective-permute-done.back_ref = bf16[128,1024]{1,0:T(8,128)(2,1)S(1)} collective-permute-done((bf16[128,1024]{1,0:T(8,128)(2,1)}, bf16[128,1024]{1,0:T(8,128)(2,1)S(1)}, u32[]{:S(2)}, u32[]{:S(2)}) %collective-permute-start) | collective-permute-done | bytes 262176 | tf_op jit(solution)/shard_map/ppermute | solution.py:45
  10.3 2.5 %load.1 = (bf16[128,1024]{1,0:T(8,128)(2,1)S(1)}, bf16[128,1024]{1,0:T(8,128)(2,1)S(1)}, bf16[1024]{0:T(1024)(128)(2,1)S(1)}, bf16[1024,2048]{1,0:T(8,128)(2,1)S...) custom-call(bf16[128,1024]{1,0:T(8,128)(2,1)S(1)} %collective-permute-done.back_ref, ...), custom_call_target="tpu_custom_call" | custom-call | tf_op jit(solution)/shard_map/load/pallas_call | solution.py:344
  12.9 4.2 %collective-permute-done.3.refs_4_ = bf16[128,1024]{1,0:T(8,128)(2,1)S(1)} collective-permute-done((bf16[128,1024]{1,0:T(8,128)(2,1)}, bf16[128,1024]{1,0:T(8,128)(2,1)S(1)}, u32[]{:S(2)}, u32[]{:S(2)}) %collective-permute-start.3) | collective-permute-done | bytes 262176 | tf_op jit(solution)/shard_map/ppermute | solution.py:45
  19.0 4.2 %project_first.1 = (bf16[2,1168,128]{2,1,0:T(8,128)(2,1)S(1)}, bf16[2,1168,128]{2,1,0:T(8,128)(2,1)S(1)}, bf16[2,1168,128]{2,1,0:T(8,128)(2,1)}, bf16[2,1168,128...) custom-call(bf16[1024]{0:T(1024)(128)(2,1)S(1)} %get-tuple-element.34.gain_ref, ...), custom_call_target="tpu_custom_call" | custom-call | tf_op jit(solution)/shard_map/project_first/pallas_call | solution.py:357
  26.7 3.0 %collective-permute-start.8 = (bf16[2,1168,128]{2,1,0:T(8,128)(2,1)}, bf16[2,1168,128]{2,1,0:T(8,128)(2,1)S(1)}, u32[]{:S(2)}, u32[]{:S(2)}) collective-permute-start(bf16[2,1168,128]{2,1,0:T(8,128)(2,1)} %get-tuple-element.45), channel_id=1, source_target_pairs={{0,3},{1,0},{2,1},{3,2},{4,7},{5,4},{6,5},{7,6},{8,11},{9,8},{10,9... | collective-permute-start | bytes 1794056 | tf_op jit(solution)/shard_map/ppermute | solution.py:52
  29.6 2.6 %project_second.1 = (bf16[2,1168,128]{2,1,0:T(8,128)(2,1)S(1)}, bf16[2,1168,128]{2,1,0:T(8,128)(2,1)S(1)}, bf16[2,1168,128]{2,1,0:T(8,128)(2,1)S(1)}, bf16[2,1168,128]{2,1,0:T(8,128)(2,1)S(1)}) custom-call(bf16[16,64,1024]{2,1,0:T(8,128)(2,1)S(1)} %get-tuple-element.40.hs, bf16[16,16,128]{2,1,0:T(8,128)(2,1)S(1)} %get-tuple-element.41.sq, ...), custom_call_target="tpu_custom_call" | custom-call | tf_op jit(solution)/shard_map/project_second/pallas_call | solution.py:366
  35.0 3.0 %collective-permute-start.12 = (bf16[2,1168,128]{2,1,0:T(8,128)(2,1)S(1)}, bf16[2,1168,128]{2,1,0:T(8,128)(2,1)}, u32[]{:S(2)}, u32[]{:S(2)}) collective-permute-start(bf16[2,1168,128]{2,1,0:T(8,128)(2,1)S(1)} %add.55.after_ref), channel_id=1, source_target_pairs={{0,3},{1,0},{2,1},{3,2},{4,7},{5,4},{6,5},{7,6},{8,11},{9,8},{10,9... | collective-permute-start | bytes 1794056 | tf_op jit(solution)/shard_map/ppermute | solution.py:52
  38.3 5.9 %load_caches.1 = (bf16[32,1024,128]{2,1,0:T(8,128)(2,1)S(1)}, bf16[32,1024,128]{2,1,0:T(8,128)(2,1)S(1)}, bf16[16,128]{1,0:T(8,128)(2,1)S(1)}) custom-call(bf16[2,1168,128]{2,1,0:T(8,128)(2,1)S(1)} %add.55.after_ref, bf16[32,1024,128]{2,1,0:T(8,128)(2,1)} %kc_hbm.1, bf16[32,1024,128]{2,1,0:T(8,128)(2,1)} %vc_hbm.1), custom_call_target="tpu_custom_call" | custom-call | tf_op jit(solution)/shard_map/load_caches/pallas_call | solution.py:386
  44.5 2.7 %collective-permute-done.10.refs_1_.p1_ref = bf16[2,1168,128]{2,1,0:T(8,128)(2,1)S(1)} collective-permute-done((bf16[2,1168,128]{2,1,0:T(8,128)(2,1)S(1)}, bf16[2,1168,128]{2,1,0:T(8,128)(2,1)S(1)}, u32[]{:S(2)}, u32[]{:S(2)}) %collective-permute-start.10) | collective-permute-done | bytes 598048 | tf_op jit(solution)/shard_map/ppermute | solution.py:52
  48.8 4.0 %collective-permute-start.13 = (bf16[1,1168,128]{2,1,0:T(8,128)(2,1)S(1)}, bf16[1,1168,128]{2,1,0:T(8,128)(2,1)S(1)}, u32[]{:S(2)}, u32[]{:S(2)}) collective-permute-start(bf16[1,1168,128]{2,1,0:T(8,128)(2,1)S(1)} %get-tuple-element.53), channel_id=1, source_target_pairs={{0,8},{1,9},{2,10},{3,11},{4,12},{5,13},{6,14},{7,15},{8,0},{9,1},... | collective-permute-start | bytes 897032 | tf_op jit(solution)/shard_map/ppermute | solution.py:59
  53.8 2.2 %collective-permute-start.15 = (bf16[1,1168,128]{2,1,0:T(8,128)(2,1)S(1)}, bf16[1,1168,128]{2,1,0:T(8,128)(2,1)S(1)}, u32[]{:S(2)}, u32[]{:S(2)}) collective-permute-start(bf16[1,1168,128]{2,1,0:T(8,128)(2,1)S(1)} %get-tuple-element.55), channel_id=1, source_target_pairs={{0,12},{1,13},{2,14},{3,15},{4,0},{5,1},{6,2},{7,3},{8,4},{9,5},{1... | collective-permute-start | bytes 897032 | tf_op jit(solution)/shard_map/ppermute | solution.py:59
  57.5 3.2 %collective-permute-done.14.r2_ref = bf16[1,1168,128]{2,1,0:T(8,128)(2,1)S(1)} collective-permute-done((bf16[1,1168,128]{2,1,0:T(8,128)(2,1)S(1)}, bf16[1,1168,128]{2,1,0:T(8,128)(2,1)S(1)}, u32[]{:S(2)}, u32[]{:S(2)}) %collective-permute-start.14) | collective-permute-done | bytes 299040 | tf_op jit(solution)/shard_map/ppermute | solution.py:59
  61.7 5.8 %attend.1 = (bf16[64,2048]{1,0:T(8,128)(2,1)S(1)}, bf16[64,128]{1,0:T(8,128)(2,1)}, bf16[64,128]{1,0:T(8,128)(2,1)}) custom-call(s32[32]{0:T(128)S(1)} %copy-done.6, f32[1,1168,128]{2,1,0:T(8,128)S(1)} %get-tuple-element.46.p0_ref, bf16[2,1168,128]{2,1,0:T(8,128)(2,1)S(1)} %collective-permute-done.10.refs_1_.p1_ref, ...), custom_call_target="tpu_custom_call" | custom-call | tf_op jit(solution)/shard_map/attend/pallas_call | solution.py:409
  69.0 2.8 %collective-permute-start.17 = (bf16[64,2048]{1,0:T(8,128)(2,1)S(1)}, bf16[64,2048]{1,0:T(8,128)(2,1)S(1)}, u32[]{:S(2)}, u32[]{:S(2)}) collective-permute-start(bf16[64,2048]{1,0:T(8,128)(2,1)S(1)} %together.1), channel_id=1, source_target_pairs={{0,2},{1,3},{2,0},{3,1},{4,6},{5,7},{6,4},{7,5},{8,10},{9,11},{10,... | collective-permute-start | bytes 786440 | tf_op jit(solution)/shard_map/ppermute | solution.py:52
  72.9 2.2 %collective-permute-start.21 = (bf16[64,2048]{1,0:T(8,128)(2,1)S(1)}, bf16[64,2048]{1,0:T(8,128)(2,1)S(1)}, u32[]{:S(2)}, u32[]{:S(2)}) collective-permute-start(bf16[64,2048]{1,0:T(8,128)(2,1)S(1)} %together.1), channel_id=1, source_target_pairs={{0,3},{1,0},{2,1},{3,2},{4,7},{5,4},{6,5},{7,6},{8,11},{9,8},{10,9... | collective-permute-start | bytes 786440 | tf_op jit(solution)/shard_map/ppermute | solution.py:52
  80.1 2.7 %collective-permute-start.22 = (bf16[128,2048]{1,0:T(8,128)(2,1)S(1)}, bf16[128,2048]{1,0:T(8,128)(2,1)S(1)}, u32[]{:S(2)}, u32[]{:S(2)}) collective-permute-start(bf16[128,2048]{1,0:T(8,128)(2,1)S(1)} %constant_dynamic-update-slice_fusion.b_ref), channel_id=1, source_target_pairs={{0,12},{1,13},{2,14},{3,15},{4,0},{5,1},{6,2},{7,3},{8,4},{9,5},{1... | collective-permute-start | bytes 1572872 | tf_op jit(solution)/shard_map/ppermute | solution.py:59
  82.8 3.2 %collective-permute-start.25 = (bf16[128,2048]{1,0:T(8,128)(2,1)S(1)}, bf16[128,2048]{1,0:T(8,128)(2,1)S(1)}, u32[]{:S(2)}, u32[]{:S(2)}) collective-permute-start(bf16[128,2048]{1,0:T(8,128)(2,1)S(1)} %pad_maximum_fusion.a_ref), channel_id=1, source_target_pairs={{0,12},{1,13},{2,14},{3,15},{4,0},{5,1},{6,2},{7,3},{8,4},{9,5},{1... | collective-permute-start | bytes 1572872 | tf_op jit(solution)/shard_map/ppermute | solution.py:59
  89.5 3.7 %collective-permute-start.23 = (bf16[128,2048]{1,0:T(8,128)(2,1)S(1)}, bf16[128,2048]{1,0:T(8,128)(2,1)S(1)}, u32[]{:S(2)}, u32[]{:S(2)}) collective-permute-start(bf16[128,2048]{1,0:T(8,128)(2,1)S(1)} %collective-permute-done.22.b_ref), channel_id=1, source_target_pairs={{0,12},{1,13},{2,14},{3,15},{4,0},{5,1},{6,2},{7,3},{8,4},{9,5},{1... | collective-permute-start | bytes 1572872 | tf_op jit(solution)/shard_map/ppermute | solution.py:59
  102.2 2.6 %collective-permute-done.26.swapped_ref = bf16[8,64,1024]{2,1,0:T(8,128)(2,1)S(1)} collective-permute-done((bf16[8,64,1024]{2,1,0:T(8,128)(2,1)S(1)}, bf16[8,64,1024]{2,1,0:T(8,128)(2,1)S(1)}, u32[]{:S(2)}, u32[]{:S(2)}) %collective-permute-start.26) | collective-permute-done | bytes 1048608 | tf_op jit(solution)/shard_map/ppermute | solution.py:41
  106.3 2.4 %collective-permute-start.31 = (bf16[64,1024]{1,0:T(8,128)(2,1)S(1)}, bf16[64,1024]{1,0:T(8,128)(2,1)S(1)}, u32[]{:S(2)}, u32[]{:S(2)}) collective-permute-start(bf16[64,1024]{1,0:T(8,128)(2,1)S(1)} %get-tuple-element.70), channel_id=1, source_target_pairs={{0,96},{1,97},{2,98},{3,99},{4,100},{5,101},{6,102},{7,103},{8,104... | collective-permute-start | bytes 393224 | tf_op jit(solution)/shard_map/ppermute | solution.py:45
  113.5 3.0 %collective-permute-start.32 = (bf16[64,1024]{1,0:T(8,128)(2,1)S(1)}, bf16[64,1024]{1,0:T(8,128)(2,1)S(1)}, u32[]{:S(2)}, u32[]{:S(2)}) collective-permute-start(bf16[64,1024]{1,0:T(8,128)(2,1)S(1)} %get-tuple-element.66), channel_id=1, source_target_pairs={{0,96},{1,97},{2,98},{3,99},{4,100},{5,101},{6,102},{7,103},{8,104... | collective-permute-start | bytes 393224 | tf_op jit(solution)/shard_map/ppermute | solution.py:45
  116.6 2.4 %collective-permute-done.32 = bf16[64,1024]{1,0:T(8,128)(2,1)S(1)} collective-permute-done((bf16[64,1024]{1,0:T(8,128)(2,1)S(1)}, bf16[64,1024]{1,0:T(8,128)(2,1)S(1)}, u32[]{:S(2)}, u32[]{:S(2)}) %collective-permute-start.32) | collective-permute-done | bytes 131104 | tf_op jit(solution)/shard_map/ppermute | solution.py:45
  119.0 3.7 %collective-permute-done.30 = bf16[64,1024]{1,0:T(8,128)(2,1)S(1)} collective-permute-done((bf16[64,1024]{1,0:T(8,128)(2,1)S(1)}, bf16[64,1024]{1,0:T(8,128)(2,1)S(1)}, u32[]{:S(2)}, u32[]{:S(2)}) %collective-permute-start.30) | collective-permute-done | bytes 131104 | tf_op jit(solution)/shard_map/ppermute | solution.py:45
  (84 shorter events, 44.0 us)
Async XLA Ops:
  0.6 9.7 %collective-permute-start = (bf16[128,1024]{1,0:T(8,128)(2,1)}, bf16[128,1024]{1,0:T(8,128)(2,1)S(1)}, u32[]{:S(2)}, u32[]{:S(2)}) collective-permute-start(bf16[128,1024]{1,0:T(8,128)(2,1)} %hidden_ref.1), channel_id=1, source_target_pairs={{0,32},{1,33},{2,34},{3,35},{4,36},{5,37},{6,38},{7,39},{8,40},{9,... | collective-permute-start | bytes 786440 | tf_op jit(solution)/shard_map/ppermute | solution.py:45
  2.4 14.7 %collective-permute-start.3 = (bf16[128,1024]{1,0:T(8,128)(2,1)}, bf16[128,1024]{1,0:T(8,128)(2,1)S(1)}, u32[]{:S(2)}, u32[]{:S(2)}) collective-permute-start(bf16[128,1024]{1,0:T(8,128)(2,1)} %hidden_ref.1), channel_id=1, source_target_pairs={{0,64},{1,65},{2,66},{3,67},{4,68},{5,69},{6,70},{7,71},{8,72},{9,... | collective-permute-start | bytes 786440 | tf_op jit(solution)/shard_map/ppermute | solution.py:45
  5.3 11.9 %collective-permute-start.5 = (bf16[128,1024]{1,0:T(8,128)(2,1)}, bf16[128,1024]{1,0:T(8,128)(2,1)S(1)}, u32[]{:S(2)}, u32[]{:S(2)}) collective-permute-start(bf16[128,1024]{1,0:T(8,128)(2,1)} %hidden_ref.1), channel_id=1, source_target_pairs={{0,96},{1,97},{2,98},{3,99},{4,100},{5,101},{6,102},{7,103},{8,104... | collective-permute-start | bytes 786440 | tf_op jit(solution)/shard_map/ppermute | solution.py:45
  6.6 11.0 %collective-permute-start.1 = (bf16[128,1024]{1,0:T(8,128)(2,1)}, bf16[128,1024]{1,0:T(8,128)(2,1)S(1)}, u32[]{:S(2)}, u32[]{:S(2)}) collective-permute-start(bf16[128,1024]{1,0:T(8,128)(2,1)} %hidden_ref.1), channel_id=1, source_target_pairs={{0,16},{1,17},{2,18},{3,19},{4,20},{5,21},{6,22},{7,23},{8,24},{9,... | collective-permute-start | bytes 786440 | tf_op jit(solution)/shard_map/ppermute | solution.py:41
  23.2 11.2 %collective-permute-start.9 = (bf16[2,1168,128]{2,1,0:T(8,128)(2,1)S(1)}, bf16[2,1168,128]{2,1,0:T(8,128)(2,1)S(1)}, u32[]{:S(2)}, u32[]{:S(2)}) collective-permute-start(bf16[2,1168,128]{2,1,0:T(8,128)(2,1)S(1)} %get-tuple-element.48), channel_id=1, source_target_pairs={{0,1},{1,2},{2,3},{3,0},{4,5},{5,6},{6,7},{7,4},{8,9},{9,10},{10,1... | collective-permute-start | bytes 1794056 | tf_op jit(solution)/shard_map/ppermute | solution.py:52
  24.7 10.2 %collective-permute-start.11 = (bf16[2,1168,128]{2,1,0:T(8,128)(2,1)S(1)}, bf16[2,1168,128]{2,1,0:T(8,128)(2,1)S(1)}, u32[]{:S(2)}, u32[]{:S(2)}) collective-permute-start(bf16[2,1168,128]{2,1,0:T(8,128)(2,1)S(1)} %get-tuple-element.51), channel_id=1, source_target_pairs={{0,3},{1,0},{2,1},{3,2},{4,7},{5,4},{6,5},{7,6},{8,11},{9,8},{10,9... | collective-permute-start | bytes 1794056 | tf_op jit(solution)/shard_map/ppermute | solution.py:52
  26.4 17.7 %collective-permute-start.7 = (bf16[2,1168,128]{2,1,0:T(8,128)(2,1)}, bf16[2,1168,128]{2,1,0:T(8,128)(2,1)S(1)}, u32[]{:S(2)}, u32[]{:S(2)}) collective-permute-start(bf16[2,1168,128]{2,1,0:T(8,128)(2,1)} %get-tuple-element.44), channel_id=1, source_target_pairs={{0,1},{1,2},{2,3},{3,0},{4,5},{5,6},{6,7},{7,4},{8,9},{9,10},{10,1... | collective-permute-start | bytes 1794056 | tf_op jit(solution)/shard_map/ppermute | solution.py:52
  26.7 17.5 %collective-permute-start.8 = (bf16[2,1168,128]{2,1,0:T(8,128)(2,1)}, bf16[2,1168,128]{2,1,0:T(8,128)(2,1)S(1)}, u32[]{:S(2)}, u32[]{:S(2)}) collective-permute-start(bf16[2,1168,128]{2,1,0:T(8,128)(2,1)} %get-tuple-element.45), channel_id=1, source_target_pairs={{0,3},{1,0},{2,1},{3,2},{4,7},{5,4},{6,5},{7,6},{8,11},{9,8},{10,9... | collective-permute-start | bytes 1794056 | tf_op jit(solution)/shard_map/ppermute | solution.py:52
  34.5 12.7 %collective-permute-start.10 = (bf16[2,1168,128]{2,1,0:T(8,128)(2,1)S(1)}, bf16[2,1168,128]{2,1,0:T(8,128)(2,1)S(1)}, u32[]{:S(2)}, u32[]{:S(2)}) collective-permute-start(bf16[2,1168,128]{2,1,0:T(8,128)(2,1)S(1)} %add.54), channel_id=1, source_target_pairs={{0,1},{1,2},{2,3},{3,0},{4,5},{5,6},{6,7},{7,4},{8,9},{9,10},{10,1... | collective-permute-start | bytes 1794056 | tf_op jit(solution)/shard_map/ppermute | solution.py:52
  35.0 12.5 %collective-permute-start.12 = (bf16[2,1168,128]{2,1,0:T(8,128)(2,1)S(1)}, bf16[2,1168,128]{2,1,0:T(8,128)(2,1)}, u32[]{:S(2)}, u32[]{:S(2)}) collective-permute-start(bf16[2,1168,128]{2,1,0:T(8,128)(2,1)S(1)} %add.55.after_ref), channel_id=1, source_target_pairs={{0,3},{1,0},{2,1},{3,2},{4,7},{5,4},{6,5},{7,6},{8,11},{9,8},{10,9... | collective-permute-start | bytes 1794056 | tf_op jit(solution)/shard_map/ppermute | solution.py:52
  48.8 8.7 %collective-permute-start.13 = (bf16[1,1168,128]{2,1,0:T(8,128)(2,1)S(1)}, bf16[1,1168,128]{2,1,0:T(8,128)(2,1)S(1)}, u32[]{:S(2)}, u32[]{:S(2)}) collective-permute-start(bf16[1,1168,128]{2,1,0:T(8,128)(2,1)S(1)} %get-tuple-element.53), channel_id=1, source_target_pairs={{0,8},{1,9},{2,10},{3,11},{4,12},{5,13},{6,14},{7,15},{8,0},{9,1},... | collective-permute-start | bytes 897032 | tf_op jit(solution)/shard_map/ppermute | solution.py:59
  52.7 8.0 %collective-permute-start.14 = (bf16[1,1168,128]{2,1,0:T(8,128)(2,1)S(1)}, bf16[1,1168,128]{2,1,0:T(8,128)(2,1)S(1)}, u32[]{:S(2)}, u32[]{:S(2)}) collective-permute-start(bf16[1,1168,128]{2,1,0:T(8,128)(2,1)S(1)} %get-tuple-element.54), channel_id=1, source_target_pairs={{0,4},{1,5},{2,6},{3,7},{4,8},{5,9},{6,10},{7,11},{8,12},{9,13},{1... | collective-permute-start | bytes 897032 | tf_op jit(solution)/shard_map/ppermute | solution.py:59
  53.8 7.9 %collective-permute-start.15 = (bf16[1,1168,128]{2,1,0:T(8,128)(2,1)S(1)}, bf16[1,1168,128]{2,1,0:T(8,128)(2,1)S(1)}, u32[]{:S(2)}, u32[]{:S(2)}) collective-permute-start(bf16[1,1168,128]{2,1,0:T(8,128)(2,1)S(1)} %get-tuple-element.55), channel_id=1, source_target_pairs={{0,12},{1,13},{2,14},{3,15},{4,0},{5,1},{6,2},{7,3},{8,4},{9,5},{1... | collective-permute-start | bytes 897032 | tf_op jit(solution)/shard_map/ppermute | solution.py:59
  69.0 8.0 %collective-permute-start.17 = (bf16[64,2048]{1,0:T(8,128)(2,1)S(1)}, bf16[64,2048]{1,0:T(8,128)(2,1)S(1)}, u32[]{:S(2)}, u32[]{:S(2)}) collective-permute-start(bf16[64,2048]{1,0:T(8,128)(2,1)S(1)} %together.1), channel_id=1, source_target_pairs={{0,2},{1,3},{2,0},{3,1},{4,6},{5,7},{6,4},{7,5},{8,10},{9,11},{10,... | collective-permute-start | bytes 786440 | tf_op jit(solution)/shard_map/ppermute | solution.py:52
  71.8 8.0 %collective-permute-start.20 = (bf16[64,2048]{1,0:T(8,128)(2,1)S(1)}, bf16[64,2048]{1,0:T(8,128)(2,1)S(1)}, u32[]{:S(2)}, u32[]{:S(2)}) collective-permute-start(bf16[64,2048]{1,0:T(8,128)(2,1)S(1)} %together.1), channel_id=1, source_target_pairs={{0,1},{1,2},{2,3},{3,0},{4,5},{5,6},{6,7},{7,4},{8,9},{9,10},{10,1... | collective-permute-start | bytes 786440 | tf_op jit(solution)/shard_map/ppermute | solution.py:52
  72.9 7.2 %collective-permute-start.21 = (bf16[64,2048]{1,0:T(8,128)(2,1)S(1)}, bf16[64,2048]{1,0:T(8,128)(2,1)S(1)}, u32[]{:S(2)}, u32[]{:S(2)}) collective-permute-start(bf16[64,2048]{1,0:T(8,128)(2,1)S(1)} %together.1), channel_id=1, source_target_pairs={{0,3},{1,0},{2,1},{3,2},{4,7},{5,4},{6,5},{7,6},{8,11},{9,8},{10,9... | collective-permute-start | bytes 786440 | tf_op jit(solution)/shard_map/ppermute | solution.py:52
  77.1 10.5 %collective-permute-start.18 = (bf16[128,2048]{1,0:T(8,128)(2,1)S(1)}, bf16[128,2048]{1,0:T(8,128)(2,1)S(1)}, u32[]{:S(2)}, u32[]{:S(2)}) collective-permute-start(bf16[128,2048]{1,0:T(8,128)(2,1)S(1)} %pad_maximum_fusion.a_ref), channel_id=1, source_target_pairs={{0,4},{1,5},{2,6},{3,7},{4,8},{5,9},{6,10},{7,11},{8,12},{9,13},{1... | collective-permute-start | bytes 1572872 | tf_op jit(solution)/shard_map/ppermute | solution.py:59
  80.1 9.4 %collective-permute-start.22 = (bf16[128,2048]{1,0:T(8,128)(2,1)S(1)}, bf16[128,2048]{1,0:T(8,128)(2,1)S(1)}, u32[]{:S(2)}, u32[]{:S(2)}) collective-permute-start(bf16[128,2048]{1,0:T(8,128)(2,1)S(1)} %constant_dynamic-update-slice_fusion.b_ref), channel_id=1, source_target_pairs={{0,12},{1,13},{2,14},{3,15},{4,0},{5,1},{6,2},{7,3},{8,4},{9,5},{1... | collective-permute-start | bytes 1572872 | tf_op jit(solution)/shard_map/ppermute | solution.py:59
  82.8 11.7 %collective-permute-start.24 = (bf16[128,2048]{1,0:T(8,128)(2,1)S(1)}, bf16[128,2048]{1,0:T(8,128)(2,1)S(1)}, u32[]{:S(2)}, u32[]{:S(2)}) collective-permute-start(bf16[128,2048]{1,0:T(8,128)(2,1)S(1)} %constant_dynamic-update-slice_fusion.b_ref), channel_id=1, source_target_pairs={{0,4},{1,5},{2,6},{3,7},{4,8},{5,9},{6,10},{7,11},{8,12},{9,13},{1... | collective-permute-start | bytes 1572872 | tf_op jit(solution)/shard_map/ppermute | solution.py:59
  82.8 12.9 %collective-permute-start.25 = (bf16[128,2048]{1,0:T(8,128)(2,1)S(1)}, bf16[128,2048]{1,0:T(8,128)(2,1)S(1)}, u32[]{:S(2)}, u32[]{:S(2)}) collective-permute-start(bf16[128,2048]{1,0:T(8,128)(2,1)S(1)} %pad_maximum_fusion.a_ref), channel_id=1, source_target_pairs={{0,12},{1,13},{2,14},{3,15},{4,0},{5,1},{6,2},{7,3},{8,4},{9,5},{1... | collective-permute-start | bytes 1572872 | tf_op jit(solution)/shard_map/ppermute | solution.py:59
  87.5 11.3 %collective-permute-start.19 = (bf16[128,2048]{1,0:T(8,128)(2,1)S(1)}, bf16[128,2048]{1,0:T(8,128)(2,1)S(1)}, u32[]{:S(2)}, u32[]{:S(2)}) collective-permute-start(bf16[128,2048]{1,0:T(8,128)(2,1)S(1)} %collective-permute-done.18.a_ref), channel_id=1, source_target_pairs={{0,4},{1,5},{2,6},{3,7},{4,8},{5,9},{6,10},{7,11},{8,12},{9,13},{1... | collective-permute-start | bytes 1572872 | tf_op jit(solution)/shard_map/ppermute | solution.py:59
  89.5 11.2 %collective-permute-start.23 = (bf16[128,2048]{1,0:T(8,128)(2,1)S(1)}, bf16[128,2048]{1,0:T(8,128)(2,1)S(1)}, u32[]{:S(2)}, u32[]{:S(2)}) collective-permute-start(bf16[128,2048]{1,0:T(8,128)(2,1)S(1)} %collective-permute-done.22.b_ref), channel_id=1, source_target_pairs={{0,12},{1,13},{2,14},{3,15},{4,0},{5,1},{6,2},{7,3},{8,4},{9,5},{1... | collective-permute-start | bytes 1572872 | tf_op jit(solution)/shard_map/ppermute | solution.py:59
  106.3 7.1 %collective-permute-start.31 = (bf16[64,1024]{1,0:T(8,128)(2,1)S(1)}, bf16[64,1024]{1,0:T(8,128)(2,1)S(1)}, u32[]{:S(2)}, u32[]{:S(2)}) collective-permute-start(bf16[64,1024]{1,0:T(8,128)(2,1)S(1)} %get-tuple-element.70), channel_id=1, source_target_pairs={{0,96},{1,97},{2,98},{3,99},{4,100},{5,101},{6,102},{7,103},{8,104... | collective-permute-start | bytes 393224 | tf_op jit(solution)/shard_map/ppermute | solution.py:45
  108.7 7.7 %collective-permute-start.27 = (bf16[64,1024]{1,0:T(8,128)(2,1)S(1)}, bf16[64,1024]{1,0:T(8,128)(2,1)S(1)}, u32[]{:S(2)}, u32[]{:S(2)}) collective-permute-start(bf16[64,1024]{1,0:T(8,128)(2,1)S(1)} %get-tuple-element.72), channel_id=1, source_target_pairs={{0,96},{1,97},{2,98},{3,99},{4,100},{5,101},{6,102},{7,103},{8,104... | collective-permute-start | bytes 393224 | tf_op jit(solution)/shard_map/ppermute | solution.py:45
  (16 other events, 112.3 us)
